TPU v7x, 128 devices: a whole 4x4x4 slice. The times are simulated.
128 devices in a mesh: task: 8 (over y, z_hi), row: 2 (over core), col: 8 (over z_lo, x).
Axes of the slice: x: 4, y: 4, z: 4 (z_hi: 2, z_lo: 2; z = z_hi * 2 + z_lo), core: 2. Of those that a mesh axis runs over, the one named last changes fastest.
Arguments:
- inputs: bfloat16 [8, 512, 4096], P('task', None, 'row'), may hold values from -6 to 6
- gate_weight: bfloat16 [8, 4096, 10240], P('task', 'row', 'col'), may hold values from -0.09375 to 0.09375
- up_weight: bfloat16 [8, 4096, 10240], P('task', 'row', 'col'), may hold values from -0.09375 to 0.09375
- cotangent: bfloat16 [8, 512, 4096], P('task', None, ('row', 'col')), may hold values from -0.59765625 to 0.59765625
- down_weight: bfloat16 [8, 10240, 4096], P('task', 'col', 'row'), may hold values from -6 to 6
Outputs:
- merged: bfloat16 [10240, 4096], P('col', 'row')
All inputs are finite; a program needn't handle non-finite values.
Results may differ from a plain program's by a relative error of at most 0.0095.
Values may be sent and summed in bfloat16 or wider, within the bound.
No kernel may reach another device: no remote copies, remote signals or barrier semaphores. Data moves between devices by JAX's collectives and lax.ppermute only.
A program may use at most 192 MiB of HBM per device.

v0:
```python
import jax
import jax.numpy as jnp
from jax import lax
from jax.sharding import PartitionSpec as P

EX = 4
LEN = 128


fisher_floor = 0.05


def body(inputs, gate_weight, up_weight, cotangent, down_weight):
    tokens = inputs[0]
    w_gate = gate_weight[0]
    w_up = up_weight[0]
    width = w_gate.shape[1]
    gate_part = jnp.dot(tokens, w_gate, preferred_element_type=jnp.float32)
    up_part = jnp.dot(tokens, w_up, preferred_element_type=jnp.float32)
    gate, up = lax.psum((gate_part, up_part), "row")
    hidden = (jax.nn.gelu(gate, approximate=True) * up).astype(jnp.bfloat16)
    out_grad = lax.all_gather(cotangent[0], "col", axis=1, tiled=True)

    def accumulate(step, total):
        start = step * LEN
        h_rows = lax.dynamic_slice_in_dim(hidden, start, LEN, 0)
        d_rows = lax.dynamic_slice_in_dim(out_grad, start, LEN, 0)
        grad = lax.dot_general(
            h_rows, d_rows, (((0,), (0,)), ((), ())), preferred_element_type=jnp.float32
        )
        return total + grad * grad

    fisher = lax.fori_loop(0, EX, accumulate, jnp.zeros((width, out_grad.shape[1]), jnp.float32))
    weight_full = fisher + fisher_floor
    numer = weight_full * down_weight[0].astype(jnp.float32)
    weight = weight_full.astype(jnp.bfloat16)
    total_num, total_den = lax.psum((numer, weight.astype(jnp.float32)), "task")
    merged = (total_num / total_den).astype(jnp.bfloat16)
    return merged


def solution(mesh):
    placed = (
        P("task", None, "row"),
        P("task", "row", "col"),
        P("task", "row", "col"),
        P("task", None, ("row", "col")),
        P("task", "col", "row"),
    )
    return jax.shard_map(
        body, mesh=mesh, in_specs=placed, out_specs=P("col", "row"), check_vma=False
    )
```

profile of v0, /device:TPU:56, one launch (start us, length us, event | category | flops | bytes accessed | tf_op | source)
XLA Modules:
  0.0 958.1 jit_solution(16081716873856149380)
XLA Ops:
  7.4 0.0 copy-start
  7.4 0.0 all-reduce.7.cloned.1.call-start
  7.4 1.6 copy-done
  9.0 6.8 fusion.6
  15.8 6.8 fusion.4
  22.6 0.0 all-reduce.7.cloned.1.call-update
  22.7 0.0 all-gather.3.cloned.1.call-start
  22.7 0.5 all-gather.3.cloned.1.call-update
  23.2 0.0 all-reduce.5.cloned.1.call-start
  23.3 37.1 %all-reduce.7.cloned.1.call-done = (f32[512,1280]{1,0:T(8,128)}, f32[512,1280]{1,0:T(8,128)}) async-done(((f32[512,1280]{1,0:T(8,128)}, f32[512,1280]{1,0:T(8,128)}), (f32[512,1280]{1,0:T(8,128)}, f32[512,1280]{1,0:T(8,128)})) %all-reduce.7.cloned.1.call-update) | async-done | bytes 5242896 | tf_op jit(solution)/shard_map/psum | solution.py:20
  60.4 3.4 fusion.16
  63.8 7.5 all-gather.3.cloned.1.call-done
  71.3 35.7 %while.14 = (s32[]{:T(128)}, f32[1280,2048]{1,0:T(8,128)}, bf16[512,1280]{1,0:T(8,128)(2,1)S(1)}, bf16[512,2048]{1,0:T(8,128)(2,1)}, s32[]{:T(128)}, /*index=5*/s32[]{:T(128)}, s32[]{:T(128)}, s32[]{:T(128)}) while((s32[]{:T(128)}, f32[1280,2048]{1,0:T(8,128)}, bf16[512,1280]{1,0:T(8,128)(2,1)S(1)}, bf16[512,2048]{1,0:T(8,128)(2,1)}, ...), condition=%wide.region_3.0_spmd.clone, body=%wide.region_2.0_spmd.clone.sunk | while | flops 678952960 | bytes 21825172 | solution.py:33
  71.3 6.6 select_add_fusion.2
  77.9 9.7 %select_add_fusion.2 = f32[1280,2048]{1,0:T(8,128)} fusion(f32[1280,2048]{1,0:T(8,128)} %get-tuple-element.148, pred[]{:T(512)S(6)} %compare.3, bf16[512,2048]{1,0:T(8,128)(2,1)} %get-tuple-element.158, s32[]{:T(128)S(6)} %select_n.10, bf16[512,1280]{1,0:T(8,128)(2,1)S(1)} %get-tuple-element.157), kind=kOutput, calls=%fused_computation.1.clone.1 | convolution fusion | flops 678952960 | bytes 21825024 | tf_op jit(solution)/shard_map/while/body/eval_jaxpr/dot_general | solution.py:28
  87.6 9.7 %select_add_fusion.2 = f32[1280,2048]{1,0:T(8,128)} fusion(f32[1280,2048]{1,0:T(8,128)} %get-tuple-element.148, pred[]{:T(512)S(6)} %compare.3, bf16[512,2048]{1,0:T(8,128)(2,1)} %get-tuple-element.158, s32[]{:T(128)S(6)} %select_n.10, bf16[512,1280]{1,0:T(8,128)(2,1)S(1)} %get-tuple-element.157), kind=kOutput, calls=%fused_computation.1.clone.1 | convolution fusion | flops 678952960 | bytes 21825024 | tf_op jit(solution)/shard_map/while/body/eval_jaxpr/dot_general | solution.py:28
  97.3 9.7 %select_add_fusion.2 = f32[1280,2048]{1,0:T(8,128)} fusion(f32[1280,2048]{1,0:T(8,128)} %get-tuple-element.148, pred[]{:T(512)S(6)} %compare.3, bf16[512,2048]{1,0:T(8,128)(2,1)} %get-tuple-element.158, s32[]{:T(128)S(6)} %select_n.10, bf16[512,1280]{1,0:T(8,128)(2,1)S(1)} %get-tuple-element.157), kind=kOutput, calls=%fused_computation.1.clone.1 | convolution fusion | flops 678952960 | bytes 21825024 | tf_op jit(solution)/shard_map/while/body/eval_jaxpr/dot_general | solution.py:28
  107.0 14.0 %fusion.3 = (f32[1280,2048]{1,0:T(8,128)}, f32[1280,2048]{1,0:T(8,128)}) fusion(f32[1280,2048]{1,0:T(8,128)} %get-tuple-element.84, bf16[1,1280,2048]{2,1,0:T(8,128)(2,1)} %param.11), kind=kLoop, calls=%fused_computation.8 | loop fusion | flops 13107200 | bytes 36700160 | tf_op jit(solution)/shard_map/convert_element_type | solution.py:37
  121.0 0.0 all-reduce.5.cloned.1.call-update
  121.0 818.0 %all-reduce.5.cloned.1.call-done = (f32[1280,2048]{1,0:T(8,128)}, f32[1280,2048]{1,0:T(8,128)}) async-done(((f32[1280,2048]{1,0:T(8,128)}, f32[1280,2048]{1,0:T(8,128)}), (f32[1280,2048]{1,0:T(8,128)}, f32[1280,2048]{1,0:T(8,128)})) %all-reduce.5.cloned.1.call-update) | async-done | bytes 20971536 | tf_op jit(solution)/shard_map/psum | solution.py:37
  939.0 0.0 copy-start.1
  939.0 11.7 %divide_convert_fusion = bf16[1280,2048]{1,0:T(8,128)(2,1)} fusion(f32[1280,2048]{1,0:T(8,128)} %get-tuple-element.108, f32[1280,2048]{1,0:T(8,128)} %get-tuple-element.109), kind=kLoop, calls=%fused_computation.6 | loop fusion | flops 5242880 | bytes 26214400 | tf_op jit(solution)/shard_map/convert_element_type | solution.py:38
  950.6 0.0 copy-done.1
  (1 shorter events, 0.0 us)
Async XLA Ops:
  7.4 1.6 copy-start
  7.4 53.0 %all-reduce.7.cloned.1.call-start = ((), (), s32[]{:S(2)}) async-start(), calls=%async_computation.2 | async-start | bytes 10485760 | tf_op jit(solution)/shard_map/psum | solution.py:20
  22.7 48.6 %all-gather.3.cloned.1.call-start = ((), (), s32[]{:S(2)}) async-start(), calls=%async_computation | async-start | bytes 2359296 | tf_op jit(solution)/shard_map/all_gather | solution.py:22
  23.2 915.7 %all-reduce.5.cloned.1.call-start = ((), (), s32[]{:S(2)}) async-start(), calls=%async_computation.1 | async-start | bytes 41943040 | tf_op jit(solution)/shard_map/psum | solution.py:37
  939.0 11.7 %copy-start.1 = (bf16[1,512,2048]{2,1,0:T(8,128)(2,1)S(1)}, bf16[1,512,2048]{2,1,0:T(8,128)(2,1)}, u32[]{:S(2)}) copy-start(bf16[1,512,2048]{2,1,0:T(8,128)(2,1)} %param.7) | copy-start | bytes 6291460
Sparse Core Ops, SparseCore 0:
  22.8 37.5 all-reduce.6
Sparse Core Ops, SparseCore 1:
  24.7 46.5 all-gather.2
  121.1 817.8 all-reduce.4
where the time goes:
time: 964 us; the launch traced here: 958 us
  waiting for transfers between devices  863 us (90%)
  matrix products  49.4 us (5%)
  other arithmetic  29.1 us (3%)
  between operations  14.9 us (2%)
    psum x1, waiting for transfers between devices, body(): total_num, total_den = lax.psum((numer, weight.astype(jnp.float32)), 'task')  818 us
    psum x1, waiting for transfers between devices, body(): gate, up = lax.psum((gate_part, up_part), 'row')  37.1 us
    dot_general x4, matrix products, accumulate(): lax.dot_general(h_rows, d_rows, (((0,), (0,)), ((), ())), preferred_eleme...  35.7 us
  transfers between devices with their start and end apart: 3, of which 3 were waited for; matrix products, arithmetic and copies ran while one was open for 0% of the time, Pallas kernels for 0%

commit v1 on v0

v1 whole, which is shorter than its diff:
```python
import functools

import jax
import jax.numpy as jnp
from jax import lax
from jax.experimental import pallas as pl
from jax.experimental.pallas import tpu as pltpu
from jax.sharding import PartitionSpec as P

LEN = 128
HALF = 256
BLK = 256
fisher_floor = 0.05
F32 = jnp.float32
BF = jnp.bfloat16
VMEM = pl.BlockSpec(memory_space=pltpu.VMEM)
SMEM = pl.BlockSpec(memory_space=pltpu.SMEM)
ANY = pl.BlockSpec(memory_space=pl.ANY)
HBM = pl.BlockSpec(memory_space=pltpu.HBM)
TOKEN = jax.ShapeDtypeStruct((8, 128), F32)
FREE = pl.CostEstimate(flops=0, bytes_accessed=0, transcendentals=0)


def task_of(y, h):
    return y * 2 + h


def y_shift(n):
    return [(task_of(y, h), task_of((y + n) % 4, h)) for y in range(4) for h in range(2)]


def x_shift(n):
    return [(z * 4 + x, z * 4 + (x + n) % 4) for z in range(2) for x in range(4)]


Z_SWAP = [(task_of(y, h), task_of(y, 1 - h)) for y in range(4) for h in range(2)]
ZLO_SWAP = [(c, (c + 4) % 8) for c in range(8)]
CORE_SWAP = [(0, 1), (1, 0)]
X_GROUPS = [[z * 4 + x for x in range(4)] for z in range(2)]
Z_MIRROR = [
    (task_of(y, h) * 8 + c, task_of(y, 1 - h) * 8 + (c + 4) % 8) for y in range(4) for h in range(2) for c in range(8)
]
RING = [
    (task_of(y, h) * 2 + r, task_of((y + (1 if r == 0 else -1)) % 4, h) * 2 + r)
    for y in range(4)
    for h in range(2)
    for r in range(2)
]


def move(x, perm, axis="task"):
    return lax.ppermute(x, axis, perm)


def project_kernel(step, offs, x_hbm, g_hbm, u_hbm, own_ref, send_ref, token, x_ref, p_ref, sum_ref, sem):
    depth, width = g_hbm.shape
    steps = depth // step
    copies = []

    def fetch(src, dst):
        copy = pltpu.make_async_copy(src, dst, sem.at[len(copies)])
        copy.start()
        copies.append(copy)

    for half, side in enumerate((offs[0], 1 - offs[0])):
        rows = pl.ds(pl.multiple_of(side * HALF, HALF), HALF)
        fetch(x_hbm.at[rows, :], x_ref.at[pl.ds(half * HALF, HALF), :])
    for n in range(steps):
        for i, hbm in enumerate((g_hbm, u_hbm)):
            fetch(hbm.at[pl.ds(n * step, step), :], p_ref.at[i, pl.ds(n * step, step), :])
    token[...] = jnp.zeros_like(token)
    copies[0].wait()
    copies[1].wait()
    for n in range(steps):
        deep = pl.ds(n * step, step)
        for i in range(2):
            copies[2 + 2 * n + i].wait()
            for c in range(width // BLK):
                cols = pl.ds(c * BLK, BLK)
                both = jnp.dot(x_ref[:, deep], p_ref[i, deep, cols], preferred_element_type=F32)
                mine, other = both[:HALF], both[HALF:]
                if n > 0:
                    mine = mine + own_ref[i, :, cols]
                    other = other + sum_ref[i, :, cols]
                own_ref[i, :, cols] = mine
                if n < steps - 1:
                    sum_ref[i, :, cols] = other
                else:
                    send_ref[i, :, cols] = other.astype(BF)


def project(offs, x, w_gate, w_up):
    depth, width = w_gate.shape
    step = 512
    return pl.pallas_call(
        functools.partial(project_kernel, step),
        in_specs=[SMEM] + [HBM] * 3,
        out_specs=[VMEM] * 3,
        out_shape=[
            jax.ShapeDtypeStruct((2, HALF, width), F32),
            jax.ShapeDtypeStruct((2, HALF, width), BF),
            TOKEN,
        ],
        scratch_shapes=[
            pltpu.VMEM(x.shape, BF),
            pltpu.VMEM((2, depth, width), BF),
            pltpu.VMEM((2, HALF, width), F32),
            pltpu.SemaphoreType.DMA((2 + 2 * (depth // step),)),
        ],
        compiler_params=pltpu.CompilerParams(vmem_limit_bytes=22 * 2**20),
        cost_estimate=FREE,
    )(offs, in_hbm(x), in_hbm(w_gate), in_hbm(w_up))


def pass_kernel(n, *refs):
    refs[-1][...] = jnp.zeros_like(refs[-1])


def hold(x, before):
    return pl.pallas_call(
        functools.partial(pass_kernel, len(before)),
        in_specs=[VMEM] * (1 + len(before)),
        out_specs=[VMEM, VMEM],
        out_shape=[jax.ShapeDtypeStruct(x.shape, x.dtype), TOKEN],
        input_output_aliases={0: 0},
        compiler_params=pltpu.CompilerParams(vmem_limit_bytes=2**20),
        cost_estimate=FREE,
    )(x, *before)


def hidden_kernel(offs, own_ref, recv_ref, w_ref, *refs):
    out_ref, away_ref, w_away_ref, token = refs[-4:]
    token[...] = jnp.zeros_like(token)
    step = 256
    for n in range(out_ref.shape[0] // step):
        cols = pl.ds(n * step, step)
        gate = own_ref[0, :, cols] + recv_ref[0, :, cols].astype(F32)
        up = own_ref[1, :, cols] + recv_ref[1, :, cols].astype(F32)
        hidden = jax.nn.gelu(gate, approximate=True) * up
        out_ref[cols, :] = hidden.T.astype(BF)
    half, wide = w_away_ref.shape
    rows = pl.ds(pl.multiple_of(offs[1], 16), half)
    away_ref[...] = out_ref[rows, :]
    w_away_ref[...] = w_ref[rows, pl.ds(pl.multiple_of(offs[2], BLK), wide)]


def make_hidden(offs, own, recv, w, before):
    width = own.shape[2]
    return pl.pallas_call(
        hidden_kernel,
        in_specs=[SMEM, VMEM, VMEM, VMEM] + [VMEM] * len(before),
        out_specs=[VMEM] * 4,
        out_shape=[
            jax.ShapeDtypeStruct((width, HALF), BF),
            jax.ShapeDtypeStruct((width // 2, HALF), BF),
            jax.ShapeDtypeStruct((w.shape[0] // 2, w.shape[1] // 2), BF),
            TOKEN,
        ],
        compiler_params=pltpu.CompilerParams(vmem_limit_bytes=6 * 2**20),
        cost_estimate=FREE,
    )(offs, own, recv, w, *before)


def join_kernel(n, *refs):
    parts, out, token = refs[:n], refs[-2], refs[-1]
    token[...] = jnp.zeros_like(token)
    for i in range(n):
        out[i] = parts[i][...]


def join(parts, token):
    return pl.pallas_call(
        functools.partial(join_kernel, len(parts)),
        in_specs=[VMEM] * (len(parts) + 1),
        out_specs=[VMEM, VMEM],
        out_shape=[jax.ShapeDtypeStruct((len(parts), *parts[0].shape), BF), TOKEN],
        compiler_params=pltpu.CompilerParams(vmem_limit_bytes=6 * 2**20),
        cost_estimate=FREE,
    )(*parts, token)


def term_kernel(rows, nb, spots, kinds, n_recv, final, offs, *refs):
    refs = list(refs)
    parts = []
    for kind in kinds:
        ha, hb, d = refs.pop(0), refs.pop(0), [refs.pop(0) for _ in range(nb)]
        parts.append((ha, hb, d, kind, refs.pop(0)))
    recv = [refs.pop(0) for _ in range(n_recv)]
    out, token = refs[-2:]
    token[...] = jnp.zeros_like(token)
    tile = next(t for t in (160, 128, 112, 96, 80, 64, 48, 32, 16) if rows % t == 0)
    toks = (offs[0] * HALF, (1 - offs[0]) * HALF)
    for j in range(nb):
        cols = pl.ds(j * BLK, BLK)

        @pl.loop(0, rows // tile)
        def _(i):
            at = pl.multiple_of(i * tile, 16)
            here = pl.ds(at, tile)
            num = den = None
            for (ha, hb, d, kind, w), (h_spot, w_row_spot, w_col_spot) in zip(parts, spots):
                row = pl.multiple_of(offs[h_spot] + at, 16)
                w_row = pl.multiple_of(offs[w_row_spot] + at, 16)
                w_col = pl.multiple_of(offs[w_col_spot + j], BLK)
                weight = jnp.full((tile, BLK), fisher_floor, F32)
                for h, tok in zip((ha, hb), toks):
                    for e in range(2):
                        there = pl.ds(pl.multiple_of(tok + e * LEN, LEN), LEN)
                        grad = jnp.dot(
                            h[pl.ds(row, tile), e * LEN : (e + 1) * LEN],
                            d[j][there, :] if kind is None else d[j][kind, there, :],
                            preferred_element_type=F32,
                        )
                        weight = weight + grad * grad
                term = weight * w[pl.ds(w_row, tile), pl.ds(w_col, BLK)].astype(F32)
                num = term if num is None else num + term
                den = weight if den is None else den + weight
            for ref in recv:
                num = num + ref[0, here, cols].astype(F32)
                den = den + ref[1, here, cols].astype(F32)
            if final:
                out[here, cols] = (num / den).astype(BF)
            else:
                out[0, here, cols] = num.astype(BF)
                out[1, here, cols] = den.astype(BF)


def terms(offs, sources, rows, recv, final, before):
    nb = len(sources[0][2])
    wide = nb * BLK
    operands = [offs]
    for ha, hb, d, kind, w, spots in sources:
        operands += [ha, hb, *d, w]
    operands += [*recv, *before]
    return pl.pallas_call(
        functools.partial(term_kernel, rows, nb, [s[5] for s in sources], [s[3] for s in sources], len(recv), final),
        in_specs=[SMEM] + [VMEM] * (len(operands) - 1),
        out_specs=[VMEM, VMEM],
        out_shape=[jax.ShapeDtypeStruct((rows, wide) if final else (2, rows, wide), BF), TOKEN],
        compiler_params=pltpu.CompilerParams(vmem_limit_bytes=6 * 2**20),
        cost_estimate=FREE,
    )(*operands)


def merge_kernel(a, b, before, out, token):
    token[...] = jnp.zeros_like(token)
    num = a[0].astype(F32) + b[0].astype(F32)
    den = a[1].astype(F32) + b[1].astype(F32)
    out[...] = (num / den).astype(BF)


def merge(a, b, token):
    return pl.pallas_call(
        merge_kernel,
        in_specs=[VMEM] * 3,
        out_specs=[VMEM, VMEM],
        out_shape=[jax.ShapeDtypeStruct(a.shape[1:], BF), TOKEN],
        compiler_params=pltpu.CompilerParams(vmem_limit_bytes=6 * 2**20),
        cost_estimate=FREE,
    )(a, b, token)


def place_kernel(plan, n_parts, offs, *refs):
    parts, out, sem = refs[:n_parts], refs[-2], refs[-1]
    copies = []
    for part, lead, rows, row_at, col_at, nb in plan:
        src = parts[part] if lead is None else parts[part].at[lead]
        row = pl.multiple_of(offs[row_at], 16)
        for j in range(nb):
            col = pl.multiple_of(offs[col_at + j], BLK)
            copy = pltpu.make_async_copy(
                src.at[:, pl.ds(j * BLK, BLK)], out.at[pl.ds(row, rows), pl.ds(col, BLK)], sem.at[len(copies)]
            )
            copy.start()
            copies.append(copy)
    for copy in copies:
        copy.wait()


def place(shape, offs, parts, plan, before):
    return pl.pallas_call(
        functools.partial(place_kernel, plan, len(parts)),
        in_specs=[SMEM] + [VMEM] * (len(parts) + len(before)),
        out_specs=HBM,
        out_shape=jax.ShapeDtypeStruct(shape, BF),
        scratch_shapes=[pltpu.SemaphoreType.DMA((sum(p[-1] for p in plan),))],
        compiler_params=pltpu.CompilerParams(vmem_limit_bytes=2**20),
        cost_estimate=FREE,
    )(offs, *parts, *before)


def in_hbm(x):
    return pltpu.with_memory_space_constraint(x, pltpu.HBM)


def ints(*values):
    return jnp.stack([jnp.asarray(v, jnp.int32) for v in values])


def body(inputs, gate_weight, up_weight, cotangent, down_weight):
    task, core, col = lax.axis_index("task"), lax.axis_index("row"), lax.axis_index("col")
    y, h = task // 2, task % 2
    z_lo, x = col // 4, col % 4
    ring = 1 - 2 * core
    width, wide = down_weight.shape[1:]
    half, quarter, part = width // 2, width // 4, width // 8
    table = [core, (1 - h) * half, (1 - z_lo) * (wide // 2)]
    block = [(x - n) % 4 * BLK for n in range(4)]
    NEAR = len(table)
    table += [z_lo * (wide // 2) + b for b in block]
    FAR = len(table)
    table += [(1 - z_lo) * (wide // 2) + b for b in block]
    ALONE = len(table)
    table += block
    RING_ROW = len(table)
    table += [(y - k * ring) % 4 * quarter for k in range(4)]
    PART = len(table)
    table += [(y - k * ring) % 4 * part for k in range(4)]
    HERE = len(table)
    table += [h * half + (y - k * ring) % 4 * part for k in range(4)]
    BACK = len(table)
    table += [(y - k) % 4 * quarter for k in range(4)]
    BACK_HERE = len(table)
    table += [h * half + (y - k) % 4 * part for k in range(4)]
    BACK_AWAY = len(table)
    table += [(1 - h) * half + (y - k) % 4 * part for k in range(4)]
    offs = ints(*table)

    mine = cotangent[0]
    near = [mine] + [move(mine, x_shift(n), "col") for n in (1, 2, 3)]
    far_mine = [move(mine, ZLO_SWAP, "col"), move(mine, Z_MIRROR, ("task", "col"))]
    w = down_weight[0]
    own, send, token = project(offs, inputs[0], gate_weight[0], up_weight[0])
    send, token = hold(send, [token, near[1], near[3]])
    ha, away, w_there, token = make_hidden(offs, own, move(send, CORE_SWAP, "row"), w, [token])
    w_here = move(w_there, Z_SWAP)
    hb = move(ha, CORE_SWAP, "row")
    za = move(away, Z_SWAP)
    zb = move(za, CORE_SWAP, "row")

    def ring_terms(p, k, recv, *before):
        at = RING_ROW + k
        d = near[2 * p : 2 * p + 2]
        return terms(offs, [(ha, hb, d, None, w, (at, at, NEAR + 2 * p))], quarter, recv, False, before)

    def far_terms(k, recv, final, *before):
        return terms(
            offs,
            [
                (ha, hb, far, 0, w, (HERE + k, HERE + k, FAR)),
                (za, zb, far, 1, w_here, (PART + k, PART + k, ALONE)),
            ],
            part, recv, final, before,
        )

    got = [(), ()]
    for k in (1, 2, 3):
        for p in range(2):
            extra = {(3, 0): lambda: [za], (3, 1): lambda: [zb, w_here]}.get((k, p), list)()
            piece, token = ring_terms(p, k, got[p], token, *extra)
            got[p] = (move(piece, RING, ("task", "row")),)
            if (k, p) == (2, 0):
                far_pair, token = join(far_mine, token)
                far = [far_pair] + [move(far_pair, x_shift(n), "col") for n in (1, 2, 3)]
    a_sum, a_got, a_all = [None, None], [None, None], [None, None]
    a_sum[0], token = ring_terms(0, 0, got[0], token)
    a_got[0] = move(a_sum[0], Z_SWAP)
    b_got = ()
    for k in (1, 2, 3):
        piece, token = far_terms(k, b_got, False, token)
        b_got = (move(piece, RING, ("task", "row")),)
        if k == 1:
            a_sum[1], token = ring_terms(1, 0, got[1], token)
            a_got[1] = move(a_sum[1], Z_SWAP)
        if k == 2:
            out, token = merge(a_sum[0], a_got[0], token)
            a_all[0] = [out] + [move(out, y_shift(k)) for k in (1, 2, 3)]
        if k == 3:
            out, token = merge(a_sum[1], a_got[1], token)
            a_all[1] = [out] + [move(out, y_shift(k)) for k in (1, 2, 3)]
    b_out, token = far_terms(0, b_got, True, token)
    b_near = [b_out] + [move(b_out, y_shift(k)) for k in (1, 2, 3)]
    b_far = [move(piece, Z_SWAP) for piece in b_near]

    plan = []
    for k in range(4):
        plan += [(4 * p + k, None, quarter, BACK + k, NEAR + 2 * p, 2) for p in range(2)]
        plan += [(8 + k, None, part, BACK_HERE + k, FAR, 4), (12 + k, None, part, BACK_AWAY + k, FAR, 4)]
    return place((width, wide), offs, [*a_all[0], *a_all[1], *b_near, *b_far], plan, [token])


def solution(mesh):
    placed = (
        P("task", None, "row"),
        P("task", "row", "col"),
        P("task", "row", "col"),
        P("task", None, ("row", "col")),
        P("task", "col", "row"),
    )
    return jax.shard_map(
        body, mesh=mesh, in_specs=placed, out_specs=P("col", "row"), check_vma=False
    )
```

time: 964 us -> 216 us (0.22)
  waiting for transfers between devices: 863 us -> 104 us
  starting transfers between devices: 0.09 us -> 76.3 us
  matrix products: 49.4 us -> 0 us
  Pallas kernels: 0 us -> 33.9 us
  other arithmetic: 29.1 us -> 0.01 us
  between operations: 14.9 us -> 0.39 us
    psum x2 -> x0, waiting for transfers between devices: 855 us -> none  [the longest x1 818 us: body(): total_num, total_den = lax.psum((numer, weight.astype(jnp.float32)), 'task')]
    ppermute x0 -> x37, waiting for transfers between devices: none -> 104 us  [move(): return lax.ppermute(x, axis, perm)]
    ppermute x0 -> x37, starting transfers between devices: none -> 76.3 us  [move(): return lax.ppermute(x, axis, perm)]
    dot_general x6 -> x0, matrix products: 49.4 us -> none  [the longest x4 35.7 us: accumulate(): lax.dot_general(h_rows, d_rows, (((0,), (0,)), ((), ())), preferred_eleme...]
    pallas_call x0 -> x19, Pallas kernels: none -> 33.9 us  [the longest x12 18.4 us: terms(): pl.pallas_call(functools.partial(term_kernel, rows, nb, [s[5] for s in so...]
    convert_element_type x3 -> x0, other arithmetic: 29.1 us -> none  [the longest x1 14 us: body(): total_num, total_den = lax.psum((numer, weight.astype(jnp.float32)), 'task')]
  transfers between devices with their start and end apart: 3 -> 37, of which waited for: 3 -> 19; matrix products, arithmetic and copies ran while one was open for 0% -> 0% of each run, Pallas kernels for 0% -> 13%
where the time goes in v1:
time: 216 us; the launch traced here: 214 us
  waiting for transfers between devices  104 us (48%)
  starting transfers between devices  76.3 us (35%)
  Pallas kernels  33.9 us (16%)
    ppermute x37, waiting for transfers between devices, move(): return lax.ppermute(x, axis, perm)  104 us
    ppermute x37, starting transfers between devices, move(): return lax.ppermute(x, axis, perm)  76.3 us
    pallas_call x12, Pallas kernels, terms(): pl.pallas_call(functools.partial(term_kernel, rows, nb, [s[5] for s in so...  18.4 us
    pallas_call x1, Pallas kernels, project(): pl.pallas_call(functools.partial(project_kernel, step), in_specs=[SMEM] +...  10.5 us
  transfers between devices with their start and end apart: 37, of which 19 were waited for; matrix products, arithmetic and copies ran while one was open for 0% of the time, Pallas kernels for 13%

profile of v1, /device:TPU:56, one launch (start us, length us, event | category | flops | bytes accessed | tf_op | source)
XLA Modules:
  0.0 214.3 jit_solution(7254774904407006051)
XLA Ops:
  0.0 2.8 %collective-permute-start.1 = (bf16[512,256]{1,0:T(8,128)(2,1)}, bf16[512,256]{1,0:T(8,128)(2,1)S(1)}, u32[]{:S(2)}, u32[]{:S(2)}) collective-permute-start(bf16[512,256]{1,0:T(8,128)(2,1)} %bitcast.57), channel_id=1, source_target_pairs={{0,3},{1,0},{2,1},{3,2},{4,7},{5,4},{6,5},{7,6},{8,11},{9,8},{10,9... | collective-permute-start | bytes 786440 | tf_op jit(solution)/shard_map/ppermute | solution.py:52
  2.9 10.5 %shard_map.55 = (f32[2,256,1280]{2,1,0:T(8,128)S(1)}, bf16[2,256,1280]{2,1,0:T(8,128)(2,1)S(1)}, f32[8,128]{1,0:T(8,128)S(1)}) custom-call(s32[39]{0:T(128)S(1)} %stack.153.offs, bf16[512,2048]{1,0:T(8,128)(2,1)} %bitcast.68, bf16[2048,1280]{1,0:T(8,128)(2,1)} %bitcast.66, bf16[2048,1280]{1,0:T(8,128)(2,1)} %bitcast.67), custom_call_target="tpu_custom_call" | custom-call | tf_op jit(solution)/shard_map/pallas_call | solution.py:95
  13.5 3.0 %collective-permute-done.2.recv_ref = bf16[2,256,1280]{2,1,0:T(8,128)(2,1)S(1)} collective-permute-done((bf16[2,256,1280]{2,1,0:T(8,128)(2,1)S(1)}, bf16[2,256,1280]{2,1,0:T(8,128)(2,1)S(1)}, u32[]{:S(2)}, u32[]{:S(2)}) %collective-permute-start.2) | collective-permute-done | bytes 1310752 | tf_op jit(solution)/shard_map/ppermute | solution.py:52
  18.1 2.0 collective-permute-done.3.refs_1_
  21.9 3.0 %collective-permute-start.14 = (bf16[640,1024]{1,0:T(8,128)(2,1)S(1)}, bf16[640,1024]{1,0:T(8,128)(2,1)S(1)}, u32[]{:S(2)}, u32[]{:S(2)}) collective-permute-start(bf16[640,1024]{1,0:T(8,128)(2,1)S(1)} %get-tuple-element.63), channel_id=1, source_target_pairs={{0,16},{16,0},{32,48},{48,32},{64,80},{80,64},{96,112},{112,96},{1... | collective-permute-start | bytes 3932168 | tf_op jit(solution)/shard_map/ppermute | solution.py:52
  24.9 2.3 %collective-permute-start.5 = (bf16[512,256]{1,0:T(8,128)(2,1)S(1)}, bf16[512,256]{1,0:T(8,128)(2,1)S(1)}, u32[]{:S(2)}, u32[]{:S(2)}) collective-permute-start(bf16[512,256]{1,0:T(8,128)(2,1)S(1)} %bitcast.60), channel_id=1, source_target_pairs={{0,2},{1,3},{2,0},{3,1},{4,6},{5,7},{6,4},{7,5},{8,10},{9,11},{10,... | collective-permute-start | bytes 786440 | tf_op jit(solution)/shard_map/ppermute | solution.py:52
  27.2 7.5 %collective-permute-done.5.refs_2_ = bf16[512,256]{1,0:T(8,128)(2,1)S(1)} collective-permute-done((bf16[512,256]{1,0:T(8,128)(2,1)S(1)}, bf16[512,256]{1,0:T(8,128)(2,1)S(1)}, u32[]{:S(2)}, u32[]{:S(2)}) %collective-permute-start.5) | collective-permute-done | bytes 262176 | tf_op jit(solution)/shard_map/ppermute | solution.py:52
  36.2 2.5 %collective-permute-start.7 = (bf16[2,320,512]{2,1,0:T(8,128)(2,1)S(1)}, bf16[2,320,512]{2,1,0:T(8,128)(2,1)S(1)}, u32[]{:S(2)}, u32[]{:S(2)}) collective-permute-start(bf16[2,320,512]{2,1,0:T(8,128)(2,1)S(1)} %get-tuple-element.55), channel_id=1, source_target_pairs={{0,32},{8,104},{16,48},{24,120},{32,64},{40,8},{48,80},{56,24},{64... | collective-permute-start | bytes 1966088 | tf_op jit(solution)/shard_map/ppermute | solution.py:52
  38.6 1.6 shard_map.60
  40.4 3.1 %collective-permute-start.10 = (bf16[640,256]{1,0:T(8,128)(2,1)S(1)}, bf16[640,256]{1,0:T(8,128)(2,1)S(1)}, u32[]{:S(2)}, u32[]{:S(2)}) collective-permute-start(bf16[640,256]{1,0:T(8,128)(2,1)S(1)} %get-tuple-element.59), channel_id=1, source_target_pairs={{0,16},{16,0},{32,48},{48,32},{64,80},{80,64},{96,112},{112,96},{1... | collective-permute-start | bytes 983048 | tf_op jit(solution)/shard_map/ppermute | solution.py:52
  43.5 23.6 %collective-permute-done.9.refs_1_ = bf16[512,256]{1,0:T(8,128)(2,1)S(1)} collective-permute-done((bf16[512,256]{1,0:T(8,128)(2,1)S(1)}, bf16[512,256]{1,0:T(8,128)(2,1)S(1)}, u32[]{:S(2)}, u32[]{:S(2)}) %collective-permute-start.9) | collective-permute-done | bytes 262176 | tf_op jit(solution)/shard_map/ppermute | solution.py:52
  67.8 7.5 %collective-permute-done.8.refs_0_ = bf16[512,256]{1,0:T(8,128)(2,1)S(1)} collective-permute-done((bf16[512,256]{1,0:T(8,128)(2,1)S(1)}, bf16[512,256]{1,0:T(8,128)(2,1)S(1)}, u32[]{:S(2)}, u32[]{:S(2)}) %collective-permute-start.8) | collective-permute-done | bytes 262176 | tf_op jit(solution)/shard_map/ppermute | solution.py:52
  75.4 1.6 shard_map.62
  76.9 2.2 %collective-permute-start.12 = (bf16[2,320,512]{2,1,0:T(8,128)(2,1)S(1)}, bf16[2,320,512]{2,1,0:T(8,128)(2,1)S(1)}, u32[]{:S(2)}, u32[]{:S(2)}) collective-permute-start(bf16[2,320,512]{2,1,0:T(8,128)(2,1)S(1)} %get-tuple-element.61), channel_id=1, source_target_pairs={{0,32},{8,104},{16,48},{24,120},{32,64},{40,8},{48,80},{56,24},{64... | collective-permute-start | bytes 1966088 | tf_op jit(solution)/shard_map/ppermute | solution.py:52
  79.2 1.6 shard_map.63
  80.8 3.3 %collective-permute-start.18 = (bf16[2,512,256]{2,1,0:T(8,128)(2,1)S(1)}, bf16[2,512,256]{2,1,0:T(8,128)(2,1)S(1)}, u32[]{:S(2)}, u32[]{:S(2)}) collective-permute-start(bf16[2,512,256]{2,1,0:T(8,128)(2,1)S(1)} %get-tuple-element.66.refs_2_.refs_9_), channel_id=1, source_target_pairs={{0,3},{1,0},{2,1},{3,2},{4,7},{5,4},{6,5},{7,6},{8,11},{9,8},{10,9... | collective-permute-start | bytes 1572872 | tf_op jit(solution)/shard_map/ppermute | solution.py:52
  85.1 2.5 %collective-permute-done.12.refs_5_ = bf16[2,320,512]{2,1,0:T(8,128)(2,1)S(1)} collective-permute-done((bf16[2,320,512]{2,1,0:T(8,128)(2,1)S(1)}, bf16[2,320,512]{2,1,0:T(8,128)(2,1)S(1)}, u32[]{:S(2)}, u32[]{:S(2)}) %collective-permute-start.12) | collective-permute-done | bytes 655392 | tf_op jit(solution)/shard_map/ppermute | solution.py:52
  87.6 1.6 shard_map.64
  89.2 3.4 %collective-permute-start.20 = (bf16[2,320,512]{2,1,0:T(8,128)(2,1)S(1)}, bf16[2,320,512]{2,1,0:T(8,128)(2,1)S(1)}, u32[]{:S(2)}, u32[]{:S(2)}) collective-permute-start(bf16[2,320,512]{2,1,0:T(8,128)(2,1)S(1)} %get-tuple-element.69), channel_id=1, source_target_pairs={{0,32},{8,104},{16,48},{24,120},{32,64},{40,8},{48,80},{56,24},{64... | collective-permute-start | bytes 1966088 | tf_op jit(solution)/shard_map/ppermute | solution.py:52
  92.6 2.0 collective-permute-done.11.refs_5_
  94.6 1.6 shard_map.65
  96.2 7.8 %collective-permute-done.18.refs_5_.refs_12_ = bf16[2,512,256]{2,1,0:T(8,128)(2,1)S(1)} collective-permute-done((bf16[2,512,256]{2,1,0:T(8,128)(2,1)S(1)}, bf16[2,512,256]{2,1,0:T(8,128)(2,1)S(1)}, u32[]{:S(2)}, u32[]{:S(2)}) %collective-permute-start.18) | collective-permute-done | bytes 524320 | tf_op jit(solution)/shard_map/ppermute | solution.py:52
  104.0 3.5 %collective-permute-done.16.refs_3_.refs_10_ = bf16[2,512,256]{2,1,0:T(8,128)(2,1)S(1)} collective-permute-done((bf16[2,512,256]{2,1,0:T(8,128)(2,1)S(1)}, bf16[2,512,256]{2,1,0:T(8,128)(2,1)S(1)}, u32[]{:S(2)}, u32[]{:S(2)}) %collective-permute-start.16) | collective-permute-done | bytes 524320 | tf_op jit(solution)/shard_map/ppermute | solution.py:52
  108.9 2.9 %collective-permute-start.19 = (bf16[2,160,1024]{2,1,0:T(8,128)(2,1)S(1)}, bf16[2,160,1024]{2,1,0:T(8,128)(2,1)S(1)}, u32[]{:S(2)}, u32[]{:S(2)}) collective-permute-start(bf16[2,160,1024]{2,1,0:T(8,128)(2,1)S(1)} %get-tuple-element.68), channel_id=1, source_target_pairs={{0,32},{8,104},{16,48},{24,120},{32,64},{40,8},{48,80},{56,24},{64... | collective-permute-start | bytes 1966088 | tf_op jit(solution)/shard_map/ppermute | solution.py:52
  111.8 3.0 %collective-permute-start.15 = (bf16[2,320,512]{2,1,0:T(8,128)(2,1)S(1)}, bf16[2,320,512]{2,1,0:T(8,128)(2,1)S(1)}, u32[]{:S(2)}, u32[]{:S(2)}) collective-permute-start(bf16[2,320,512]{2,1,0:T(8,128)(2,1)S(1)} %get-tuple-element.65.a), channel_id=1, source_target_pairs={{0,16},{16,0},{32,48},{48,32},{64,80},{80,64},{96,112},{112,96},{1... | collective-permute-start | bytes 1966088 | tf_op jit(solution)/shard_map/ppermute | solution.py:52
  114.8 1.6 shard_map.67
  116.3 3.9 %collective-permute-done.19.refs_14_ = bf16[2,160,1024]{2,1,0:T(8,128)(2,1)S(1)} collective-permute-done((bf16[2,160,1024]{2,1,0:T(8,128)(2,1)S(1)}, bf16[2,160,1024]{2,1,0:T(8,128)(2,1)S(1)}, u32[]{:S(2)}, u32[]{:S(2)}) %collective-permute-start.19) | collective-permute-done | bytes 655392 | tf_op jit(solution)/shard_map/ppermute | solution.py:52
  121.8 3.4 %collective-permute-start.25 = (bf16[2,160,1024]{2,1,0:T(8,128)(2,1)S(1)}, bf16[2,160,1024]{2,1,0:T(8,128)(2,1)S(1)}, u32[]{:S(2)}, u32[]{:S(2)}) collective-permute-start(bf16[2,160,1024]{2,1,0:T(8,128)(2,1)S(1)} %get-tuple-element.75), channel_id=1, source_target_pairs={{0,32},{8,104},{16,48},{24,120},{32,64},{40,8},{48,80},{56,24},{64... | collective-permute-start | bytes 1966088 | tf_op jit(solution)/shard_map/ppermute | solution.py:52
  125.2 3.0 %collective-permute-start.24 = (bf16[2,320,512]{2,1,0:T(8,128)(2,1)S(1)}, bf16[2,320,512]{2,1,0:T(8,128)(2,1)S(1)}, u32[]{:S(2)}, u32[]{:S(2)}) collective-permute-start(bf16[2,320,512]{2,1,0:T(8,128)(2,1)S(1)} %get-tuple-element.74.a), channel_id=1, source_target_pairs={{0,16},{16,0},{32,48},{48,32},{64,80},{80,64},{96,112},{112,96},{1... | collective-permute-start | bytes 1966088 | tf_op jit(solution)/shard_map/ppermute | solution.py:52
  128.2 2.8 %collective-permute-done.15.b = bf16[2,320,512]{2,1,0:T(8,128)(2,1)S(1)} collective-permute-done((bf16[2,320,512]{2,1,0:T(8,128)(2,1)S(1)}, bf16[2,320,512]{2,1,0:T(8,128)(2,1)S(1)}, u32[]{:S(2)}, u32[]{:S(2)}) %collective-permute-start.15) | collective-permute-done | bytes 655392 | tf_op jit(solution)/shard_map/ppermute | solution.py:52
  131.2 2.1 collective-permute-done.25.refs_14_
  134.8 3.8 %collective-permute-start.29 = (bf16[2,160,1024]{2,1,0:T(8,128)(2,1)S(1)}, bf16[2,160,1024]{2,1,0:T(8,128)(2,1)S(1)}, u32[]{:S(2)}, u32[]{:S(2)}) collective-permute-start(bf16[2,160,1024]{2,1,0:T(8,128)(2,1)S(1)} %get-tuple-element.79), channel_id=1, source_target_pairs={{0,32},{8,104},{16,48},{24,120},{32,64},{40,8},{48,80},{56,24},{64... | collective-permute-start | bytes 1966088 | tf_op jit(solution)/shard_map/ppermute | solution.py:52
  138.6 1.5 collective-permute-start.22
  140.1 1.7 collective-permute-start.21
  141.8 1.6 collective-permute-done.24.b
  144.7 7.8 %collective-permute-done.29.refs_14_ = bf16[2,160,1024]{2,1,0:T(8,128)(2,1)S(1)} collective-permute-done((bf16[2,160,1024]{2,1,0:T(8,128)(2,1)S(1)}, bf16[2,160,1024]{2,1,0:T(8,128)(2,1)S(1)}, u32[]{:S(2)}, u32[]{:S(2)}) %collective-permute-start.29) | collective-permute-done | bytes 655392 | tf_op jit(solution)/shard_map/ppermute | solution.py:52
  152.5 3.2 %collective-permute-start.27 = (bf16[320,512]{1,0:T(8,128)(2,1)S(1)}, bf16[320,512]{1,0:T(8,128)(2,1)S(1)}, u32[]{:S(2)}, u32[]{:S(2)}) collective-permute-start(bf16[320,512]{1,0:T(8,128)(2,1)S(1)} %get-tuple-element.78.refs_4_), channel_id=1, source_target_pairs={{0,64},{16,80},{32,96},{48,112},{64,0},{80,16},{96,32},{112,48},{1... | collective-permute-start | bytes 983048 | tf_op jit(solution)/shard_map/ppermute | solution.py:52
  155.7 1.5 shard_map.72
  157.2 7.4 %collective-permute-start.32 = (bf16[160,1024]{1,0:T(8,128)(2,1)S(1)}, bf16[160,1024]{1,0:T(8,128)(2,1)S(1)}, u32[]{:S(2)}, u32[]{:S(2)}) collective-permute-start(bf16[160,1024]{1,0:T(8,128)(2,1)S(1)} %get-tuple-element.81.refs_8_), channel_id=1, source_target_pairs={{0,96},{16,112},{32,0},{48,16},{64,32},{80,48},{96,64},{112,80},{1... | collective-permute-start | bytes 983048 | tf_op jit(solution)/shard_map/ppermute | solution.py:52
  165.3 2.2 %collective-permute-start.30 = (bf16[160,1024]{1,0:T(8,128)(2,1)S(1)}, bf16[160,1024]{1,0:T(8,128)(2,1)S(1)}, u32[]{:S(2)}, u32[]{:S(2)}) collective-permute-start(bf16[160,1024]{1,0:T(8,128)(2,1)S(1)} %get-tuple-element.81.refs_8_), channel_id=1, source_target_pairs={{0,32},{16,48},{32,64},{48,80},{64,96},{80,112},{96,0},{112,16},{1... | collective-permute-start | bytes 983048 | tf_op jit(solution)/shard_map/ppermute | solution.py:52
  170.0 4.0 %collective-permute-start.33 = (bf16[160,1024]{1,0:T(8,128)(2,1)S(1)}, bf16[160,1024]{1,0:T(8,128)(2,1)S(1)}, u32[]{:S(2)}, u32[]{:S(2)}) collective-permute-start(bf16[160,1024]{1,0:T(8,128)(2,1)S(1)} %get-tuple-element.81.refs_8_), channel_id=1, source_target_pairs={{0,16},{16,0},{32,48},{48,32},{64,80},{80,64},{96,112},{112,96},{1... | collective-permute-start | bytes 983048 | tf_op jit(solution)/shard_map/ppermute | solution.py:52
  174.0 6.1 %collective-permute-done.32.refs_11_ = bf16[160,1024]{1,0:T(8,128)(2,1)S(1)} collective-permute-done((bf16[160,1024]{1,0:T(8,128)(2,1)S(1)}, bf16[160,1024]{1,0:T(8,128)(2,1)S(1)}, u32[]{:S(2)}, u32[]{:S(2)}) %collective-permute-start.32) | collective-permute-done | bytes 327712 | tf_op jit(solution)/shard_map/ppermute | solution.py:52
  180.1 8.5 %collective-permute-start.36 = (bf16[160,1024]{1,0:T(8,128)(2,1)S(1)}, bf16[160,1024]{1,0:T(8,128)(2,1)S(1)}, u32[]{:S(2)}, u32[]{:S(2)}) collective-permute-start(bf16[160,1024]{1,0:T(8,128)(2,1)S(1)} %collective-permute-done.32.refs_11_), channel_id=1, source_target_pairs={{0,16},{16,0},{32,48},{48,32},{64,80},{80,64},{96,112},{112,96},{1... | collective-permute-start | bytes 983048 | tf_op jit(solution)/shard_map/ppermute | solution.py:52
  188.7 3.5 %collective-permute-start.34 = (bf16[160,1024]{1,0:T(8,128)(2,1)S(1)}, bf16[160,1024]{1,0:T(8,128)(2,1)S(1)}, u32[]{:S(2)}, u32[]{:S(2)}) collective-permute-start(bf16[160,1024]{1,0:T(8,128)(2,1)S(1)} %collective-permute-done.30.refs_9_), channel_id=1, source_target_pairs={{0,16},{16,0},{32,48},{48,32},{64,80},{80,64},{96,112},{112,96},{1... | collective-permute-start | bytes 983048 | tf_op jit(solution)/shard_map/ppermute | solution.py:52
  192.2 4.7 %collective-permute-done.36.refs_15_ = bf16[160,1024]{1,0:T(8,128)(2,1)S(1)} collective-permute-done((bf16[160,1024]{1,0:T(8,128)(2,1)S(1)}, bf16[160,1024]{1,0:T(8,128)(2,1)S(1)}, u32[]{:S(2)}, u32[]{:S(2)}) %collective-permute-start.36) | collective-permute-done | bytes 327712 | tf_op jit(solution)/shard_map/ppermute | solution.py:52
  196.9 7.0 %collective-permute-done.35.refs_14_ = bf16[160,1024]{1,0:T(8,128)(2,1)S(1)} collective-permute-done((bf16[160,1024]{1,0:T(8,128)(2,1)S(1)}, bf16[160,1024]{1,0:T(8,128)(2,1)S(1)}, u32[]{:S(2)}, u32[]{:S(2)}) %collective-permute-start.35) | collective-permute-done | bytes 327712 | tf_op jit(solution)/shard_map/ppermute | solution.py:52
  203.9 7.0 %collective-permute-done.34.refs_13_ = bf16[160,1024]{1,0:T(8,128)(2,1)S(1)} collective-permute-done((bf16[160,1024]{1,0:T(8,128)(2,1)S(1)}, bf16[160,1024]{1,0:T(8,128)(2,1)S(1)}, u32[]{:S(2)}, u32[]{:S(2)}) %collective-permute-start.34) | collective-permute-done | bytes 327712 | tf_op jit(solution)/shard_map/ppermute | solution.py:52
  210.9 3.3 %shard_map.73 = bf16[1280,2048]{1,0:T(8,128)(2,1)} custom-call(s32[39]{0:T(128)S(1)} %stack.153.offs, bf16[320,512]{1,0:T(8,128)(2,1)S(1)} %get-tuple-element.73.refs_0_, bf16[320,512]{1,0:T(8,128)(2,1)S(1)} %collective-permute-done.21.refs_1_, bf16[320,512]{1,0:T(8,128)(2,1)S(1)} %collective-permute-done.22.refs_2_, ...), custom_call_target="tpu_custom_call" | custom-call | tf_op jit(solution)/shard_map/pallas_call | solution.py:281
  (53 shorter events, 16.3 us)
Async XLA Ops:
  0.0 13.4 %collective-permute-start.1 = (bf16[512,256]{1,0:T(8,128)(2,1)}, bf16[512,256]{1,0:T(8,128)(2,1)S(1)}, u32[]{:S(2)}, u32[]{:S(2)}) collective-permute-start(bf16[512,256]{1,0:T(8,128)(2,1)} %bitcast.57), channel_id=1, source_target_pairs={{0,3},{1,0},{2,1},{3,2},{4,7},{5,4},{6,5},{7,6},{8,11},{9,8},{10,9... | collective-permute-start | bytes 786440 | tf_op jit(solution)/shard_map/ppermute | solution.py:52
  2.8 10.7 %collective-permute-start = (bf16[512,256]{1,0:T(8,128)(2,1)}, bf16[512,256]{1,0:T(8,128)(2,1)S(1)}, u32[]{:S(2)}, u32[]{:S(2)}) collective-permute-start(bf16[512,256]{1,0:T(8,128)(2,1)} %bitcast.58), channel_id=1, source_target_pairs={{0,1},{1,2},{2,3},{3,0},{4,5},{5,6},{6,7},{7,4},{8,9},{9,10},{10,1... | collective-permute-start | bytes 786440 | tf_op jit(solution)/shard_map/ppermute | solution.py:52
  2.9 13.7 %slice-start = ((s8[5242880]{0:T(1024)(128)(4,1)}), s8[4194304]{0:T(1024)(128)(4,1)S(1)}, s32[]{:S(2)}) async-start(s8[5242880]{0:T(1024)(128)(4,1)} %bitcast.42), calls=%async_computation | async-start | bytes 8388608
  2.9 13.7 %slice-start.1 = ((s8[5242880]{0:T(1024)(128)(4,1)}), s8[1048576]{0:T(1024)(128)(4,1)S(1)}, s32[]{:S(2)}) async-start(s8[5242880]{0:T(1024)(128)(4,1)} %bitcast.42), calls=%async_computation.1 | async-start | bytes 2097152
  13.4 3.1 %collective-permute-start.2 = (bf16[2,256,1280]{2,1,0:T(8,128)(2,1)S(1)}, bf16[2,256,1280]{2,1,0:T(8,128)(2,1)S(1)}, u32[]{:S(2)}, u32[]{:S(2)}) collective-permute-start(bf16[2,256,1280]{2,1,0:T(8,128)(2,1)S(1)} %get-tuple-element.47), channel_id=1, source_target_pairs={{0,8},{8,0},{1,9},{9,1},{2,10},{10,2},{3,11},{11,3},{4,12},{12,4},... | collective-permute-start | bytes 3932168 | tf_op jit(solution)/shard_map/ppermute | solution.py:52
  16.6 3.5 %copy-start = (bf16[1,512,256]{2,1,0:T(8,128)(2,1)S(1)}, bf16[1,512,256]{2,1,0:T(8,128)(2,1)}, u32[]{:S(2)}) copy-start(bf16[1,512,256]{2,1,0:T(8,128)(2,1)} %param.8) | copy-start | bytes 786436
  17.9 2.2 %collective-permute-start.3 = (bf16[1280,256]{1,0:T(8,128)(2,1)S(1)}, bf16[1280,256]{1,0:T(8,128)(2,1)S(1)}, u32[]{:S(2)}, u32[]{:S(2)}) collective-permute-start(bf16[1280,256]{1,0:T(8,128)(2,1)S(1)} %get-tuple-element.49.refs_0_), channel_id=1, source_target_pairs={{0,8},{8,0},{1,9},{9,1},{2,10},{10,2},{3,11},{11,3},{4,12},{12,4},... | collective-permute-start | bytes 1966088 | tf_op jit(solution)/shard_map/ppermute | solution.py:52
  21.6 17.1 %collective-permute-start.4 = (bf16[2,320,512]{2,1,0:T(8,128)(2,1)S(1)}, bf16[2,320,512]{2,1,0:T(8,128)(2,1)S(1)}, u32[]{:S(2)}, u32[]{:S(2)}) collective-permute-start(bf16[2,320,512]{2,1,0:T(8,128)(2,1)S(1)} %get-tuple-element.51), channel_id=1, source_target_pairs={{0,32},{8,104},{16,48},{24,120},{32,64},{40,8},{48,80},{56,24},{64... | collective-permute-start | bytes 1966088 | tf_op jit(solution)/shard_map/ppermute | solution.py:52
  21.9 62.3 %collective-permute-start.14 = (bf16[640,1024]{1,0:T(8,128)(2,1)S(1)}, bf16[640,1024]{1,0:T(8,128)(2,1)S(1)}, u32[]{:S(2)}, u32[]{:S(2)}) collective-permute-start(bf16[640,1024]{1,0:T(8,128)(2,1)S(1)} %get-tuple-element.63), channel_id=1, source_target_pairs={{0,16},{16,0},{32,48},{48,32},{64,80},{80,64},{96,112},{112,96},{1... | collective-permute-start | bytes 3932168 | tf_op jit(solution)/shard_map/ppermute | solution.py:52
  24.9 9.8 %collective-permute-start.5 = (bf16[512,256]{1,0:T(8,128)(2,1)S(1)}, bf16[512,256]{1,0:T(8,128)(2,1)S(1)}, u32[]{:S(2)}, u32[]{:S(2)}) collective-permute-start(bf16[512,256]{1,0:T(8,128)(2,1)S(1)} %bitcast.60), channel_id=1, source_target_pairs={{0,2},{1,3},{2,0},{3,1},{4,6},{5,7},{6,4},{7,5},{8,10},{9,11},{10,... | collective-permute-start | bytes 786440 | tf_op jit(solution)/shard_map/ppermute | solution.py:52
  36.2 39.2 %collective-permute-start.7 = (bf16[2,320,512]{2,1,0:T(8,128)(2,1)S(1)}, bf16[2,320,512]{2,1,0:T(8,128)(2,1)S(1)}, u32[]{:S(2)}, u32[]{:S(2)}) collective-permute-start(bf16[2,320,512]{2,1,0:T(8,128)(2,1)S(1)} %get-tuple-element.55), channel_id=1, source_target_pairs={{0,32},{8,104},{16,48},{24,120},{32,64},{40,8},{48,80},{56,24},{64... | collective-permute-start | bytes 1966088 | tf_op jit(solution)/shard_map/ppermute | solution.py:52
  40.2 39.0 %collective-permute-start.6 = (bf16[2,320,512]{2,1,0:T(8,128)(2,1)S(1)}, bf16[2,320,512]{2,1,0:T(8,128)(2,1)S(1)}, u32[]{:S(2)}, u32[]{:S(2)}) collective-permute-start(bf16[2,320,512]{2,1,0:T(8,128)(2,1)S(1)} %get-tuple-element.54), channel_id=1, source_target_pairs={{0,32},{8,104},{16,48},{24,120},{32,64},{40,8},{48,80},{56,24},{64... | collective-permute-start | bytes 1966088 | tf_op jit(solution)/shard_map/ppermute | solution.py:52
  40.3 26.8 %collective-permute-start.9 = (bf16[512,256]{1,0:T(8,128)(2,1)S(1)}, bf16[512,256]{1,0:T(8,128)(2,1)S(1)}, u32[]{:S(2)}, u32[]{:S(2)}) collective-permute-start(bf16[512,256]{1,0:T(8,128)(2,1)S(1)} %bitcast.62), channel_id=1, source_target_pairs={{0,20},{1,21},{2,22},{3,23},{4,16},{5,17},{6,18},{7,19},{16,4},{17... | collective-permute-start | bytes 786440 | tf_op jit(solution)/shard_map/ppermute | solution.py:52
  40.4 27.4 %collective-permute-start.10 = (bf16[640,256]{1,0:T(8,128)(2,1)S(1)}, bf16[640,256]{1,0:T(8,128)(2,1)S(1)}, u32[]{:S(2)}, u32[]{:S(2)}) collective-permute-start(bf16[640,256]{1,0:T(8,128)(2,1)S(1)} %get-tuple-element.59), channel_id=1, source_target_pairs={{0,16},{16,0},{32,48},{48,32},{64,80},{80,64},{96,112},{112,96},{1... | collective-permute-start | bytes 983048 | tf_op jit(solution)/shard_map/ppermute | solution.py:52
  67.1 8.2 %collective-permute-start.8 = (bf16[512,256]{1,0:T(8,128)(2,1)S(1)}, bf16[512,256]{1,0:T(8,128)(2,1)S(1)}, u32[]{:S(2)}, u32[]{:S(2)}) collective-permute-start(bf16[512,256]{1,0:T(8,128)(2,1)S(1)} %bitcast.63), channel_id=1, source_target_pairs={{0,4},{1,5},{2,6},{3,7},{4,0},{5,1},{6,2},{7,3},{8,12},{9,13},{10,... | collective-permute-start | bytes 786440 | tf_op jit(solution)/shard_map/ppermute | solution.py:52
  67.8 16.3 %collective-permute-start.13 = (bf16[640,256]{1,0:T(8,128)(2,1)S(1)}, bf16[640,256]{1,0:T(8,128)(2,1)S(1)}, u32[]{:S(2)}, u32[]{:S(2)}) collective-permute-start(bf16[640,256]{1,0:T(8,128)(2,1)S(1)} %collective-permute-done.10.refs_7_), channel_id=1, source_target_pairs={{0,8},{8,0},{1,9},{9,1},{2,10},{10,2},{3,11},{11,3},{4,12},{12,4},... | collective-permute-start | bytes 983048 | tf_op jit(solution)/shard_map/ppermute | solution.py:52
  76.9 10.7 %collective-permute-start.12 = (bf16[2,320,512]{2,1,0:T(8,128)(2,1)S(1)}, bf16[2,320,512]{2,1,0:T(8,128)(2,1)S(1)}, u32[]{:S(2)}, u32[]{:S(2)}) collective-permute-start(bf16[2,320,512]{2,1,0:T(8,128)(2,1)S(1)} %get-tuple-element.61), channel_id=1, source_target_pairs={{0,32},{8,104},{16,48},{24,120},{32,64},{40,8},{48,80},{56,24},{64... | collective-permute-start | bytes 1966088 | tf_op jit(solution)/shard_map/ppermute | solution.py:52
  80.7 13.9 %collective-permute-start.11 = (bf16[2,320,512]{2,1,0:T(8,128)(2,1)S(1)}, bf16[2,320,512]{2,1,0:T(8,128)(2,1)S(1)}, u32[]{:S(2)}, u32[]{:S(2)}) collective-permute-start(bf16[2,320,512]{2,1,0:T(8,128)(2,1)S(1)} %get-tuple-element.60), channel_id=1, source_target_pairs={{0,32},{8,104},{16,48},{24,120},{32,64},{40,8},{48,80},{56,24},{64... | collective-permute-start | bytes 1966088 | tf_op jit(solution)/shard_map/ppermute | solution.py:52
  80.8 23.1 %collective-permute-start.18 = (bf16[2,512,256]{2,1,0:T(8,128)(2,1)S(1)}, bf16[2,512,256]{2,1,0:T(8,128)(2,1)S(1)}, u32[]{:S(2)}, u32[]{:S(2)}) collective-permute-start(bf16[2,512,256]{2,1,0:T(8,128)(2,1)S(1)} %get-tuple-element.66.refs_2_.refs_9_), channel_id=1, source_target_pairs={{0,3},{1,0},{2,1},{3,2},{4,7},{5,4},{6,5},{7,6},{8,11},{9,8},{10,9... | collective-permute-start | bytes 1572872 | tf_op jit(solution)/shard_map/ppermute | solution.py:52
  84.1 19.8 %collective-permute-start.17 = (bf16[2,512,256]{2,1,0:T(8,128)(2,1)S(1)}, bf16[2,512,256]{2,1,0:T(8,128)(2,1)S(1)}, u32[]{:S(2)}, u32[]{:S(2)}) collective-permute-start(bf16[2,512,256]{2,1,0:T(8,128)(2,1)S(1)} %get-tuple-element.66.refs_2_.refs_9_), channel_id=1, source_target_pairs={{0,2},{1,3},{2,0},{3,1},{4,6},{5,7},{6,4},{7,5},{8,10},{9,11},{10,... | collective-permute-start | bytes 1572872 | tf_op jit(solution)/shard_map/ppermute | solution.py:52
  84.1 23.3 %collective-permute-start.16 = (bf16[2,512,256]{2,1,0:T(8,128)(2,1)S(1)}, bf16[2,512,256]{2,1,0:T(8,128)(2,1)S(1)}, u32[]{:S(2)}, u32[]{:S(2)}) collective-permute-start(bf16[2,512,256]{2,1,0:T(8,128)(2,1)S(1)} %get-tuple-element.66.refs_2_.refs_9_), channel_id=1, source_target_pairs={{0,1},{1,2},{2,3},{3,0},{4,5},{5,6},{6,7},{7,4},{8,9},{9,10},{10,1... | collective-permute-start | bytes 1572872 | tf_op jit(solution)/shard_map/ppermute | solution.py:52
  89.2 25.6 %collective-permute-start.20 = (bf16[2,320,512]{2,1,0:T(8,128)(2,1)S(1)}, bf16[2,320,512]{2,1,0:T(8,128)(2,1)S(1)}, u32[]{:S(2)}, u32[]{:S(2)}) collective-permute-start(bf16[2,320,512]{2,1,0:T(8,128)(2,1)S(1)} %get-tuple-element.69), channel_id=1, source_target_pairs={{0,32},{8,104},{16,48},{24,120},{32,64},{40,8},{48,80},{56,24},{64... | collective-permute-start | bytes 1966088 | tf_op jit(solution)/shard_map/ppermute | solution.py:52
  108.9 11.3 %collective-permute-start.19 = (bf16[2,160,1024]{2,1,0:T(8,128)(2,1)S(1)}, bf16[2,160,1024]{2,1,0:T(8,128)(2,1)S(1)}, u32[]{:S(2)}, u32[]{:S(2)}) collective-permute-start(bf16[2,160,1024]{2,1,0:T(8,128)(2,1)S(1)} %get-tuple-element.68), channel_id=1, source_target_pairs={{0,32},{8,104},{16,48},{24,120},{32,64},{40,8},{48,80},{56,24},{64... | collective-permute-start | bytes 1966088 | tf_op jit(solution)/shard_map/ppermute | solution.py:52
  111.8 19.2 %collective-permute-start.15 = (bf16[2,320,512]{2,1,0:T(8,128)(2,1)S(1)}, bf16[2,320,512]{2,1,0:T(8,128)(2,1)S(1)}, u32[]{:S(2)}, u32[]{:S(2)}) collective-permute-start(bf16[2,320,512]{2,1,0:T(8,128)(2,1)S(1)} %get-tuple-element.65.a), channel_id=1, source_target_pairs={{0,16},{16,0},{32,48},{48,32},{64,80},{80,64},{96,112},{112,96},{1... | collective-permute-start | bytes 1966088 | tf_op jit(solution)/shard_map/ppermute | solution.py:52
  121.8 11.5 %collective-permute-start.25 = (bf16[2,160,1024]{2,1,0:T(8,128)(2,1)S(1)}, bf16[2,160,1024]{2,1,0:T(8,128)(2,1)S(1)}, u32[]{:S(2)}, u32[]{:S(2)}) collective-permute-start(bf16[2,160,1024]{2,1,0:T(8,128)(2,1)S(1)} %get-tuple-element.75), channel_id=1, source_target_pairs={{0,32},{8,104},{16,48},{24,120},{32,64},{40,8},{48,80},{56,24},{64... | collective-permute-start | bytes 1966088 | tf_op jit(solution)/shard_map/ppermute | solution.py:52
  125.2 18.2 %collective-permute-start.24 = (bf16[2,320,512]{2,1,0:T(8,128)(2,1)S(1)}, bf16[2,320,512]{2,1,0:T(8,128)(2,1)S(1)}, u32[]{:S(2)}, u32[]{:S(2)}) collective-permute-start(bf16[2,320,512]{2,1,0:T(8,128)(2,1)S(1)} %get-tuple-element.74.a), channel_id=1, source_target_pairs={{0,16},{16,0},{32,48},{48,32},{64,80},{80,64},{96,112},{112,96},{1... | collective-permute-start | bytes 1966088 | tf_op jit(solution)/shard_map/ppermute | solution.py:52
  134.8 17.7 %collective-permute-start.29 = (bf16[2,160,1024]{2,1,0:T(8,128)(2,1)S(1)}, bf16[2,160,1024]{2,1,0:T(8,128)(2,1)S(1)}, u32[]{:S(2)}, u32[]{:S(2)}) collective-permute-start(bf16[2,160,1024]{2,1,0:T(8,128)(2,1)S(1)} %get-tuple-element.79), channel_id=1, source_target_pairs={{0,32},{8,104},{16,48},{24,120},{32,64},{40,8},{48,80},{56,24},{64... | collective-permute-start | bytes 1966088 | tf_op jit(solution)/shard_map/ppermute | solution.py:52
  138.6 18.7 %collective-permute-start.23 = (bf16[320,512]{1,0:T(8,128)(2,1)S(1)}, bf16[320,512]{1,0:T(8,128)(2,1)S(1)}, u32[]{:S(2)}, u32[]{:S(2)}) collective-permute-start(bf16[320,512]{1,0:T(8,128)(2,1)S(1)} %get-tuple-element.73.refs_0_), channel_id=1, source_target_pairs={{0,96},{16,112},{32,0},{48,16},{64,32},{80,48},{96,64},{112,80},{1... | collective-permute-start | bytes 983048 | tf_op jit(solution)/shard_map/ppermute | solution.py:52
  138.6 26.1 %collective-permute-start.22 = (bf16[320,512]{1,0:T(8,128)(2,1)S(1)}, bf16[320,512]{1,0:T(8,128)(2,1)S(1)}, u32[]{:S(2)}, u32[]{:S(2)}) collective-permute-start(bf16[320,512]{1,0:T(8,128)(2,1)S(1)} %get-tuple-element.73.refs_0_), channel_id=1, source_target_pairs={{0,64},{16,80},{32,96},{48,112},{64,0},{80,16},{96,32},{112,48},{1... | collective-permute-start | bytes 983048 | tf_op jit(solution)/shard_map/ppermute | solution.py:52
  140.1 25.2 %collective-permute-start.21 = (bf16[320,512]{1,0:T(8,128)(2,1)S(1)}, bf16[320,512]{1,0:T(8,128)(2,1)S(1)}, u32[]{:S(2)}, u32[]{:S(2)}) collective-permute-start(bf16[320,512]{1,0:T(8,128)(2,1)S(1)} %get-tuple-element.73.refs_0_), channel_id=1, source_target_pairs={{0,32},{16,48},{32,64},{48,80},{64,96},{80,112},{96,0},{112,16},{1... | collective-permute-start | bytes 983048 | tf_op jit(solution)/shard_map/ppermute | solution.py:52
  143.6 23.9 %collective-permute-start.28 = (bf16[320,512]{1,0:T(8,128)(2,1)S(1)}, bf16[320,512]{1,0:T(8,128)(2,1)S(1)}, u32[]{:S(2)}, u32[]{:S(2)}) collective-permute-start(bf16[320,512]{1,0:T(8,128)(2,1)S(1)} %get-tuple-element.78.refs_4_), channel_id=1, source_target_pairs={{0,96},{16,112},{32,0},{48,16},{64,32},{80,48},{96,64},{112,80},{1... | collective-permute-start | bytes 983048 | tf_op jit(solution)/shard_map/ppermute | solution.py:52
  152.5 17.5 %collective-permute-start.27 = (bf16[320,512]{1,0:T(8,128)(2,1)S(1)}, bf16[320,512]{1,0:T(8,128)(2,1)S(1)}, u32[]{:S(2)}, u32[]{:S(2)}) collective-permute-start(bf16[320,512]{1,0:T(8,128)(2,1)S(1)} %get-tuple-element.78.refs_4_), channel_id=1, source_target_pairs={{0,64},{16,80},{32,96},{48,112},{64,0},{80,16},{96,32},{112,48},{1... | collective-permute-start | bytes 983048 | tf_op jit(solution)/shard_map/ppermute | solution.py:52
  157.2 22.9 %collective-permute-start.32 = (bf16[160,1024]{1,0:T(8,128)(2,1)S(1)}, bf16[160,1024]{1,0:T(8,128)(2,1)S(1)}, u32[]{:S(2)}, u32[]{:S(2)}) collective-permute-start(bf16[160,1024]{1,0:T(8,128)(2,1)S(1)} %get-tuple-element.81.refs_8_), channel_id=1, source_target_pairs={{0,96},{16,112},{32,0},{48,16},{64,32},{80,48},{96,64},{112,80},{1... | collective-permute-start | bytes 983048 | tf_op jit(solution)/shard_map/ppermute | solution.py:52
  164.7 24.0 %collective-permute-start.31 = (bf16[160,1024]{1,0:T(8,128)(2,1)S(1)}, bf16[160,1024]{1,0:T(8,128)(2,1)S(1)}, u32[]{:S(2)}, u32[]{:S(2)}) collective-permute-start(bf16[160,1024]{1,0:T(8,128)(2,1)S(1)} %get-tuple-element.81.refs_8_), channel_id=1, source_target_pairs={{0,64},{16,80},{32,96},{48,112},{64,0},{80,16},{96,32},{112,48},{1... | collective-permute-start | bytes 983048 | tf_op jit(solution)/shard_map/ppermute | solution.py:52
  165.3 23.4 %collective-permute-start.30 = (bf16[160,1024]{1,0:T(8,128)(2,1)S(1)}, bf16[160,1024]{1,0:T(8,128)(2,1)S(1)}, u32[]{:S(2)}, u32[]{:S(2)}) collective-permute-start(bf16[160,1024]{1,0:T(8,128)(2,1)S(1)} %get-tuple-element.81.refs_8_), channel_id=1, source_target_pairs={{0,32},{16,48},{32,64},{48,80},{64,96},{80,112},{96,0},{112,16},{1... | collective-permute-start | bytes 983048 | tf_op jit(solution)/shard_map/ppermute | solution.py:52
  167.5 24.7 %collective-permute-start.26 = (bf16[320,512]{1,0:T(8,128)(2,1)S(1)}, bf16[320,512]{1,0:T(8,128)(2,1)S(1)}, u32[]{:S(2)}, u32[]{:S(2)}) collective-permute-start(bf16[320,512]{1,0:T(8,128)(2,1)S(1)} %get-tuple-element.78.refs_4_), channel_id=1, source_target_pairs={{0,32},{16,48},{32,64},{48,80},{64,96},{80,112},{96,0},{112,16},{1... | collective-permute-start | bytes 983048 | tf_op jit(solution)/shard_map/ppermute | solution.py:52
  170.0 22.2 %collective-permute-start.33 = (bf16[160,1024]{1,0:T(8,128)(2,1)S(1)}, bf16[160,1024]{1,0:T(8,128)(2,1)S(1)}, u32[]{:S(2)}, u32[]{:S(2)}) collective-permute-start(bf16[160,1024]{1,0:T(8,128)(2,1)S(1)} %get-tuple-element.81.refs_8_), channel_id=1, source_target_pairs={{0,16},{16,0},{32,48},{48,32},{64,80},{80,64},{96,112},{112,96},{1... | collective-permute-start | bytes 983048 | tf_op jit(solution)/shard_map/ppermute | solution.py:52
  180.1 16.8 %collective-permute-start.36 = (bf16[160,1024]{1,0:T(8,128)(2,1)S(1)}, bf16[160,1024]{1,0:T(8,128)(2,1)S(1)}, u32[]{:S(2)}, u32[]{:S(2)}) collective-permute-start(bf16[160,1024]{1,0:T(8,128)(2,1)S(1)} %collective-permute-done.32.refs_11_), channel_id=1, source_target_pairs={{0,16},{16,0},{32,48},{48,32},{64,80},{80,64},{96,112},{112,96},{1... | collective-permute-start | bytes 983048 | tf_op jit(solution)/shard_map/ppermute | solution.py:52
  188.6 15.3 %collective-permute-start.35 = (bf16[160,1024]{1,0:T(8,128)(2,1)S(1)}, bf16[160,1024]{1,0:T(8,128)(2,1)S(1)}, u32[]{:S(2)}, u32[]{:S(2)}) collective-permute-start(bf16[160,1024]{1,0:T(8,128)(2,1)S(1)} %collective-permute-done.31.refs_10_), channel_id=1, source_target_pairs={{0,16},{16,0},{32,48},{48,32},{64,80},{80,64},{96,112},{112,96},{1... | collective-permute-start | bytes 983048 | tf_op jit(solution)/shard_map/ppermute | solution.py:52
  188.7 22.2 %collective-permute-start.34 = (bf16[160,1024]{1,0:T(8,128)(2,1)S(1)}, bf16[160,1024]{1,0:T(8,128)(2,1)S(1)}, u32[]{:S(2)}, u32[]{:S(2)}) collective-permute-start(bf16[160,1024]{1,0:T(8,128)(2,1)S(1)} %collective-permute-done.30.refs_9_), channel_id=1, source_target_pairs={{0,16},{16,0},{32,48},{48,32},{64,80},{80,64},{96,112},{112,96},{1... | collective-permute-start | bytes 983048 | tf_op jit(solution)/shard_map/ppermute | solution.py:52

commit v2 on v1

--- a/solution.py
+++ b/solution.py
@@ -128,8 +128,8 @@
     )(x, *before)
 
 
-def hidden_kernel(offs, own_ref, recv_ref, w_ref, *refs):
-    out_ref, away_ref, w_away_ref, token = refs[-4:]
+def hidden_kernel(offs, own_ref, recv_ref, w_ref, c0_ref, c1_ref, *refs):
+    out_ref, away_ref, pair_ref, token = refs[-4:]
     token[...] = jnp.zeros_like(token)
     step = 256
     for n in range(out_ref.shape[0] // step):
@@ -138,45 +138,46 @@
         up = own_ref[1, :, cols] + recv_ref[1, :, cols].astype(F32)
         hidden = jax.nn.gelu(gate, approximate=True) * up
         out_ref[cols, :] = hidden.T.astype(BF)
-    half, wide = w_away_ref.shape
+    half, wide = away_ref.shape
+    wide -= HALF
     rows = pl.ds(pl.multiple_of(offs[1], 16), half)
-    away_ref[...] = out_ref[rows, :]
-    w_away_ref[...] = w_ref[rows, pl.ds(pl.multiple_of(offs[2], BLK), wide)]
-
-
-def make_hidden(offs, own, recv, w, before):
+    away_ref[:, wide:] = out_ref[rows, :]
+    away_ref[:, :wide] = w_ref[rows, pl.ds(pl.multiple_of(offs[2], BLK), wide)]
+    pair_ref[0] = c0_ref[...]
+    pair_ref[1] = c1_ref[...]
+
+
+def make_hidden(offs, own, recv, w, pair, before):
     width = own.shape[2]
     return pl.pallas_call(
         hidden_kernel,
-        in_specs=[SMEM, VMEM, VMEM, VMEM] + [VMEM] * len(before),
+        in_specs=[SMEM] + [VMEM] * (5 + len(before)),
         out_specs=[VMEM] * 4,
         out_shape=[
             jax.ShapeDtypeStruct((width, HALF), BF),
-            jax.ShapeDtypeStruct((width // 2, HALF), BF),
-            jax.ShapeDtypeStruct((w.shape[0] // 2, w.shape[1] // 2), BF),
+            jax.ShapeDtypeStruct((w.shape[0] // 2, w.shape[1] // 2 + HALF), BF),
+            jax.ShapeDtypeStruct((2, *pair[0].shape), BF),
             TOKEN,
         ],
         compiler_params=pltpu.CompilerParams(vmem_limit_bytes=6 * 2**20),
         cost_estimate=FREE,
-    )(offs, own, recv, w, *before)
-
-
-def join_kernel(n, *refs):
-    parts, out, token = refs[:n], refs[-2], refs[-1]
+    )(offs, own, recv, w, *pair, *before)
+
+
+def cut_kernel(a_ref, before, out_ref, token):
     token[...] = jnp.zeros_like(token)
-    for i in range(n):
-        out[i] = parts[i][...]
-
-
-def join(parts, token):
-    return pl.pallas_call(
-        functools.partial(join_kernel, len(parts)),
-        in_specs=[VMEM] * (len(parts) + 1),
+    out_ref[...] = a_ref[:, a_ref.shape[1] - out_ref.shape[1] :]
+
+
+def cut(a, wide, token):
+    return pl.pallas_call(
+        cut_kernel,
+        in_specs=[VMEM, VMEM],
         out_specs=[VMEM, VMEM],
-        out_shape=[jax.ShapeDtypeStruct((len(parts), *parts[0].shape), BF), TOKEN],
+        out_shape=[jax.ShapeDtypeStruct((a.shape[0], wide), BF), TOKEN],
         compiler_params=pltpu.CompilerParams(vmem_limit_bytes=6 * 2**20),
         cost_estimate=FREE,
-    )(*parts, token)
+    )(a, token)
 
 
 def term_kernel(rows, nb, spots, kinds, n_recv, final, offs, *refs):
@@ -198,16 +199,16 @@
             at = pl.multiple_of(i * tile, 16)
             here = pl.ds(at, tile)
             num = den = None
-            for (ha, hb, d, kind, w), (h_spot, w_row_spot, w_col_spot) in zip(parts, spots):
+            for (ha, hb, d, kind, w), (h_spot, a_col, w_row_spot, w_col_spot) in zip(parts, spots):
                 row = pl.multiple_of(offs[h_spot] + at, 16)
                 w_row = pl.multiple_of(offs[w_row_spot] + at, 16)
                 w_col = pl.multiple_of(offs[w_col_spot + j], BLK)
                 weight = jnp.full((tile, BLK), fisher_floor, F32)
-                for h, tok in zip((ha, hb), toks):
+                for h, h_col, tok in zip((ha, hb), (a_col, 0), toks):
                     for e in range(2):
                         there = pl.ds(pl.multiple_of(tok + e * LEN, LEN), LEN)
                         grad = jnp.dot(
-                            h[pl.ds(row, tile), e * LEN : (e + 1) * LEN],
+                            h[pl.ds(row, tile), h_col + e * LEN : h_col + (e + 1) * LEN],
                             d[j][there, :] if kind is None else d[j][kind, there, :],
                             preferred_element_type=F32,
                         )
@@ -319,11 +320,11 @@
     HERE = len(table)
     table += [h * half + (y - k * ring) % 4 * part for k in range(4)]
     BACK = len(table)
-    table += [(y - k) % 4 * quarter for k in range(4)]
+    table += [(y - k * ring) % 4 * quarter for k in range(4)]
     BACK_HERE = len(table)
-    table += [h * half + (y - k) % 4 * part for k in range(4)]
+    table += [h * half + (y - k * ring) % 4 * part for k in range(4)]
     BACK_AWAY = len(table)
-    table += [(1 - h) * half + (y - k) % 4 * part for k in range(4)]
+    table += [(1 - h) * half + (y - k * ring) % 4 * part for k in range(4)]
     offs = ints(*table)
 
     mine = cotangent[0]
@@ -331,37 +332,41 @@
     far_mine = [move(mine, ZLO_SWAP, "col"), move(mine, Z_MIRROR, ("task", "col"))]
     w = down_weight[0]
     own, send, token = project(offs, inputs[0], gate_weight[0], up_weight[0])
-    send, token = hold(send, [token, near[1], near[3]])
-    ha, away, w_there, token = make_hidden(offs, own, move(send, CORE_SWAP, "row"), w, [token])
-    w_here = move(w_there, Z_SWAP)
+    send, token = hold(send, [token, *near[1:], *far_mine])
+    ha, away, far_pair, token = make_hidden(offs, own, move(send, CORE_SWAP, "row"), w, far_mine, [token])
     hb = move(ha, CORE_SWAP, "row")
+    far = [far_pair] + [move(far_pair, x_shift(n), "col") for n in (1, 2, 3)]
     za = move(away, Z_SWAP)
-    zb = move(za, CORE_SWAP, "row")
 
     def ring_terms(p, k, recv, *before):
         at = RING_ROW + k
         d = near[2 * p : 2 * p + 2]
-        return terms(offs, [(ha, hb, d, None, w, (at, at, NEAR + 2 * p))], quarter, recv, False, before)
+        return terms(offs, [(ha, hb, d, None, w, (at, 0, at, NEAR + 2 * p))], quarter, recv, False, before)
 
     def far_terms(k, recv, final, *before):
         return terms(
             offs,
             [
-                (ha, hb, far, 0, w, (HERE + k, HERE + k, FAR)),
-                (za, zb, far, 1, w_here, (PART + k, PART + k, ALONE)),
+                (ha, hb, far, 0, w, (HERE + k, 0, HERE + k, FAR)),
+                (za, zb, far, 1, za, (PART + k, wide // 2, PART + k, ALONE)),
             ],
             part, recv, final, before,
         )
 
+    def around(piece):
+        pieces = [piece]
+        for _ in range(3):
+            pieces.append(move(pieces[-1], RING, ("task", "row")))
+        return pieces
+
     got = [(), ()]
     for k in (1, 2, 3):
         for p in range(2):
-            extra = {(3, 0): lambda: [za], (3, 1): lambda: [zb, w_here]}.get((k, p), list)()
+            extra = {(2, 1): far[1:2], (3, 0): far[3:4], (3, 1): far[2:3]}.get((k, p), [])
             piece, token = ring_terms(p, k, got[p], token, *extra)
             got[p] = (move(piece, RING, ("task", "row")),)
-            if (k, p) == (2, 0):
-                far_pair, token = join(far_mine, token)
-                far = [far_pair] + [move(far_pair, x_shift(n), "col") for n in (1, 2, 3)]
+    zb, token = cut(za, HALF, token)
+    zb = move(zb, CORE_SWAP, "row")
     a_sum, a_got, a_all = [None, None], [None, None], [None, None]
     a_sum[0], token = ring_terms(0, 0, got[0], token)
     a_got[0] = move(a_sum[0], Z_SWAP)
@@ -374,12 +379,12 @@
             a_got[1] = move(a_sum[1], Z_SWAP)
         if k == 2:
             out, token = merge(a_sum[0], a_got[0], token)
-            a_all[0] = [out] + [move(out, y_shift(k)) for k in (1, 2, 3)]
+            a_all[0] = around(out)
         if k == 3:
             out, token = merge(a_sum[1], a_got[1], token)
-            a_all[1] = [out] + [move(out, y_shift(k)) for k in (1, 2, 3)]
+            a_all[1] = around(out)
     b_out, token = far_terms(0, b_got, True, token)
-    b_near = [b_out] + [move(b_out, y_shift(k)) for k in (1, 2, 3)]
+    b_near = around(b_out)
     b_far = [move(piece, Z_SWAP) for piece in b_near]
 
     plan = []

time: 216 us -> 171 us (0.79)
  waiting for transfers between devices: 104 us -> 78.7 us
  starting transfers between devices: 76.3 us -> 54.2 us
    ppermute x37 -> x36, waiting for transfers between devices: 104 us -> 78.7 us  [move(): return lax.ppermute(x, axis, perm)]
    ppermute x37 -> x36, starting transfers between devices: 76.3 us -> 54.2 us  [move(): return lax.ppermute(x, axis, perm)]
  transfers between devices with their start and end apart: 37 -> 36, of which waited for: 19 -> 20; matrix products, arithmetic and copies ran while one was open for 0% -> 0% of each run, Pallas kernels for 13% -> 17%
where the time goes in v2:
time: 171 us; the launch traced here: 167 us
  waiting for transfers between devices  78.7 us (46%)
  starting transfers between devices  54.2 us (32%)
  Pallas kernels  33.9 us (20%)
    ppermute x36, waiting for transfers between devices, move(): return lax.ppermute(x, axis, perm)  78.7 us
    ppermute x36, starting transfers between devices, move(): return lax.ppermute(x, axis, perm)  54.2 us
    pallas_call x12, Pallas kernels, terms(): pl.pallas_call(functools.partial(term_kernel, rows, nb, [s[5] for s in so...  18.4 us
    pallas_call x1, Pallas kernels, project(): pl.pallas_call(functools.partial(project_kernel, step), in_specs=[SMEM] +...  10.5 us
  transfers between devices with their start and end apart: 36, of which 20 were waited for; matrix products, arithmetic and copies ran while one was open for 0% of the time, Pallas kernels for 17%

profile of v2, /device:TPU:56, one launch (start us, length us, event | category | flops | bytes accessed | tf_op | source)
XLA Modules:
  0.0 167.3 jit_solution(7118025598775988681)
XLA Ops:
  0.0 1.9 %collective-permute-start.4 = (bf16[512,256]{1,0:T(8,128)(2,1)}, bf16[512,256]{1,0:T(8,128)(2,1)S(1)}, u32[]{:S(2)}, u32[]{:S(2)}) collective-permute-start(bf16[512,256]{1,0:T(8,128)(2,1)} %bitcast.51), channel_id=1, source_target_pairs={{0,20},{1,21},{2,22},{3,23},{4,16},{5,17},{6,18},{7,19},{16,4},{17... | collective-permute-start | bytes 786440 | tf_op jit(solution)/shard_map/ppermute | solution.py:52
  1.9 2.2 %collective-permute-start.3 = (bf16[512,256]{1,0:T(8,128)(2,1)}, bf16[512,256]{1,0:T(8,128)(2,1)S(1)}, u32[]{:S(2)}, u32[]{:S(2)}) collective-permute-start(bf16[512,256]{1,0:T(8,128)(2,1)} %bitcast.52), channel_id=1, source_target_pairs={{0,4},{1,5},{2,6},{3,7},{4,0},{5,1},{6,2},{7,3},{8,12},{9,13},{10,... | collective-permute-start | bytes 786440 | tf_op jit(solution)/shard_map/ppermute | solution.py:52
  4.1 2.8 %collective-permute-start.2 = (bf16[512,256]{1,0:T(8,128)(2,1)}, bf16[512,256]{1,0:T(8,128)(2,1)S(1)}, u32[]{:S(2)}, u32[]{:S(2)}) collective-permute-start(bf16[512,256]{1,0:T(8,128)(2,1)} %bitcast.53), channel_id=1, source_target_pairs={{0,3},{1,0},{2,1},{3,2},{4,7},{5,4},{6,5},{7,6},{8,11},{9,8},{10,9... | collective-permute-start | bytes 786440 | tf_op jit(solution)/shard_map/ppermute | solution.py:52
  8.7 10.5 %shard_map.55 = (f32[2,256,1280]{2,1,0:T(8,128)S(1)}, bf16[2,256,1280]{2,1,0:T(8,128)(2,1)S(1)}, f32[8,128]{1,0:T(8,128)S(1)}) custom-call(s32[39]{0:T(128)S(1)} %stack.135.offs, bf16[512,2048]{1,0:T(8,128)(2,1)} %bitcast.62, bf16[2048,1280]{1,0:T(8,128)(2,1)} %bitcast.60, bf16[2048,1280]{1,0:T(8,128)(2,1)} %bitcast.61), custom_call_target="tpu_custom_call" | custom-call | tf_op jit(solution)/shard_map/pallas_call | solution.py:95
  19.3 2.2 %collective-permute-done.refs_2_.refs_3_ = bf16[512,256]{1,0:T(8,128)(2,1)S(1)} collective-permute-done((bf16[512,256]{1,0:T(8,128)(2,1)}, bf16[512,256]{1,0:T(8,128)(2,1)S(1)}, u32[]{:S(2)}, u32[]{:S(2)}) %collective-permute-start) | collective-permute-done | bytes 262176 | tf_op jit(solution)/shard_map/ppermute | solution.py:52
  21.5 3.0 %collective-permute-done.5.recv_ref = bf16[2,256,1280]{2,1,0:T(8,128)(2,1)S(1)} collective-permute-done((bf16[2,256,1280]{2,1,0:T(8,128)(2,1)S(1)}, bf16[2,256,1280]{2,1,0:T(8,128)(2,1)S(1)}, u32[]{:S(2)}, u32[]{:S(2)}) %collective-permute-start.5) | collective-permute-done | bytes 1310752 | tf_op jit(solution)/shard_map/ppermute | solution.py:52
  26.1 2.0 %collective-permute-done.6.refs_1_ = bf16[1280,256]{1,0:T(8,128)(2,1)S(1)} collective-permute-done((bf16[1280,256]{1,0:T(8,128)(2,1)S(1)}, bf16[1280,256]{1,0:T(8,128)(2,1)S(1)}, u32[]{:S(2)}, u32[]{:S(2)}) %collective-permute-start.6) | collective-permute-done | bytes 655392 | tf_op jit(solution)/shard_map/ppermute | solution.py:52
  31.3 1.6 collective-permute-start.9
  33.0 7.2 %collective-permute-done.7.refs_5_ = bf16[2,320,512]{2,1,0:T(8,128)(2,1)S(1)} collective-permute-done((bf16[2,320,512]{2,1,0:T(8,128)(2,1)S(1)}, bf16[2,320,512]{2,1,0:T(8,128)(2,1)S(1)}, u32[]{:S(2)}, u32[]{:S(2)}) %collective-permute-start.7) | collective-permute-done | bytes 655392 | tf_op jit(solution)/shard_map/ppermute | solution.py:52
  40.2 1.6 shard_map.60
  41.8 1.7 %collective-permute-start.8 = (bf16[2,320,512]{2,1,0:T(8,128)(2,1)S(1)}, bf16[2,320,512]{2,1,0:T(8,128)(2,1)S(1)}, u32[]{:S(2)}, u32[]{:S(2)}) collective-permute-start(bf16[2,320,512]{2,1,0:T(8,128)(2,1)S(1)} %get-tuple-element.54), channel_id=1, source_target_pairs={{0,32},{8,104},{16,48},{24,120},{32,64},{40,8},{48,80},{56,24},{64... | collective-permute-start | bytes 1966088 | tf_op jit(solution)/shard_map/ppermute | solution.py:52
  44.1 2.9 %collective-permute-done.10.refs_7_.refs_3_.refs_10_ = bf16[2,512,256]{2,1,0:T(8,128)(2,1)S(1)} collective-permute-done((bf16[2,512,256]{2,1,0:T(8,128)(2,1)S(1)}, bf16[2,512,256]{2,1,0:T(8,128)(2,1)S(1)}, u32[]{:S(2)}, u32[]{:S(2)}) %collective-permute-start.10) | collective-permute-done | bytes 524320 | tf_op jit(solution)/shard_map/ppermute | solution.py:52
  47.2 1.6 shard_map.61
  48.8 2.6 %collective-permute-start.14 = (bf16[2,320,512]{2,1,0:T(8,128)(2,1)S(1)}, bf16[2,320,512]{2,1,0:T(8,128)(2,1)S(1)}, u32[]{:S(2)}, u32[]{:S(2)}) collective-permute-start(bf16[2,320,512]{2,1,0:T(8,128)(2,1)S(1)} %get-tuple-element.61), channel_id=1, source_target_pairs={{0,32},{8,104},{16,48},{24,120},{32,64},{40,8},{48,80},{56,24},{64... | collective-permute-start | bytes 1966088 | tf_op jit(solution)/shard_map/ppermute | solution.py:52
  51.4 6.9 %collective-permute-done.11.refs_7_.refs_5_.refs_12_ = bf16[2,512,256]{2,1,0:T(8,128)(2,1)S(1)} collective-permute-done((bf16[2,512,256]{2,1,0:T(8,128)(2,1)S(1)}, bf16[2,512,256]{2,1,0:T(8,128)(2,1)S(1)}, u32[]{:S(2)}, u32[]{:S(2)}) %collective-permute-start.11) | collective-permute-done | bytes 524320 | tf_op jit(solution)/shard_map/ppermute | solution.py:52
  58.3 1.6 shard_map.62
  60.0 4.7 %collective-permute-done.15.refs_7_.refs_4_.refs_11_ = bf16[2,512,256]{2,1,0:T(8,128)(2,1)S(1)} collective-permute-done((bf16[2,512,256]{2,1,0:T(8,128)(2,1)S(1)}, bf16[2,512,256]{2,1,0:T(8,128)(2,1)S(1)}, u32[]{:S(2)}, u32[]{:S(2)}) %collective-permute-start.15) | collective-permute-done | bytes 524320 | tf_op jit(solution)/shard_map/ppermute | solution.py:52
  64.6 1.6 shard_map.63
  66.2 3.2 %collective-permute-done.13.a_ref.refs_7_.refs_13_ = bf16[640,1280]{1,0:T(8,128)(2,1)S(1)} collective-permute-done((bf16[640,1280]{1,0:T(8,128)(2,1)S(1)}, bf16[640,1280]{1,0:T(8,128)(2,1)S(1)}, u32[]{:S(2)}, u32[]{:S(2)}) %collective-permute-start.13) | collective-permute-done | bytes 1638432 | tf_op jit(solution)/shard_map/ppermute | solution.py:52
  69.5 2.3 %collective-permute-start.19 = (bf16[2,320,512]{2,1,0:T(8,128)(2,1)S(1)}, bf16[2,320,512]{2,1,0:T(8,128)(2,1)S(1)}, u32[]{:S(2)}, u32[]{:S(2)}) collective-permute-start(bf16[2,320,512]{2,1,0:T(8,128)(2,1)S(1)} %get-tuple-element.69), channel_id=1, source_target_pairs={{0,32},{8,104},{16,48},{24,120},{32,64},{40,8},{48,80},{56,24},{64... | collective-permute-start | bytes 1966088 | tf_op jit(solution)/shard_map/ppermute | solution.py:52
  71.8 1.6 shard_map.65
  74.9 1.7 %collective-permute-start.16 = (bf16[2,320,512]{2,1,0:T(8,128)(2,1)S(1)}, bf16[2,320,512]{2,1,0:T(8,128)(2,1)S(1)}, u32[]{:S(2)}, u32[]{:S(2)}) collective-permute-start(bf16[2,320,512]{2,1,0:T(8,128)(2,1)S(1)} %get-tuple-element.65.a), channel_id=1, source_target_pairs={{0,16},{16,0},{32,48},{48,32},{64,80},{80,64},{96,112},{112,96},{1... | collective-permute-start | bytes 1966088 | tf_op jit(solution)/shard_map/ppermute | solution.py:52
  76.6 3.6 %collective-permute-done.19.refs_5_ = bf16[2,320,512]{2,1,0:T(8,128)(2,1)S(1)} collective-permute-done((bf16[2,320,512]{2,1,0:T(8,128)(2,1)S(1)}, bf16[2,320,512]{2,1,0:T(8,128)(2,1)S(1)}, u32[]{:S(2)}, u32[]{:S(2)}) %collective-permute-start.19) | collective-permute-done | bytes 655392 | tf_op jit(solution)/shard_map/ppermute | solution.py:52
  80.2 1.6 shard_map.67
  81.8 5.5 %collective-permute-done.18.refs_14_ = bf16[2,160,1024]{2,1,0:T(8,128)(2,1)S(1)} collective-permute-done((bf16[2,160,1024]{2,1,0:T(8,128)(2,1)S(1)}, bf16[2,160,1024]{2,1,0:T(8,128)(2,1)S(1)}, u32[]{:S(2)}, u32[]{:S(2)}) %collective-permute-start.18) | collective-permute-done | bytes 655392 | tf_op jit(solution)/shard_map/ppermute | solution.py:52
  87.2 1.5 shard_map.68
  88.7 3.5 %collective-permute-start.24 = (bf16[2,160,1024]{2,1,0:T(8,128)(2,1)S(1)}, bf16[2,160,1024]{2,1,0:T(8,128)(2,1)S(1)}, u32[]{:S(2)}, u32[]{:S(2)}) collective-permute-start(bf16[2,160,1024]{2,1,0:T(8,128)(2,1)S(1)} %get-tuple-element.75), channel_id=1, source_target_pairs={{0,32},{8,104},{16,48},{24,120},{32,64},{40,8},{48,80},{56,24},{64... | collective-permute-start | bytes 1966088 | tf_op jit(solution)/shard_map/ppermute | solution.py:52
  92.4 7.9 %collective-permute-done.24.refs_14_ = bf16[2,160,1024]{2,1,0:T(8,128)(2,1)S(1)} collective-permute-done((bf16[2,160,1024]{2,1,0:T(8,128)(2,1)S(1)}, bf16[2,160,1024]{2,1,0:T(8,128)(2,1)S(1)}, u32[]{:S(2)}, u32[]{:S(2)}) %collective-permute-start.24) | collective-permute-done | bytes 655392 | tf_op jit(solution)/shard_map/ppermute | solution.py:52
  100.3 1.5 shard_map.70
  101.8 3.8 %collective-permute-start.28 = (bf16[2,160,1024]{2,1,0:T(8,128)(2,1)S(1)}, bf16[2,160,1024]{2,1,0:T(8,128)(2,1)S(1)}, u32[]{:S(2)}, u32[]{:S(2)}) collective-permute-start(bf16[2,160,1024]{2,1,0:T(8,128)(2,1)S(1)} %get-tuple-element.79), channel_id=1, source_target_pairs={{0,32},{8,104},{16,48},{24,120},{32,64},{40,8},{48,80},{56,24},{64... | collective-permute-start | bytes 1966088 | tf_op jit(solution)/shard_map/ppermute | solution.py:52
  105.7 2.0 %collective-permute-done.23.b = bf16[2,320,512]{2,1,0:T(8,128)(2,1)S(1)} collective-permute-done((bf16[2,320,512]{2,1,0:T(8,128)(2,1)S(1)}, bf16[2,320,512]{2,1,0:T(8,128)(2,1)S(1)}, u32[]{:S(2)}, u32[]{:S(2)}) %collective-permute-start.23) | collective-permute-done | bytes 655392 | tf_op jit(solution)/shard_map/ppermute | solution.py:52
  107.8 5.8 %collective-permute-done.28.refs_14_ = bf16[2,160,1024]{2,1,0:T(8,128)(2,1)S(1)} collective-permute-done((bf16[2,160,1024]{2,1,0:T(8,128)(2,1)S(1)}, bf16[2,160,1024]{2,1,0:T(8,128)(2,1)S(1)}, u32[]{:S(2)}, u32[]{:S(2)}) %collective-permute-start.28) | collective-permute-done | bytes 655392 | tf_op jit(solution)/shard_map/ppermute | solution.py:52
  113.7 1.5 shard_map.72
  115.2 3.8 %collective-permute-start.29 = (bf16[160,1024]{1,0:T(8,128)(2,1)S(1)}, bf16[160,1024]{1,0:T(8,128)(2,1)S(1)}, u32[]{:S(2)}, u32[]{:S(2)}) collective-permute-start(bf16[160,1024]{1,0:T(8,128)(2,1)S(1)} %get-tuple-element.81.refs_8_), channel_id=1, source_target_pairs={{0,32},{8,104},{16,48},{24,120},{32,64},{40,8},{48,80},{56,24},{64... | collective-permute-start | bytes 983048 | tf_op jit(solution)/shard_map/ppermute | solution.py:52
  119.1 1.8 %collective-permute-start.21 = (bf16[320,512]{1,0:T(8,128)(2,1)S(1)}, bf16[320,512]{1,0:T(8,128)(2,1)S(1)}, u32[]{:S(2)}, u32[]{:S(2)}) collective-permute-start(bf16[320,512]{1,0:T(8,128)(2,1)S(1)} %collective-permute-done.20.refs_1_), channel_id=1, source_target_pairs={{0,32},{8,104},{16,48},{24,120},{32,64},{40,8},{48,80},{56,24},{64... | collective-permute-start | bytes 983048 | tf_op jit(solution)/shard_map/ppermute | solution.py:52
  120.9 2.7 %collective-permute-done.29.refs_9_ = bf16[160,1024]{1,0:T(8,128)(2,1)S(1)} collective-permute-done((bf16[160,1024]{1,0:T(8,128)(2,1)S(1)}, bf16[160,1024]{1,0:T(8,128)(2,1)S(1)}, u32[]{:S(2)}, u32[]{:S(2)}) %collective-permute-start.29) | collective-permute-done | bytes 327712 | tf_op jit(solution)/shard_map/ppermute | solution.py:52
  123.6 3.7 %collective-permute-start.30 = (bf16[160,1024]{1,0:T(8,128)(2,1)S(1)}, bf16[160,1024]{1,0:T(8,128)(2,1)S(1)}, u32[]{:S(2)}, u32[]{:S(2)}) collective-permute-start(bf16[160,1024]{1,0:T(8,128)(2,1)S(1)} %collective-permute-done.29.refs_9_), channel_id=1, source_target_pairs={{0,32},{8,104},{16,48},{24,120},{32,64},{40,8},{48,80},{56,24},{64... | collective-permute-start | bytes 983048 | tf_op jit(solution)/shard_map/ppermute | solution.py:52
  127.3 3.5 %collective-permute-start.26 = (bf16[320,512]{1,0:T(8,128)(2,1)S(1)}, bf16[320,512]{1,0:T(8,128)(2,1)S(1)}, u32[]{:S(2)}, u32[]{:S(2)}) collective-permute-start(bf16[320,512]{1,0:T(8,128)(2,1)S(1)} %collective-permute-done.25.refs_5_), channel_id=1, source_target_pairs={{0,32},{8,104},{16,48},{24,120},{32,64},{40,8},{48,80},{56,24},{64... | collective-permute-start | bytes 983048 | tf_op jit(solution)/shard_map/ppermute | solution.py:52
  130.8 3.5 %collective-permute-start.22 = (bf16[320,512]{1,0:T(8,128)(2,1)S(1)}, bf16[320,512]{1,0:T(8,128)(2,1)S(1)}, u32[]{:S(2)}, u32[]{:S(2)}) collective-permute-start(bf16[320,512]{1,0:T(8,128)(2,1)S(1)} %collective-permute-done.21.refs_2_), channel_id=1, source_target_pairs={{0,32},{8,104},{16,48},{24,120},{32,64},{40,8},{48,80},{56,24},{64... | collective-permute-start | bytes 983048 | tf_op jit(solution)/shard_map/ppermute | solution.py:52
  134.3 3.5 %collective-permute-start.31 = (bf16[160,1024]{1,0:T(8,128)(2,1)S(1)}, bf16[160,1024]{1,0:T(8,128)(2,1)S(1)}, u32[]{:S(2)}, u32[]{:S(2)}) collective-permute-start(bf16[160,1024]{1,0:T(8,128)(2,1)S(1)} %collective-permute-done.30.refs_10_), channel_id=1, source_target_pairs={{0,32},{8,104},{16,48},{24,120},{32,64},{40,8},{48,80},{56,24},{64... | collective-permute-start | bytes 983048 | tf_op jit(solution)/shard_map/ppermute | solution.py:52
  137.8 3.5 %collective-permute-start.27 = (bf16[320,512]{1,0:T(8,128)(2,1)S(1)}, bf16[320,512]{1,0:T(8,128)(2,1)S(1)}, u32[]{:S(2)}, u32[]{:S(2)}) collective-permute-start(bf16[320,512]{1,0:T(8,128)(2,1)S(1)} %collective-permute-done.26.refs_6_), channel_id=1, source_target_pairs={{0,32},{8,104},{16,48},{24,120},{32,64},{40,8},{48,80},{56,24},{64... | collective-permute-start | bytes 983048 | tf_op jit(solution)/shard_map/ppermute | solution.py:52
  141.4 3.5 %collective-permute-start.34 = (bf16[160,1024]{1,0:T(8,128)(2,1)S(1)}, bf16[160,1024]{1,0:T(8,128)(2,1)S(1)}, u32[]{:S(2)}, u32[]{:S(2)}) collective-permute-start(bf16[160,1024]{1,0:T(8,128)(2,1)S(1)} %collective-permute-done.30.refs_10_), channel_id=1, source_target_pairs={{0,16},{16,0},{32,48},{48,32},{64,80},{80,64},{96,112},{112,96},{1... | collective-permute-start | bytes 983048 | tf_op jit(solution)/shard_map/ppermute | solution.py:52
  144.9 3.2 %collective-permute-done.27.refs_7_ = bf16[320,512]{1,0:T(8,128)(2,1)S(1)} collective-permute-done((bf16[320,512]{1,0:T(8,128)(2,1)S(1)}, bf16[320,512]{1,0:T(8,128)(2,1)S(1)}, u32[]{:S(2)}, u32[]{:S(2)}) %collective-permute-start.27) | collective-permute-done | bytes 327712 | tf_op jit(solution)/shard_map/ppermute | solution.py:52
  148.2 1.8 %collective-permute-done.32.refs_12_ = bf16[160,1024]{1,0:T(8,128)(2,1)S(1)} collective-permute-done((bf16[160,1024]{1,0:T(8,128)(2,1)S(1)}, bf16[160,1024]{1,0:T(8,128)(2,1)S(1)}, u32[]{:S(2)}, u32[]{:S(2)}) %collective-permute-start.32) | collective-permute-done | bytes 327712 | tf_op jit(solution)/shard_map/ppermute | solution.py:52
  150.0 6.9 %collective-permute-done.33.refs_13_ = bf16[160,1024]{1,0:T(8,128)(2,1)S(1)} collective-permute-done((bf16[160,1024]{1,0:T(8,128)(2,1)S(1)}, bf16[160,1024]{1,0:T(8,128)(2,1)S(1)}, u32[]{:S(2)}, u32[]{:S(2)}) %collective-permute-start.33) | collective-permute-done | bytes 327712 | tf_op jit(solution)/shard_map/ppermute | solution.py:52
  156.9 3.5 %collective-permute-done.34.refs_14_ = bf16[160,1024]{1,0:T(8,128)(2,1)S(1)} collective-permute-done((bf16[160,1024]{1,0:T(8,128)(2,1)S(1)}, bf16[160,1024]{1,0:T(8,128)(2,1)S(1)}, u32[]{:S(2)}, u32[]{:S(2)}) %collective-permute-start.34) | collective-permute-done | bytes 327712 | tf_op jit(solution)/shard_map/ppermute | solution.py:52
  160.4 3.5 %collective-permute-done.35.refs_15_ = bf16[160,1024]{1,0:T(8,128)(2,1)S(1)} collective-permute-done((bf16[160,1024]{1,0:T(8,128)(2,1)S(1)}, bf16[160,1024]{1,0:T(8,128)(2,1)S(1)}, u32[]{:S(2)}, u32[]{:S(2)}) %collective-permute-start.35) | collective-permute-done | bytes 327712 | tf_op jit(solution)/shard_map/ppermute | solution.py:52
  163.9 3.3 %shard_map.73 = bf16[1280,2048]{1,0:T(8,128)(2,1)} custom-call(s32[39]{0:T(128)S(1)} %stack.135.offs, bf16[320,512]{1,0:T(8,128)(2,1)S(1)} %get-tuple-element.73.refs_0_, bf16[320,512]{1,0:T(8,128)(2,1)S(1)} %collective-permute-done.20.refs_1_, bf16[320,512]{1,0:T(8,128)(2,1)S(1)} %collective-permute-done.21.refs_2_, ...), custom_call_target="tpu_custom_call" | custom-call | tf_op jit(solution)/shard_map/pallas_call | solution.py:282
  (51 shorter events, 9.9 us)
Async XLA Ops:
  0.0 19.2 %collective-permute-start.4 = (bf16[512,256]{1,0:T(8,128)(2,1)}, bf16[512,256]{1,0:T(8,128)(2,1)S(1)}, u32[]{:S(2)}, u32[]{:S(2)}) collective-permute-start(bf16[512,256]{1,0:T(8,128)(2,1)} %bitcast.51), channel_id=1, source_target_pairs={{0,20},{1,21},{2,22},{3,23},{4,16},{5,17},{6,18},{7,19},{16,4},{17... | collective-permute-start | bytes 786440 | tf_op jit(solution)/shard_map/ppermute | solution.py:52
  1.9 17.3 %collective-permute-start.3 = (bf16[512,256]{1,0:T(8,128)(2,1)}, bf16[512,256]{1,0:T(8,128)(2,1)S(1)}, u32[]{:S(2)}, u32[]{:S(2)}) collective-permute-start(bf16[512,256]{1,0:T(8,128)(2,1)} %bitcast.52), channel_id=1, source_target_pairs={{0,4},{1,5},{2,6},{3,7},{4,0},{5,1},{6,2},{7,3},{8,12},{9,13},{10,... | collective-permute-start | bytes 786440 | tf_op jit(solution)/shard_map/ppermute | solution.py:52
  4.1 15.1 %collective-permute-start.2 = (bf16[512,256]{1,0:T(8,128)(2,1)}, bf16[512,256]{1,0:T(8,128)(2,1)S(1)}, u32[]{:S(2)}, u32[]{:S(2)}) collective-permute-start(bf16[512,256]{1,0:T(8,128)(2,1)} %bitcast.53), channel_id=1, source_target_pairs={{0,3},{1,0},{2,1},{3,2},{4,7},{5,4},{6,5},{7,6},{8,11},{9,8},{10,9... | collective-permute-start | bytes 786440 | tf_op jit(solution)/shard_map/ppermute | solution.py:52
  6.9 12.4 %collective-permute-start.1 = (bf16[512,256]{1,0:T(8,128)(2,1)}, bf16[512,256]{1,0:T(8,128)(2,1)S(1)}, u32[]{:S(2)}, u32[]{:S(2)}) collective-permute-start(bf16[512,256]{1,0:T(8,128)(2,1)} %bitcast.54), channel_id=1, source_target_pairs={{0,2},{1,3},{2,0},{3,1},{4,6},{5,7},{6,4},{7,5},{8,10},{9,11},{10,... | collective-permute-start | bytes 786440 | tf_op jit(solution)/shard_map/ppermute | solution.py:52
  7.7 13.7 %collective-permute-start = (bf16[512,256]{1,0:T(8,128)(2,1)}, bf16[512,256]{1,0:T(8,128)(2,1)S(1)}, u32[]{:S(2)}, u32[]{:S(2)}) collective-permute-start(bf16[512,256]{1,0:T(8,128)(2,1)} %bitcast.55), channel_id=1, source_target_pairs={{0,1},{1,2},{2,3},{3,0},{4,5},{5,6},{6,7},{7,4},{8,9},{9,10},{10,1... | collective-permute-start | bytes 786440 | tf_op jit(solution)/shard_map/ppermute | solution.py:52
  8.7 15.8 %slice-start = ((s8[5242880]{0:T(1024)(128)(4,1)}), s8[4194304]{0:T(1024)(128)(4,1)S(1)}, s32[]{:S(2)}) async-start(s8[5242880]{0:T(1024)(128)(4,1)} %bitcast.36), calls=%async_computation | async-start | bytes 8388608
  8.7 15.8 %slice-start.1 = ((s8[5242880]{0:T(1024)(128)(4,1)}), s8[1048576]{0:T(1024)(128)(4,1)S(1)}, s32[]{:S(2)}) async-start(s8[5242880]{0:T(1024)(128)(4,1)} %bitcast.36), calls=%async_computation.1 | async-start | bytes 2097152
  21.4 3.0 %collective-permute-start.5 = (bf16[2,256,1280]{2,1,0:T(8,128)(2,1)S(1)}, bf16[2,256,1280]{2,1,0:T(8,128)(2,1)S(1)}, u32[]{:S(2)}, u32[]{:S(2)}) collective-permute-start(bf16[2,256,1280]{2,1,0:T(8,128)(2,1)S(1)} %get-tuple-element.47), channel_id=1, source_target_pairs={{0,8},{8,0},{1,9},{9,1},{2,10},{10,2},{3,11},{11,3},{4,12},{12,4},... | collective-permute-start | bytes 3932168 | tf_op jit(solution)/shard_map/ppermute | solution.py:52
  24.5 3.5 %copy-start = (bf16[1,512,256]{2,1,0:T(8,128)(2,1)S(1)}, bf16[1,512,256]{2,1,0:T(8,128)(2,1)}, u32[]{:S(2)}) copy-start(bf16[1,512,256]{2,1,0:T(8,128)(2,1)} %param.8) | copy-start | bytes 786436
  25.9 2.2 %collective-permute-start.6 = (bf16[1280,256]{1,0:T(8,128)(2,1)S(1)}, bf16[1280,256]{1,0:T(8,128)(2,1)S(1)}, u32[]{:S(2)}, u32[]{:S(2)}) collective-permute-start(bf16[1280,256]{1,0:T(8,128)(2,1)S(1)} %get-tuple-element.49.refs_0_), channel_id=1, source_target_pairs={{0,8},{8,0},{1,9},{9,1},{2,10},{10,2},{3,11},{11,3},{4,12},{12,4},... | collective-permute-start | bytes 1966088 | tf_op jit(solution)/shard_map/ppermute | solution.py:52
  29.5 10.7 %collective-permute-start.7 = (bf16[2,320,512]{2,1,0:T(8,128)(2,1)S(1)}, bf16[2,320,512]{2,1,0:T(8,128)(2,1)S(1)}, u32[]{:S(2)}, u32[]{:S(2)}) collective-permute-start(bf16[2,320,512]{2,1,0:T(8,128)(2,1)S(1)} %get-tuple-element.51), channel_id=1, source_target_pairs={{0,32},{8,104},{16,48},{24,120},{32,64},{40,8},{48,80},{56,24},{64... | collective-permute-start | bytes 1966088 | tf_op jit(solution)/shard_map/ppermute | solution.py:52
  29.8 39.6 %collective-permute-start.13 = (bf16[640,1280]{1,0:T(8,128)(2,1)S(1)}, bf16[640,1280]{1,0:T(8,128)(2,1)S(1)}, u32[]{:S(2)}, u32[]{:S(2)}) collective-permute-start(bf16[640,1280]{1,0:T(8,128)(2,1)S(1)} %get-tuple-element.60), channel_id=1, source_target_pairs={{0,16},{16,0},{32,48},{48,32},{64,80},{80,64},{96,112},{112,96},{1... | collective-permute-start | bytes 4915208 | tf_op jit(solution)/shard_map/ppermute | solution.py:52
  31.3 15.9 %collective-permute-start.9 = (bf16[2,320,512]{2,1,0:T(8,128)(2,1)S(1)}, bf16[2,320,512]{2,1,0:T(8,128)(2,1)S(1)}, u32[]{:S(2)}, u32[]{:S(2)}) collective-permute-start(bf16[2,320,512]{2,1,0:T(8,128)(2,1)S(1)} %get-tuple-element.55), channel_id=1, source_target_pairs={{0,32},{8,104},{16,48},{24,120},{32,64},{40,8},{48,80},{56,24},{64... | collective-permute-start | bytes 1966088 | tf_op jit(solution)/shard_map/ppermute | solution.py:52
  33.0 14.0 %collective-permute-start.10 = (bf16[2,512,256]{2,1,0:T(8,128)(2,1)S(1)}, bf16[2,512,256]{2,1,0:T(8,128)(2,1)S(1)}, u32[]{:S(2)}, u32[]{:S(2)}) collective-permute-start(bf16[2,512,256]{2,1,0:T(8,128)(2,1)S(1)} %get-tuple-element.57.refs_2_.refs_9_), channel_id=1, source_target_pairs={{0,1},{1,2},{2,3},{3,0},{4,5},{5,6},{6,7},{7,4},{8,9},{9,10},{10,1... | collective-permute-start | bytes 1572872 | tf_op jit(solution)/shard_map/ppermute | solution.py:52
  41.8 16.5 %collective-permute-start.8 = (bf16[2,320,512]{2,1,0:T(8,128)(2,1)S(1)}, bf16[2,320,512]{2,1,0:T(8,128)(2,1)S(1)}, u32[]{:S(2)}, u32[]{:S(2)}) collective-permute-start(bf16[2,320,512]{2,1,0:T(8,128)(2,1)S(1)} %get-tuple-element.54), channel_id=1, source_target_pairs={{0,32},{8,104},{16,48},{24,120},{32,64},{40,8},{48,80},{56,24},{64... | collective-permute-start | bytes 1966088 | tf_op jit(solution)/shard_map/ppermute | solution.py:52
  43.4 14.9 %collective-permute-start.11 = (bf16[2,512,256]{2,1,0:T(8,128)(2,1)S(1)}, bf16[2,512,256]{2,1,0:T(8,128)(2,1)S(1)}, u32[]{:S(2)}, u32[]{:S(2)}) collective-permute-start(bf16[2,512,256]{2,1,0:T(8,128)(2,1)S(1)} %get-tuple-element.57.refs_2_.refs_9_), channel_id=1, source_target_pairs={{0,3},{1,0},{2,1},{3,2},{4,7},{5,4},{6,5},{7,6},{8,11},{9,8},{10,9... | collective-permute-start | bytes 1572872 | tf_op jit(solution)/shard_map/ppermute | solution.py:52
  48.8 15.8 %collective-permute-start.14 = (bf16[2,320,512]{2,1,0:T(8,128)(2,1)S(1)}, bf16[2,320,512]{2,1,0:T(8,128)(2,1)S(1)}, u32[]{:S(2)}, u32[]{:S(2)}) collective-permute-start(bf16[2,320,512]{2,1,0:T(8,128)(2,1)S(1)} %get-tuple-element.61), channel_id=1, source_target_pairs={{0,32},{8,104},{16,48},{24,120},{32,64},{40,8},{48,80},{56,24},{64... | collective-permute-start | bytes 1966088 | tf_op jit(solution)/shard_map/ppermute | solution.py:52
  51.4 13.2 %collective-permute-start.15 = (bf16[2,512,256]{2,1,0:T(8,128)(2,1)S(1)}, bf16[2,512,256]{2,1,0:T(8,128)(2,1)S(1)}, u32[]{:S(2)}, u32[]{:S(2)}) collective-permute-start(bf16[2,512,256]{2,1,0:T(8,128)(2,1)S(1)} %get-tuple-element.57.refs_2_.refs_9_), channel_id=1, source_target_pairs={{0,2},{1,3},{2,0},{3,1},{4,6},{5,7},{6,4},{7,5},{8,10},{9,11},{10,... | collective-permute-start | bytes 1572872 | tf_op jit(solution)/shard_map/ppermute | solution.py:52
  59.9 11.9 %collective-permute-start.12 = (bf16[2,320,512]{2,1,0:T(8,128)(2,1)S(1)}, bf16[2,320,512]{2,1,0:T(8,128)(2,1)S(1)}, u32[]{:S(2)}, u32[]{:S(2)}) collective-permute-start(bf16[2,320,512]{2,1,0:T(8,128)(2,1)S(1)} %get-tuple-element.59), channel_id=1, source_target_pairs={{0,32},{8,104},{16,48},{24,120},{32,64},{40,8},{48,80},{56,24},{64... | collective-permute-start | bytes 1966088 | tf_op jit(solution)/shard_map/ppermute | solution.py:52
  69.4 3.9 %collective-permute-start.17 = (bf16[640,256]{1,0:T(8,128)(2,1)S(1)}, bf16[640,256]{1,0:T(8,128)(2,1)S(1)}, u32[]{:S(2)}, u32[]{:S(2)}) collective-permute-start(bf16[640,256]{1,0:T(8,128)(2,1)S(1)} %get-tuple-element.66), channel_id=1, source_target_pairs={{0,8},{8,0},{1,9},{9,1},{2,10},{10,2},{3,11},{11,3},{4,12},{12,4},... | collective-permute-start | bytes 983048 | tf_op jit(solution)/shard_map/ppermute | solution.py:52
  69.5 10.7 %collective-permute-start.19 = (bf16[2,320,512]{2,1,0:T(8,128)(2,1)S(1)}, bf16[2,320,512]{2,1,0:T(8,128)(2,1)S(1)}, u32[]{:S(2)}, u32[]{:S(2)}) collective-permute-start(bf16[2,320,512]{2,1,0:T(8,128)(2,1)S(1)} %get-tuple-element.69), channel_id=1, source_target_pairs={{0,32},{8,104},{16,48},{24,120},{32,64},{40,8},{48,80},{56,24},{64... | collective-permute-start | bytes 1966088 | tf_op jit(solution)/shard_map/ppermute | solution.py:52
  74.9 12.4 %collective-permute-start.18 = (bf16[2,160,1024]{2,1,0:T(8,128)(2,1)S(1)}, bf16[2,160,1024]{2,1,0:T(8,128)(2,1)S(1)}, u32[]{:S(2)}, u32[]{:S(2)}) collective-permute-start(bf16[2,160,1024]{2,1,0:T(8,128)(2,1)S(1)} %get-tuple-element.68), channel_id=1, source_target_pairs={{0,32},{8,104},{16,48},{24,120},{32,64},{40,8},{48,80},{56,24},{64... | collective-permute-start | bytes 1966088 | tf_op jit(solution)/shard_map/ppermute | solution.py:52
  74.9 17.3 %collective-permute-start.16 = (bf16[2,320,512]{2,1,0:T(8,128)(2,1)S(1)}, bf16[2,320,512]{2,1,0:T(8,128)(2,1)S(1)}, u32[]{:S(2)}, u32[]{:S(2)}) collective-permute-start(bf16[2,320,512]{2,1,0:T(8,128)(2,1)S(1)} %get-tuple-element.65.a), channel_id=1, source_target_pairs={{0,16},{16,0},{32,48},{48,32},{64,80},{80,64},{96,112},{112,96},{1... | collective-permute-start | bytes 1966088 | tf_op jit(solution)/shard_map/ppermute | solution.py:52
  88.7 11.6 %collective-permute-start.24 = (bf16[2,160,1024]{2,1,0:T(8,128)(2,1)S(1)}, bf16[2,160,1024]{2,1,0:T(8,128)(2,1)S(1)}, u32[]{:S(2)}, u32[]{:S(2)}) collective-permute-start(bf16[2,160,1024]{2,1,0:T(8,128)(2,1)S(1)} %get-tuple-element.75), channel_id=1, source_target_pairs={{0,32},{8,104},{16,48},{24,120},{32,64},{40,8},{48,80},{56,24},{64... | collective-permute-start | bytes 1966088 | tf_op jit(solution)/shard_map/ppermute | solution.py:52
  92.2 15.5 %collective-permute-start.23 = (bf16[2,320,512]{2,1,0:T(8,128)(2,1)S(1)}, bf16[2,320,512]{2,1,0:T(8,128)(2,1)S(1)}, u32[]{:S(2)}, u32[]{:S(2)}) collective-permute-start(bf16[2,320,512]{2,1,0:T(8,128)(2,1)S(1)} %get-tuple-element.74.a), channel_id=1, source_target_pairs={{0,16},{16,0},{32,48},{48,32},{64,80},{80,64},{96,112},{112,96},{1... | collective-permute-start | bytes 1966088 | tf_op jit(solution)/shard_map/ppermute | solution.py:52
  101.8 11.9 %collective-permute-start.28 = (bf16[2,160,1024]{2,1,0:T(8,128)(2,1)S(1)}, bf16[2,160,1024]{2,1,0:T(8,128)(2,1)S(1)}, u32[]{:S(2)}, u32[]{:S(2)}) collective-permute-start(bf16[2,160,1024]{2,1,0:T(8,128)(2,1)S(1)} %get-tuple-element.79), channel_id=1, source_target_pairs={{0,32},{8,104},{16,48},{24,120},{32,64},{40,8},{48,80},{56,24},{64... | collective-permute-start | bytes 1966088 | tf_op jit(solution)/shard_map/ppermute | solution.py:52
  105.6 13.5 %collective-permute-start.20 = (bf16[320,512]{1,0:T(8,128)(2,1)S(1)}, bf16[320,512]{1,0:T(8,128)(2,1)S(1)}, u32[]{:S(2)}, u32[]{:S(2)}) collective-permute-start(bf16[320,512]{1,0:T(8,128)(2,1)S(1)} %get-tuple-element.73.refs_0_), channel_id=1, source_target_pairs={{0,32},{8,104},{16,48},{24,120},{32,64},{40,8},{48,80},{56,24},{64... | collective-permute-start | bytes 983048 | tf_op jit(solution)/shard_map/ppermute | solution.py:52
  115.2 8.4 %collective-permute-start.29 = (bf16[160,1024]{1,0:T(8,128)(2,1)S(1)}, bf16[160,1024]{1,0:T(8,128)(2,1)S(1)}, u32[]{:S(2)}, u32[]{:S(2)}) collective-permute-start(bf16[160,1024]{1,0:T(8,128)(2,1)S(1)} %get-tuple-element.81.refs_8_), channel_id=1, source_target_pairs={{0,32},{8,104},{16,48},{24,120},{32,64},{40,8},{48,80},{56,24},{64... | collective-permute-start | bytes 983048 | tf_op jit(solution)/shard_map/ppermute | solution.py:52
  119.0 8.3 %collective-permute-start.25 = (bf16[320,512]{1,0:T(8,128)(2,1)S(1)}, bf16[320,512]{1,0:T(8,128)(2,1)S(1)}, u32[]{:S(2)}, u32[]{:S(2)}) collective-permute-start(bf16[320,512]{1,0:T(8,128)(2,1)S(1)} %get-tuple-element.78.refs_4_), channel_id=1, source_target_pairs={{0,32},{8,104},{16,48},{24,120},{32,64},{40,8},{48,80},{56,24},{64... | collective-permute-start | bytes 983048 | tf_op jit(solution)/shard_map/ppermute | solution.py:52
  119.1 11.7 %collective-permute-start.21 = (bf16[320,512]{1,0:T(8,128)(2,1)S(1)}, bf16[320,512]{1,0:T(8,128)(2,1)S(1)}, u32[]{:S(2)}, u32[]{:S(2)}) collective-permute-start(bf16[320,512]{1,0:T(8,128)(2,1)S(1)} %collective-permute-done.20.refs_1_), channel_id=1, source_target_pairs={{0,32},{8,104},{16,48},{24,120},{32,64},{40,8},{48,80},{56,24},{64... | collective-permute-start | bytes 983048 | tf_op jit(solution)/shard_map/ppermute | solution.py:52
  123.6 10.7 %collective-permute-start.30 = (bf16[160,1024]{1,0:T(8,128)(2,1)S(1)}, bf16[160,1024]{1,0:T(8,128)(2,1)S(1)}, u32[]{:S(2)}, u32[]{:S(2)}) collective-permute-start(bf16[160,1024]{1,0:T(8,128)(2,1)S(1)} %collective-permute-done.29.refs_9_), channel_id=1, source_target_pairs={{0,32},{8,104},{16,48},{24,120},{32,64},{40,8},{48,80},{56,24},{64... | collective-permute-start | bytes 983048 | tf_op jit(solution)/shard_map/ppermute | solution.py:52
  127.3 10.5 %collective-permute-start.26 = (bf16[320,512]{1,0:T(8,128)(2,1)S(1)}, bf16[320,512]{1,0:T(8,128)(2,1)S(1)}, u32[]{:S(2)}, u32[]{:S(2)}) collective-permute-start(bf16[320,512]{1,0:T(8,128)(2,1)S(1)} %collective-permute-done.25.refs_5_), channel_id=1, source_target_pairs={{0,32},{8,104},{16,48},{24,120},{32,64},{40,8},{48,80},{56,24},{64... | collective-permute-start | bytes 983048 | tf_op jit(solution)/shard_map/ppermute | solution.py:52
  130.8 10.6 %collective-permute-start.22 = (bf16[320,512]{1,0:T(8,128)(2,1)S(1)}, bf16[320,512]{1,0:T(8,128)(2,1)S(1)}, u32[]{:S(2)}, u32[]{:S(2)}) collective-permute-start(bf16[320,512]{1,0:T(8,128)(2,1)S(1)} %collective-permute-done.21.refs_2_), channel_id=1, source_target_pairs={{0,32},{8,104},{16,48},{24,120},{32,64},{40,8},{48,80},{56,24},{64... | collective-permute-start | bytes 983048 | tf_op jit(solution)/shard_map/ppermute | solution.py:52
  134.3 10.6 %collective-permute-start.31 = (bf16[160,1024]{1,0:T(8,128)(2,1)S(1)}, bf16[160,1024]{1,0:T(8,128)(2,1)S(1)}, u32[]{:S(2)}, u32[]{:S(2)}) collective-permute-start(bf16[160,1024]{1,0:T(8,128)(2,1)S(1)} %collective-permute-done.30.refs_10_), channel_id=1, source_target_pairs={{0,32},{8,104},{16,48},{24,120},{32,64},{40,8},{48,80},{56,24},{64... | collective-permute-start | bytes 983048 | tf_op jit(solution)/shard_map/ppermute | solution.py:52
  137.8 12.2 %collective-permute-start.32 = (bf16[160,1024]{1,0:T(8,128)(2,1)S(1)}, bf16[160,1024]{1,0:T(8,128)(2,1)S(1)}, u32[]{:S(2)}, u32[]{:S(2)}) collective-permute-start(bf16[160,1024]{1,0:T(8,128)(2,1)S(1)} %get-tuple-element.81.refs_8_), channel_id=1, source_target_pairs={{0,16},{16,0},{32,48},{48,32},{64,80},{80,64},{96,112},{112,96},{1... | collective-permute-start | bytes 983048 | tf_op jit(solution)/shard_map/ppermute | solution.py:52
  137.8 10.3 %collective-permute-start.27 = (bf16[320,512]{1,0:T(8,128)(2,1)S(1)}, bf16[320,512]{1,0:T(8,128)(2,1)S(1)}, u32[]{:S(2)}, u32[]{:S(2)}) collective-permute-start(bf16[320,512]{1,0:T(8,128)(2,1)S(1)} %collective-permute-done.26.refs_6_), channel_id=1, source_target_pairs={{0,32},{8,104},{16,48},{24,120},{32,64},{40,8},{48,80},{56,24},{64... | collective-permute-start | bytes 983048 | tf_op jit(solution)/shard_map/ppermute | solution.py:52
  141.3 15.6 %collective-permute-start.33 = (bf16[160,1024]{1,0:T(8,128)(2,1)S(1)}, bf16[160,1024]{1,0:T(8,128)(2,1)S(1)}, u32[]{:S(2)}, u32[]{:S(2)}) collective-permute-start(bf16[160,1024]{1,0:T(8,128)(2,1)S(1)} %collective-permute-done.29.refs_9_), channel_id=1, source_target_pairs={{0,16},{16,0},{32,48},{48,32},{64,80},{80,64},{96,112},{112,96},{1... | collective-permute-start | bytes 983048 | tf_op jit(solution)/shard_map/ppermute | solution.py:52
  141.4 19.0 %collective-permute-start.34 = (bf16[160,1024]{1,0:T(8,128)(2,1)S(1)}, bf16[160,1024]{1,0:T(8,128)(2,1)S(1)}, u32[]{:S(2)}, u32[]{:S(2)}) collective-permute-start(bf16[160,1024]{1,0:T(8,128)(2,1)S(1)} %collective-permute-done.30.refs_10_), channel_id=1, source_target_pairs={{0,16},{16,0},{32,48},{48,32},{64,80},{80,64},{96,112},{112,96},{1... | collective-permute-start | bytes 983048 | tf_op jit(solution)/shard_map/ppermute | solution.py:52
  144.8 19.0 %collective-permute-start.35 = (bf16[160,1024]{1,0:T(8,128)(2,1)S(1)}, bf16[160,1024]{1,0:T(8,128)(2,1)S(1)}, u32[]{:S(2)}, u32[]{:S(2)}) collective-permute-start(bf16[160,1024]{1,0:T(8,128)(2,1)S(1)} %collective-permute-done.31.refs_11_), channel_id=1, source_target_pairs={{0,16},{16,0},{32,48},{48,32},{64,80},{80,64},{96,112},{112,96},{1... | collective-permute-start | bytes 983048 | tf_op jit(solution)/shard_map/ppermute | solution.py:52

commit v3 on v2

--- a/solution.py
+++ b/solution.py
@@ -332,7 +332,7 @@
     far_mine = [move(mine, ZLO_SWAP, "col"), move(mine, Z_MIRROR, ("task", "col"))]
     w = down_weight[0]
     own, send, token = project(offs, inputs[0], gate_weight[0], up_weight[0])
-    send, token = hold(send, [token, *near[1:], *far_mine])
+    send, token = hold(send, [token, *far_mine, near[1], near[3], near[2]])
     ha, away, far_pair, token = make_hidden(offs, own, move(send, CORE_SWAP, "row"), w, far_mine, [token])
     hb = move(ha, CORE_SWAP, "row")
     far = [far_pair] + [move(far_pair, x_shift(n), "col") for n in (1, 2, 3)]
@@ -353,16 +353,13 @@
             part, recv, final, before,
         )
 
-    def around(piece):
-        pieces = [piece]
-        for _ in range(3):
-            pieces.append(move(pieces[-1], RING, ("task", "row")))
-        return pieces
+    def onward(piece):
+        return move(piece, RING, ("task", "row"))
 
     got = [(), ()]
     for k in (1, 2, 3):
         for p in range(2):
-            extra = {(2, 1): far[1:2], (3, 0): far[3:4], (3, 1): far[2:3]}.get((k, p), [])
+            extra = {(2, 1): [far[1], far[3]], (3, 1): far[2:3]}.get((k, p), [])
             piece, token = ring_terms(p, k, got[p], token, *extra)
             got[p] = (move(piece, RING, ("task", "row")),)
     zb, token = cut(za, HALF, token)
@@ -370,22 +367,32 @@
     a_sum, a_got, a_all = [None, None], [None, None], [None, None]
     a_sum[0], token = ring_terms(0, 0, got[0], token)
     a_got[0] = move(a_sum[0], Z_SWAP)
-    b_got = ()
+    b_got, early = (), []
     for k in (1, 2, 3):
         piece, token = far_terms(k, b_got, False, token)
-        b_got = (move(piece, RING, ("task", "row")),)
+        b_got = (onward(piece),)
         if k == 1:
             a_sum[1], token = ring_terms(1, 0, got[1], token)
             a_got[1] = move(a_sum[1], Z_SWAP)
         if k == 2:
             out, token = merge(a_sum[0], a_got[0], token)
-            a_all[0] = around(out)
+            a_all[0] = [out, onward(out)]
+            early = [a_all[0][1]]
         if k == 3:
+            a_all[0].append(onward(a_all[0][1]))
             out, token = merge(a_sum[1], a_got[1], token)
-            a_all[1] = around(out)
+            a_all[1] = [out, onward(out)]
     b_out, token = far_terms(0, b_got, True, token)
-    b_near = around(b_out)
+    a_all[0].append(onward(a_all[0][2]))
+    b_near = [b_out, onward(b_out)]
     b_far = [move(piece, Z_SWAP) for piece in b_near]
+    b_near.append(onward(b_near[1]))
+    a_all[1].append(onward(a_all[1][1]))
+    b_near[2], _ = hold(b_near[2], [b_far[0]])
+    b_near.append(onward(b_near[2]))
+    a_all[1][2], _ = hold(a_all[1][2], [b_far[1]])
+    a_all[1].append(onward(a_all[1][2]))
+    b_far += [move(piece, Z_SWAP) for piece in b_near[2:]]
 
     plan = []
     for k in range(4):

time: 171 us -> 159 us (0.930); the launches traced: 167 us -> 159 us
  waiting for transfers between devices: 78.7 us -> 65.9 us
  starting transfers between devices: 54.2 us -> 57.4 us
    ppermute x36, waiting for transfers between devices: 78.7 us -> 65.9 us  [move(): return lax.ppermute(x, axis, perm)]
    ppermute x36, starting transfers between devices: 54.2 us -> 57.4 us  [move(): return lax.ppermute(x, axis, perm)]
  transfers between devices with their start and end apart: 36 -> 36, of which waited for: 20 -> 19; matrix products, arithmetic and copies ran while one was open for 0% -> 0% of each run, Pallas kernels for 17% -> 17%
where the time goes in v3:
time: 159 us
  waiting for transfers between devices  65.9 us (41%)
  starting transfers between devices  57.4 us (36%)
  Pallas kernels  35.1 us (22%)
    ppermute x36, waiting for transfers between devices, move(): return lax.ppermute(x, axis, perm)  65.9 us
    ppermute x36, starting transfers between devices, move(): return lax.ppermute(x, axis, perm)  57.4 us
    pallas_call x12, Pallas kernels, terms(): pl.pallas_call(functools.partial(term_kernel, rows, nb, [s[5] for s in so...  18.4 us
    pallas_call x1, Pallas kernels, project(): pl.pallas_call(functools.partial(project_kernel, step), in_specs=[SMEM] +...  10.5 us
    pallas_call x1, Pallas kernels, place(): pl.pallas_call(functools.partial(place_kernel, plan, len(parts)), in_spec...  3.27 us
  transfers between devices with their start and end apart: 36, of which 19 were waited for; matrix products, arithmetic and copies ran while one was open for 0% of the time, Pallas kernels for 17%

profile of v3, /device:TPU:56, one launch (start us, length us, event | category | flops | bytes accessed | tf_op | source)
XLA Modules:
  0.0 158.9 jit_solution(16711092066780386127)
XLA Ops:
  0.0 3.0 %collective-permute-start.4 = (bf16[512,256]{1,0:T(8,128)(2,1)}, bf16[512,256]{1,0:T(8,128)(2,1)S(1)}, u32[]{:S(2)}, u32[]{:S(2)}) collective-permute-start(bf16[512,256]{1,0:T(8,128)(2,1)} %bitcast.51), channel_id=1, source_target_pairs={{0,2},{1,3},{2,0},{3,1},{4,6},{5,7},{6,4},{7,5},{8,10},{9,11},{10,... | collective-permute-start | bytes 786440 | tf_op jit(solution)/shard_map/ppermute | solution.py:52
  5.1 1.9 %collective-permute-start.1 = (bf16[512,256]{1,0:T(8,128)(2,1)}, bf16[512,256]{1,0:T(8,128)(2,1)S(1)}, u32[]{:S(2)}, u32[]{:S(2)}) collective-permute-start(bf16[512,256]{1,0:T(8,128)(2,1)} %bitcast.54), channel_id=1, source_target_pairs={{0,20},{1,21},{2,22},{3,23},{4,16},{5,17},{6,18},{7,19},{16,4},{17... | collective-permute-start | bytes 786440 | tf_op jit(solution)/shard_map/ppermute | solution.py:52
  7.0 2.2 %collective-permute-start = (bf16[512,256]{1,0:T(8,128)(2,1)}, bf16[512,256]{1,0:T(8,128)(2,1)S(1)}, u32[]{:S(2)}, u32[]{:S(2)}) collective-permute-start(bf16[512,256]{1,0:T(8,128)(2,1)} %bitcast.55), channel_id=1, source_target_pairs={{0,4},{1,5},{2,6},{3,7},{4,0},{5,1},{6,2},{7,3},{8,12},{9,13},{10,... | collective-permute-start | bytes 786440 | tf_op jit(solution)/shard_map/ppermute | solution.py:52
  9.3 10.5 %shard_map.55 = (f32[2,256,1280]{2,1,0:T(8,128)S(1)}, bf16[2,256,1280]{2,1,0:T(8,128)(2,1)S(1)}, f32[8,128]{1,0:T(8,128)S(1)}) custom-call(s32[39]{0:T(128)S(1)} %stack.135.offs, bf16[512,2048]{1,0:T(8,128)(2,1)} %bitcast.62, bf16[2048,1280]{1,0:T(8,128)(2,1)} %bitcast.60, bf16[2048,1280]{1,0:T(8,128)(2,1)} %bitcast.61), custom_call_target="tpu_custom_call" | custom-call | tf_op jit(solution)/shard_map/pallas_call | solution.py:95
  20.0 3.0 %collective-permute-done.5.recv_ref = bf16[2,256,1280]{2,1,0:T(8,128)(2,1)S(1)} collective-permute-done((bf16[2,256,1280]{2,1,0:T(8,128)(2,1)S(1)}, bf16[2,256,1280]{2,1,0:T(8,128)(2,1)S(1)}, u32[]{:S(2)}, u32[]{:S(2)}) %collective-permute-start.5) | collective-permute-done | bytes 1310752 | tf_op jit(solution)/shard_map/ppermute | solution.py:52
  24.6 2.0 %collective-permute-done.6.refs_1_ = bf16[1280,256]{1,0:T(8,128)(2,1)S(1)} collective-permute-done((bf16[1280,256]{1,0:T(8,128)(2,1)S(1)}, bf16[1280,256]{1,0:T(8,128)(2,1)S(1)}, u32[]{:S(2)}, u32[]{:S(2)}) %collective-permute-start.6) | collective-permute-done | bytes 655392 | tf_op jit(solution)/shard_map/ppermute | solution.py:52
  26.6 1.5 shard_map.58
  28.4 1.5 shard_map.59
  29.9 1.6 %collective-permute-start.9 = (bf16[2,320,512]{2,1,0:T(8,128)(2,1)S(1)}, bf16[2,320,512]{2,1,0:T(8,128)(2,1)S(1)}, u32[]{:S(2)}, u32[]{:S(2)}) collective-permute-start(bf16[2,320,512]{2,1,0:T(8,128)(2,1)S(1)} %get-tuple-element.57), channel_id=1, source_target_pairs={{0,32},{8,104},{16,48},{24,120},{32,64},{40,8},{48,80},{56,24},{64... | collective-permute-start | bytes 1966088 | tf_op jit(solution)/shard_map/ppermute | solution.py:52
  31.5 2.3 %collective-permute-start.11 = (bf16[2,512,256]{2,1,0:T(8,128)(2,1)S(1)}, bf16[2,512,256]{2,1,0:T(8,128)(2,1)S(1)}, u32[]{:S(2)}, u32[]{:S(2)}) collective-permute-start(bf16[2,512,256]{2,1,0:T(8,128)(2,1)S(1)} %get-tuple-element.59.refs_2_.refs_9_), channel_id=1, source_target_pairs={{0,3},{1,0},{2,1},{3,2},{4,7},{5,4},{6,5},{7,6},{8,11},{9,8},{10,9... | collective-permute-start | bytes 1572872 | tf_op jit(solution)/shard_map/ppermute | solution.py:52
  33.9 4.8 %collective-permute-done.7.refs_5_ = bf16[2,320,512]{2,1,0:T(8,128)(2,1)S(1)} collective-permute-done((bf16[2,320,512]{2,1,0:T(8,128)(2,1)S(1)}, bf16[2,320,512]{2,1,0:T(8,128)(2,1)S(1)}, u32[]{:S(2)}, u32[]{:S(2)}) %collective-permute-start.7) | collective-permute-done | bytes 655392 | tf_op jit(solution)/shard_map/ppermute | solution.py:52
  38.7 1.6 shard_map.60
  40.3 1.5 collective-permute-start.8
  41.8 2.5 %collective-permute-done.11.refs_8_.refs_5_.refs_12_ = bf16[2,512,256]{2,1,0:T(8,128)(2,1)S(1)} collective-permute-done((bf16[2,512,256]{2,1,0:T(8,128)(2,1)S(1)}, bf16[2,512,256]{2,1,0:T(8,128)(2,1)S(1)}, u32[]{:S(2)}, u32[]{:S(2)}) %collective-permute-start.11) | collective-permute-done | bytes 524320 | tf_op jit(solution)/shard_map/ppermute | solution.py:52
  44.3 3.3 %collective-permute-done.10.refs_7_.refs_3_.refs_10_ = bf16[2,512,256]{2,1,0:T(8,128)(2,1)S(1)} collective-permute-done((bf16[2,512,256]{2,1,0:T(8,128)(2,1)S(1)}, bf16[2,512,256]{2,1,0:T(8,128)(2,1)S(1)}, u32[]{:S(2)}, u32[]{:S(2)}) %collective-permute-start.10) | collective-permute-done | bytes 524320 | tf_op jit(solution)/shard_map/ppermute | solution.py:52
  47.6 1.6 shard_map.61
  49.2 2.9 %collective-permute-start.14 = (bf16[2,320,512]{2,1,0:T(8,128)(2,1)S(1)}, bf16[2,320,512]{2,1,0:T(8,128)(2,1)S(1)}, u32[]{:S(2)}, u32[]{:S(2)}) collective-permute-start(bf16[2,320,512]{2,1,0:T(8,128)(2,1)S(1)} %get-tuple-element.63), channel_id=1, source_target_pairs={{0,32},{8,104},{16,48},{24,120},{32,64},{40,8},{48,80},{56,24},{64... | collective-permute-start | bytes 1966088 | tf_op jit(solution)/shard_map/ppermute | solution.py:52
  52.8 1.6 shard_map.62
  54.3 1.5 collective-permute-start.12
  55.8 7.5 %collective-permute-done.15.refs_7_.refs_4_.refs_11_ = bf16[2,512,256]{2,1,0:T(8,128)(2,1)S(1)} collective-permute-done((bf16[2,512,256]{2,1,0:T(8,128)(2,1)S(1)}, bf16[2,512,256]{2,1,0:T(8,128)(2,1)S(1)}, u32[]{:S(2)}, u32[]{:S(2)}) %collective-permute-start.15) | collective-permute-done | bytes 524320 | tf_op jit(solution)/shard_map/ppermute | solution.py:52
  63.3 1.6 shard_map.63
  64.9 3.1 %collective-permute-done.13.a_ref.refs_7_.refs_13_ = bf16[640,1280]{1,0:T(8,128)(2,1)S(1)} collective-permute-done((bf16[640,1280]{1,0:T(8,128)(2,1)S(1)}, bf16[640,1280]{1,0:T(8,128)(2,1)S(1)}, u32[]{:S(2)}, u32[]{:S(2)}) %collective-permute-start.13) | collective-permute-done | bytes 1638432 | tf_op jit(solution)/shard_map/ppermute | solution.py:52
  68.1 2.3 %collective-permute-start.19 = (bf16[2,320,512]{2,1,0:T(8,128)(2,1)S(1)}, bf16[2,320,512]{2,1,0:T(8,128)(2,1)S(1)}, u32[]{:S(2)}, u32[]{:S(2)}) collective-permute-start(bf16[2,320,512]{2,1,0:T(8,128)(2,1)S(1)} %get-tuple-element.71), channel_id=1, source_target_pairs={{0,32},{8,104},{16,48},{24,120},{32,64},{40,8},{48,80},{56,24},{64... | collective-permute-start | bytes 1966088 | tf_op jit(solution)/shard_map/ppermute | solution.py:52
  70.4 1.6 shard_map.65
  71.9 1.5 shard_map.66
  74.0 3.3 %collective-permute-start.16 = (bf16[2,320,512]{2,1,0:T(8,128)(2,1)S(1)}, bf16[2,320,512]{2,1,0:T(8,128)(2,1)S(1)}, u32[]{:S(2)}, u32[]{:S(2)}) collective-permute-start(bf16[2,320,512]{2,1,0:T(8,128)(2,1)S(1)} %get-tuple-element.67.a), channel_id=1, source_target_pairs={{0,16},{16,0},{32,48},{48,32},{64,80},{80,64},{96,112},{112,96},{1... | collective-permute-start | bytes 1966088 | tf_op jit(solution)/shard_map/ppermute | solution.py:52
  77.2 1.5 collective-permute-done.19.refs_5_
  78.7 1.6 shard_map.67
  80.3 5.5 %collective-permute-done.18.refs_14_ = bf16[2,160,1024]{2,1,0:T(8,128)(2,1)S(1)} collective-permute-done((bf16[2,160,1024]{2,1,0:T(8,128)(2,1)S(1)}, bf16[2,160,1024]{2,1,0:T(8,128)(2,1)S(1)}, u32[]{:S(2)}, u32[]{:S(2)}) %collective-permute-start.18) | collective-permute-done | bytes 655392 | tf_op jit(solution)/shard_map/ppermute | solution.py:52
  85.8 1.5 shard_map.68
  87.3 3.5 %collective-permute-start.24 = (bf16[2,160,1024]{2,1,0:T(8,128)(2,1)S(1)}, bf16[2,160,1024]{2,1,0:T(8,128)(2,1)S(1)}, u32[]{:S(2)}, u32[]{:S(2)}) collective-permute-start(bf16[2,160,1024]{2,1,0:T(8,128)(2,1)S(1)} %get-tuple-element.77), channel_id=1, source_target_pairs={{0,32},{8,104},{16,48},{24,120},{32,64},{40,8},{48,80},{56,24},{64... | collective-permute-start | bytes 1966088 | tf_op jit(solution)/shard_map/ppermute | solution.py:52
  91.8 7.0 %collective-permute-done.24.refs_14_ = bf16[2,160,1024]{2,1,0:T(8,128)(2,1)S(1)} collective-permute-done((bf16[2,160,1024]{2,1,0:T(8,128)(2,1)S(1)}, bf16[2,160,1024]{2,1,0:T(8,128)(2,1)S(1)}, u32[]{:S(2)}, u32[]{:S(2)}) %collective-permute-start.24) | collective-permute-done | bytes 655392 | tf_op jit(solution)/shard_map/ppermute | solution.py:52
  98.9 1.5 shard_map.70
  100.4 3.8 %collective-permute-start.27 = (bf16[2,160,1024]{2,1,0:T(8,128)(2,1)S(1)}, bf16[2,160,1024]{2,1,0:T(8,128)(2,1)S(1)}, u32[]{:S(2)}, u32[]{:S(2)}) collective-permute-start(bf16[2,160,1024]{2,1,0:T(8,128)(2,1)S(1)} %get-tuple-element.81), channel_id=1, source_target_pairs={{0,32},{8,104},{16,48},{24,120},{32,64},{40,8},{48,80},{56,24},{64... | collective-permute-start | bytes 1966088 | tf_op jit(solution)/shard_map/ppermute | solution.py:52
  104.1 2.1 %collective-permute-done.23.b = bf16[2,320,512]{2,1,0:T(8,128)(2,1)S(1)} collective-permute-done((bf16[2,320,512]{2,1,0:T(8,128)(2,1)S(1)}, bf16[2,320,512]{2,1,0:T(8,128)(2,1)S(1)}, u32[]{:S(2)}, u32[]{:S(2)}) %collective-permute-start.23) | collective-permute-done | bytes 655392 | tf_op jit(solution)/shard_map/ppermute | solution.py:52
  106.4 5.8 %collective-permute-done.27.refs_14_ = bf16[2,160,1024]{2,1,0:T(8,128)(2,1)S(1)} collective-permute-done((bf16[2,160,1024]{2,1,0:T(8,128)(2,1)S(1)}, bf16[2,160,1024]{2,1,0:T(8,128)(2,1)S(1)}, u32[]{:S(2)}, u32[]{:S(2)}) %collective-permute-start.27) | collective-permute-done | bytes 655392 | tf_op jit(solution)/shard_map/ppermute | solution.py:52
  112.2 1.5 shard_map.72
  113.8 3.8 %collective-permute-start.28 = (bf16[160,1024]{1,0:T(8,128)(2,1)S(1)}, bf16[160,1024]{1,0:T(8,128)(2,1)S(1)}, u32[]{:S(2)}, u32[]{:S(2)}) collective-permute-start(bf16[160,1024]{1,0:T(8,128)(2,1)S(1)} %get-tuple-element.83.refs_8_), channel_id=1, source_target_pairs={{0,32},{8,104},{16,48},{24,120},{32,64},{40,8},{48,80},{56,24},{64... | collective-permute-start | bytes 983048 | tf_op jit(solution)/shard_map/ppermute | solution.py:52
  118.6 3.6 %collective-permute-done.28.refs_9_ = bf16[160,1024]{1,0:T(8,128)(2,1)S(1)} collective-permute-done((bf16[160,1024]{1,0:T(8,128)(2,1)S(1)}, bf16[160,1024]{1,0:T(8,128)(2,1)S(1)}, u32[]{:S(2)}, u32[]{:S(2)}) %collective-permute-start.28) | collective-permute-done | bytes 327712 | tf_op jit(solution)/shard_map/ppermute | solution.py:52
  122.1 3.7 %collective-permute-start.31 = (bf16[160,1024]{1,0:T(8,128)(2,1)S(1)}, bf16[160,1024]{1,0:T(8,128)(2,1)S(1)}, u32[]{:S(2)}, u32[]{:S(2)}) collective-permute-start(bf16[160,1024]{1,0:T(8,128)(2,1)S(1)} %collective-permute-done.28.refs_9_), channel_id=1, source_target_pairs={{0,32},{8,104},{16,48},{24,120},{32,64},{40,8},{48,80},{56,24},{64... | collective-permute-start | bytes 983048 | tf_op jit(solution)/shard_map/ppermute | solution.py:52
  125.8 3.5 %collective-permute-start.21 = (bf16[320,512]{1,0:T(8,128)(2,1)S(1)}, bf16[320,512]{1,0:T(8,128)(2,1)S(1)}, u32[]{:S(2)}, u32[]{:S(2)}) collective-permute-start(bf16[320,512]{1,0:T(8,128)(2,1)S(1)} %collective-permute-done.20.refs_1_), channel_id=1, source_target_pairs={{0,32},{8,104},{16,48},{24,120},{32,64},{40,8},{48,80},{56,24},{64... | collective-permute-start | bytes 983048 | tf_op jit(solution)/shard_map/ppermute | solution.py:52
  129.3 3.5 %collective-permute-start.26 = (bf16[320,512]{1,0:T(8,128)(2,1)S(1)}, bf16[320,512]{1,0:T(8,128)(2,1)S(1)}, u32[]{:S(2)}, u32[]{:S(2)}) collective-permute-start(bf16[320,512]{1,0:T(8,128)(2,1)S(1)} %collective-permute-done.25.refs_5_), channel_id=1, source_target_pairs={{0,32},{8,104},{16,48},{24,120},{32,64},{40,8},{48,80},{56,24},{64... | collective-permute-start | bytes 983048 | tf_op jit(solution)/shard_map/ppermute | solution.py:52
  134.3 2.6 %collective-permute-start.33 = (bf16[160,1024]{1,0:T(8,128)(2,1)S(1)}, bf16[160,1024]{1,0:T(8,128)(2,1)S(1)}, u32[]{:S(2)}, u32[]{:S(2)}) collective-permute-start(bf16[160,1024]{1,0:T(8,128)(2,1)S(1)} %get-tuple-element.85.refs_10_), channel_id=1, source_target_pairs={{0,32},{8,104},{16,48},{24,120},{32,64},{40,8},{48,80},{56,24},{64... | collective-permute-start | bytes 983048 | tf_op jit(solution)/shard_map/ppermute | solution.py:52
  136.9 2.9 %collective-permute-start.22 = (bf16[320,512]{1,0:T(8,128)(2,1)S(1)}, bf16[320,512]{1,0:T(8,128)(2,1)S(1)}, u32[]{:S(2)}, u32[]{:S(2)}) collective-permute-start(bf16[320,512]{1,0:T(8,128)(2,1)S(1)} %collective-permute-done.21.refs_2_), channel_id=1, source_target_pairs={{0,32},{8,104},{16,48},{24,120},{32,64},{40,8},{48,80},{56,24},{64... | collective-permute-start | bytes 983048 | tf_op jit(solution)/shard_map/ppermute | solution.py:52
  140.7 4.1 %collective-permute-done.29.refs_1_.refs_13_ = bf16[160,1024]{1,0:T(8,128)(2,1)S(1)} collective-permute-done((bf16[160,1024]{1,0:T(8,128)(2,1)S(1)}, bf16[160,1024]{1,0:T(8,128)(2,1)S(1)}, u32[]{:S(2)}, u32[]{:S(2)}) %collective-permute-start.29) | collective-permute-done | bytes 327712 | tf_op jit(solution)/shard_map/ppermute | solution.py:52
  146.7 5.2 %collective-permute-done.34.refs_14_ = bf16[160,1024]{1,0:T(8,128)(2,1)S(1)} collective-permute-done((bf16[160,1024]{1,0:T(8,128)(2,1)S(1)}, bf16[160,1024]{1,0:T(8,128)(2,1)S(1)}, u32[]{:S(2)}, u32[]{:S(2)}) %collective-permute-start.34) | collective-permute-done | bytes 327712 | tf_op jit(solution)/shard_map/ppermute | solution.py:52
  152.5 2.9 %collective-permute-done.35.refs_15_ = bf16[160,1024]{1,0:T(8,128)(2,1)S(1)} collective-permute-done((bf16[160,1024]{1,0:T(8,128)(2,1)S(1)}, bf16[160,1024]{1,0:T(8,128)(2,1)S(1)}, u32[]{:S(2)}, u32[]{:S(2)}) %collective-permute-start.35) | collective-permute-done | bytes 327712 | tf_op jit(solution)/shard_map/ppermute | solution.py:52
  155.5 3.3 %shard_map.75 = bf16[1280,2048]{1,0:T(8,128)(2,1)} custom-call(s32[39]{0:T(128)S(1)} %stack.135.offs, bf16[320,512]{1,0:T(8,128)(2,1)S(1)} %get-tuple-element.75.refs_0_, bf16[320,512]{1,0:T(8,128)(2,1)S(1)} %collective-permute-done.20.refs_1_, bf16[320,512]{1,0:T(8,128)(2,1)S(1)} %collective-permute-done.21.refs_2_, ...), custom_call_target="tpu_custom_call" | custom-call | tf_op jit(solution)/shard_map/pallas_call | solution.py:282
  (53 shorter events, 12.7 us)
Async XLA Ops:
  0.0 19.8 %collective-permute-start.4 = (bf16[512,256]{1,0:T(8,128)(2,1)}, bf16[512,256]{1,0:T(8,128)(2,1)S(1)}, u32[]{:S(2)}, u32[]{:S(2)}) collective-permute-start(bf16[512,256]{1,0:T(8,128)(2,1)} %bitcast.51), channel_id=1, source_target_pairs={{0,2},{1,3},{2,0},{3,1},{4,6},{5,7},{6,4},{7,5},{8,10},{9,11},{10,... | collective-permute-start | bytes 786440 | tf_op jit(solution)/shard_map/ppermute | solution.py:52
  3.0 16.8 %collective-permute-start.3 = (bf16[512,256]{1,0:T(8,128)(2,1)}, bf16[512,256]{1,0:T(8,128)(2,1)S(1)}, u32[]{:S(2)}, u32[]{:S(2)}) collective-permute-start(bf16[512,256]{1,0:T(8,128)(2,1)} %bitcast.52), channel_id=1, source_target_pairs={{0,3},{1,0},{2,1},{3,2},{4,7},{5,4},{6,5},{7,6},{8,11},{9,8},{10,9... | collective-permute-start | bytes 786440 | tf_op jit(solution)/shard_map/ppermute | solution.py:52
  4.2 15.7 %collective-permute-start.2 = (bf16[512,256]{1,0:T(8,128)(2,1)}, bf16[512,256]{1,0:T(8,128)(2,1)S(1)}, u32[]{:S(2)}, u32[]{:S(2)}) collective-permute-start(bf16[512,256]{1,0:T(8,128)(2,1)} %bitcast.53), channel_id=1, source_target_pairs={{0,1},{1,2},{2,3},{3,0},{4,5},{5,6},{6,7},{7,4},{8,9},{9,10},{10,1... | collective-permute-start | bytes 786440 | tf_op jit(solution)/shard_map/ppermute | solution.py:52
  5.1 14.8 %collective-permute-start.1 = (bf16[512,256]{1,0:T(8,128)(2,1)}, bf16[512,256]{1,0:T(8,128)(2,1)S(1)}, u32[]{:S(2)}, u32[]{:S(2)}) collective-permute-start(bf16[512,256]{1,0:T(8,128)(2,1)} %bitcast.54), channel_id=1, source_target_pairs={{0,20},{1,21},{2,22},{3,23},{4,16},{5,17},{6,18},{7,19},{16,4},{17... | collective-permute-start | bytes 786440 | tf_op jit(solution)/shard_map/ppermute | solution.py:52
  7.0 12.9 %collective-permute-start = (bf16[512,256]{1,0:T(8,128)(2,1)}, bf16[512,256]{1,0:T(8,128)(2,1)S(1)}, u32[]{:S(2)}, u32[]{:S(2)}) collective-permute-start(bf16[512,256]{1,0:T(8,128)(2,1)} %bitcast.55), channel_id=1, source_target_pairs={{0,4},{1,5},{2,6},{3,7},{4,0},{5,1},{6,2},{7,3},{8,12},{9,13},{10,... | collective-permute-start | bytes 786440 | tf_op jit(solution)/shard_map/ppermute | solution.py:52
  9.3 13.7 %slice-start = ((s8[5242880]{0:T(1024)(128)(4,1)}), s8[4194304]{0:T(1024)(128)(4,1)S(1)}, s32[]{:S(2)}) async-start(s8[5242880]{0:T(1024)(128)(4,1)} %bitcast.36), calls=%async_computation | async-start | bytes 8388608
  9.3 13.7 %slice-start.1 = ((s8[5242880]{0:T(1024)(128)(4,1)}), s8[1048576]{0:T(1024)(128)(4,1)S(1)}, s32[]{:S(2)}) async-start(s8[5242880]{0:T(1024)(128)(4,1)} %bitcast.36), calls=%async_computation.1 | async-start | bytes 2097152
  19.9 3.1 %collective-permute-start.5 = (bf16[2,256,1280]{2,1,0:T(8,128)(2,1)S(1)}, bf16[2,256,1280]{2,1,0:T(8,128)(2,1)S(1)}, u32[]{:S(2)}, u32[]{:S(2)}) collective-permute-start(bf16[2,256,1280]{2,1,0:T(8,128)(2,1)S(1)} %get-tuple-element.49), channel_id=1, source_target_pairs={{0,8},{8,0},{1,9},{9,1},{2,10},{10,2},{3,11},{11,3},{4,12},{12,4},... | collective-permute-start | bytes 3932168 | tf_op jit(solution)/shard_map/ppermute | solution.py:52
  23.0 3.5 %copy-start = (bf16[1,512,256]{2,1,0:T(8,128)(2,1)S(1)}, bf16[1,512,256]{2,1,0:T(8,128)(2,1)}, u32[]{:S(2)}) copy-start(bf16[1,512,256]{2,1,0:T(8,128)(2,1)} %param.8) | copy-start | bytes 786436
  24.4 2.2 %collective-permute-start.6 = (bf16[1280,256]{1,0:T(8,128)(2,1)S(1)}, bf16[1280,256]{1,0:T(8,128)(2,1)S(1)}, u32[]{:S(2)}, u32[]{:S(2)}) collective-permute-start(bf16[1280,256]{1,0:T(8,128)(2,1)S(1)} %get-tuple-element.51.refs_0_), channel_id=1, source_target_pairs={{0,8},{8,0},{1,9},{9,1},{2,10},{10,2},{3,11},{11,3},{4,12},{12,4},... | collective-permute-start | bytes 1966088 | tf_op jit(solution)/shard_map/ppermute | solution.py:52
  28.1 10.7 %collective-permute-start.7 = (bf16[2,320,512]{2,1,0:T(8,128)(2,1)S(1)}, bf16[2,320,512]{2,1,0:T(8,128)(2,1)S(1)}, u32[]{:S(2)}, u32[]{:S(2)}) collective-permute-start(bf16[2,320,512]{2,1,0:T(8,128)(2,1)S(1)} %get-tuple-element.53), channel_id=1, source_target_pairs={{0,32},{8,104},{16,48},{24,120},{32,64},{40,8},{48,80},{56,24},{64... | collective-permute-start | bytes 1966088 | tf_op jit(solution)/shard_map/ppermute | solution.py:52
  28.4 39.6 %collective-permute-start.13 = (bf16[640,1280]{1,0:T(8,128)(2,1)S(1)}, bf16[640,1280]{1,0:T(8,128)(2,1)S(1)}, u32[]{:S(2)}, u32[]{:S(2)}) collective-permute-start(bf16[640,1280]{1,0:T(8,128)(2,1)S(1)} %get-tuple-element.62), channel_id=1, source_target_pairs={{0,16},{16,0},{32,48},{48,32},{64,80},{80,64},{96,112},{112,96},{1... | collective-permute-start | bytes 4915208 | tf_op jit(solution)/shard_map/ppermute | solution.py:52
  29.9 17.7 %collective-permute-start.9 = (bf16[2,320,512]{2,1,0:T(8,128)(2,1)S(1)}, bf16[2,320,512]{2,1,0:T(8,128)(2,1)S(1)}, u32[]{:S(2)}, u32[]{:S(2)}) collective-permute-start(bf16[2,320,512]{2,1,0:T(8,128)(2,1)S(1)} %get-tuple-element.57), channel_id=1, source_target_pairs={{0,32},{8,104},{16,48},{24,120},{32,64},{40,8},{48,80},{56,24},{64... | collective-permute-start | bytes 1966088 | tf_op jit(solution)/shard_map/ppermute | solution.py:52
  31.5 12.8 %collective-permute-start.11 = (bf16[2,512,256]{2,1,0:T(8,128)(2,1)S(1)}, bf16[2,512,256]{2,1,0:T(8,128)(2,1)S(1)}, u32[]{:S(2)}, u32[]{:S(2)}) collective-permute-start(bf16[2,512,256]{2,1,0:T(8,128)(2,1)S(1)} %get-tuple-element.59.refs_2_.refs_9_), channel_id=1, source_target_pairs={{0,3},{1,0},{2,1},{3,2},{4,7},{5,4},{6,5},{7,6},{8,11},{9,8},{10,9... | collective-permute-start | bytes 1572872 | tf_op jit(solution)/shard_map/ppermute | solution.py:52
  33.9 13.7 %collective-permute-start.10 = (bf16[2,512,256]{2,1,0:T(8,128)(2,1)S(1)}, bf16[2,512,256]{2,1,0:T(8,128)(2,1)S(1)}, u32[]{:S(2)}, u32[]{:S(2)}) collective-permute-start(bf16[2,512,256]{2,1,0:T(8,128)(2,1)S(1)} %get-tuple-element.59.refs_2_.refs_9_), channel_id=1, source_target_pairs={{0,1},{1,2},{2,3},{3,0},{4,5},{5,6},{6,7},{7,4},{8,9},{9,10},{10,1... | collective-permute-start | bytes 1572872 | tf_op jit(solution)/shard_map/ppermute | solution.py:52
  40.3 12.5 %collective-permute-start.8 = (bf16[2,320,512]{2,1,0:T(8,128)(2,1)S(1)}, bf16[2,320,512]{2,1,0:T(8,128)(2,1)S(1)}, u32[]{:S(2)}, u32[]{:S(2)}) collective-permute-start(bf16[2,320,512]{2,1,0:T(8,128)(2,1)S(1)} %get-tuple-element.56), channel_id=1, source_target_pairs={{0,32},{8,104},{16,48},{24,120},{32,64},{40,8},{48,80},{56,24},{64... | collective-permute-start | bytes 1966088 | tf_op jit(solution)/shard_map/ppermute | solution.py:52
  49.2 14.1 %collective-permute-start.14 = (bf16[2,320,512]{2,1,0:T(8,128)(2,1)S(1)}, bf16[2,320,512]{2,1,0:T(8,128)(2,1)S(1)}, u32[]{:S(2)}, u32[]{:S(2)}) collective-permute-start(bf16[2,320,512]{2,1,0:T(8,128)(2,1)S(1)} %get-tuple-element.63), channel_id=1, source_target_pairs={{0,32},{8,104},{16,48},{24,120},{32,64},{40,8},{48,80},{56,24},{64... | collective-permute-start | bytes 1966088 | tf_op jit(solution)/shard_map/ppermute | solution.py:52
  52.0 11.3 %collective-permute-start.15 = (bf16[2,512,256]{2,1,0:T(8,128)(2,1)S(1)}, bf16[2,512,256]{2,1,0:T(8,128)(2,1)S(1)}, u32[]{:S(2)}, u32[]{:S(2)}) collective-permute-start(bf16[2,512,256]{2,1,0:T(8,128)(2,1)S(1)} %get-tuple-element.59.refs_2_.refs_9_), channel_id=1, source_target_pairs={{0,2},{1,3},{2,0},{3,1},{4,6},{5,7},{6,4},{7,5},{8,10},{9,11},{10,... | collective-permute-start | bytes 1572872 | tf_op jit(solution)/shard_map/ppermute | solution.py:52
  54.3 16.0 %collective-permute-start.12 = (bf16[2,320,512]{2,1,0:T(8,128)(2,1)S(1)}, bf16[2,320,512]{2,1,0:T(8,128)(2,1)S(1)}, u32[]{:S(2)}, u32[]{:S(2)}) collective-permute-start(bf16[2,320,512]{2,1,0:T(8,128)(2,1)S(1)} %get-tuple-element.61), channel_id=1, source_target_pairs={{0,32},{8,104},{16,48},{24,120},{32,64},{40,8},{48,80},{56,24},{64... | collective-permute-start | bytes 1966088 | tf_op jit(solution)/shard_map/ppermute | solution.py:52
  68.0 3.9 %collective-permute-start.17 = (bf16[640,256]{1,0:T(8,128)(2,1)S(1)}, bf16[640,256]{1,0:T(8,128)(2,1)S(1)}, u32[]{:S(2)}, u32[]{:S(2)}) collective-permute-start(bf16[640,256]{1,0:T(8,128)(2,1)S(1)} %get-tuple-element.68), channel_id=1, source_target_pairs={{0,8},{8,0},{1,9},{9,1},{2,10},{10,2},{3,11},{11,3},{4,12},{12,4},... | collective-permute-start | bytes 983048 | tf_op jit(solution)/shard_map/ppermute | solution.py:52
  68.1 10.7 %collective-permute-start.19 = (bf16[2,320,512]{2,1,0:T(8,128)(2,1)S(1)}, bf16[2,320,512]{2,1,0:T(8,128)(2,1)S(1)}, u32[]{:S(2)}, u32[]{:S(2)}) collective-permute-start(bf16[2,320,512]{2,1,0:T(8,128)(2,1)S(1)} %get-tuple-element.71), channel_id=1, source_target_pairs={{0,32},{8,104},{16,48},{24,120},{32,64},{40,8},{48,80},{56,24},{64... | collective-permute-start | bytes 1966088 | tf_op jit(solution)/shard_map/ppermute | solution.py:52
  73.4 12.4 %collective-permute-start.18 = (bf16[2,160,1024]{2,1,0:T(8,128)(2,1)S(1)}, bf16[2,160,1024]{2,1,0:T(8,128)(2,1)S(1)}, u32[]{:S(2)}, u32[]{:S(2)}) collective-permute-start(bf16[2,160,1024]{2,1,0:T(8,128)(2,1)S(1)} %get-tuple-element.70), channel_id=1, source_target_pairs={{0,32},{8,104},{16,48},{24,120},{32,64},{40,8},{48,80},{56,24},{64... | collective-permute-start | bytes 1966088 | tf_op jit(solution)/shard_map/ppermute | solution.py:52
  74.0 17.7 %collective-permute-start.16 = (bf16[2,320,512]{2,1,0:T(8,128)(2,1)S(1)}, bf16[2,320,512]{2,1,0:T(8,128)(2,1)S(1)}, u32[]{:S(2)}, u32[]{:S(2)}) collective-permute-start(bf16[2,320,512]{2,1,0:T(8,128)(2,1)S(1)} %get-tuple-element.67.a), channel_id=1, source_target_pairs={{0,16},{16,0},{32,48},{48,32},{64,80},{80,64},{96,112},{112,96},{1... | collective-permute-start | bytes 1966088 | tf_op jit(solution)/shard_map/ppermute | solution.py:52
  87.3 11.6 %collective-permute-start.24 = (bf16[2,160,1024]{2,1,0:T(8,128)(2,1)S(1)}, bf16[2,160,1024]{2,1,0:T(8,128)(2,1)S(1)}, u32[]{:S(2)}, u32[]{:S(2)}) collective-permute-start(bf16[2,160,1024]{2,1,0:T(8,128)(2,1)S(1)} %get-tuple-element.77), channel_id=1, source_target_pairs={{0,32},{8,104},{16,48},{24,120},{32,64},{40,8},{48,80},{56,24},{64... | collective-permute-start | bytes 1966088 | tf_op jit(solution)/shard_map/ppermute | solution.py:52
  90.7 15.4 %collective-permute-start.23 = (bf16[2,320,512]{2,1,0:T(8,128)(2,1)S(1)}, bf16[2,320,512]{2,1,0:T(8,128)(2,1)S(1)}, u32[]{:S(2)}, u32[]{:S(2)}) collective-permute-start(bf16[2,320,512]{2,1,0:T(8,128)(2,1)S(1)} %get-tuple-element.76.a), channel_id=1, source_target_pairs={{0,16},{16,0},{32,48},{48,32},{64,80},{80,64},{96,112},{112,96},{1... | collective-permute-start | bytes 1966088 | tf_op jit(solution)/shard_map/ppermute | solution.py:52
  100.4 11.9 %collective-permute-start.27 = (bf16[2,160,1024]{2,1,0:T(8,128)(2,1)S(1)}, bf16[2,160,1024]{2,1,0:T(8,128)(2,1)S(1)}, u32[]{:S(2)}, u32[]{:S(2)}) collective-permute-start(bf16[2,160,1024]{2,1,0:T(8,128)(2,1)S(1)} %get-tuple-element.81), channel_id=1, source_target_pairs={{0,32},{8,104},{16,48},{24,120},{32,64},{40,8},{48,80},{56,24},{64... | collective-permute-start | bytes 1966088 | tf_op jit(solution)/shard_map/ppermute | solution.py:52
  113.8 8.4 %collective-permute-start.28 = (bf16[160,1024]{1,0:T(8,128)(2,1)S(1)}, bf16[160,1024]{1,0:T(8,128)(2,1)S(1)}, u32[]{:S(2)}, u32[]{:S(2)}) collective-permute-start(bf16[160,1024]{1,0:T(8,128)(2,1)S(1)} %get-tuple-element.83.refs_8_), channel_id=1, source_target_pairs={{0,32},{8,104},{16,48},{24,120},{32,64},{40,8},{48,80},{56,24},{64... | collective-permute-start | bytes 983048 | tf_op jit(solution)/shard_map/ppermute | solution.py:52
  117.5 8.3 %collective-permute-start.20 = (bf16[320,512]{1,0:T(8,128)(2,1)S(1)}, bf16[320,512]{1,0:T(8,128)(2,1)S(1)}, u32[]{:S(2)}, u32[]{:S(2)}) collective-permute-start(bf16[320,512]{1,0:T(8,128)(2,1)S(1)} %get-tuple-element.75.refs_0_), channel_id=1, source_target_pairs={{0,32},{8,104},{16,48},{24,120},{32,64},{40,8},{48,80},{56,24},{64... | collective-permute-start | bytes 983048 | tf_op jit(solution)/shard_map/ppermute | solution.py:52
  117.6 11.7 %collective-permute-start.25 = (bf16[320,512]{1,0:T(8,128)(2,1)S(1)}, bf16[320,512]{1,0:T(8,128)(2,1)S(1)}, u32[]{:S(2)}, u32[]{:S(2)}) collective-permute-start(bf16[320,512]{1,0:T(8,128)(2,1)S(1)} %get-tuple-element.80.refs_4_), channel_id=1, source_target_pairs={{0,32},{8,104},{16,48},{24,120},{32,64},{40,8},{48,80},{56,24},{64... | collective-permute-start | bytes 983048 | tf_op jit(solution)/shard_map/ppermute | solution.py:52
  117.7 16.0 %collective-permute-start.32 = (bf16[160,1024]{1,0:T(8,128)(2,1)S(1)}, bf16[160,1024]{1,0:T(8,128)(2,1)S(1)}, u32[]{:S(2)}, u32[]{:S(2)}) collective-permute-start(bf16[160,1024]{1,0:T(8,128)(2,1)S(1)} %get-tuple-element.83.refs_8_), channel_id=1, source_target_pairs={{0,16},{16,0},{32,48},{48,32},{64,80},{80,64},{96,112},{112,96},{1... | collective-permute-start | bytes 983048 | tf_op jit(solution)/shard_map/ppermute | solution.py:52
  122.1 11.6 %collective-permute-start.31 = (bf16[160,1024]{1,0:T(8,128)(2,1)S(1)}, bf16[160,1024]{1,0:T(8,128)(2,1)S(1)}, u32[]{:S(2)}, u32[]{:S(2)}) collective-permute-start(bf16[160,1024]{1,0:T(8,128)(2,1)S(1)} %collective-permute-done.28.refs_9_), channel_id=1, source_target_pairs={{0,32},{8,104},{16,48},{24,120},{32,64},{40,8},{48,80},{56,24},{64... | collective-permute-start | bytes 983048 | tf_op jit(solution)/shard_map/ppermute | solution.py:52
  125.8 11.1 %collective-permute-start.21 = (bf16[320,512]{1,0:T(8,128)(2,1)S(1)}, bf16[320,512]{1,0:T(8,128)(2,1)S(1)}, u32[]{:S(2)}, u32[]{:S(2)}) collective-permute-start(bf16[320,512]{1,0:T(8,128)(2,1)S(1)} %collective-permute-done.20.refs_1_), channel_id=1, source_target_pairs={{0,32},{8,104},{16,48},{24,120},{32,64},{40,8},{48,80},{56,24},{64... | collective-permute-start | bytes 983048 | tf_op jit(solution)/shard_map/ppermute | solution.py:52
  129.3 11.4 %collective-permute-start.26 = (bf16[320,512]{1,0:T(8,128)(2,1)S(1)}, bf16[320,512]{1,0:T(8,128)(2,1)S(1)}, u32[]{:S(2)}, u32[]{:S(2)}) collective-permute-start(bf16[320,512]{1,0:T(8,128)(2,1)S(1)} %collective-permute-done.25.refs_5_), channel_id=1, source_target_pairs={{0,32},{8,104},{16,48},{24,120},{32,64},{40,8},{48,80},{56,24},{64... | collective-permute-start | bytes 983048 | tf_op jit(solution)/shard_map/ppermute | solution.py:52
  132.8 12.0 %collective-permute-start.29 = (bf16[160,1024]{1,0:T(8,128)(2,1)S(1)}, bf16[160,1024]{1,0:T(8,128)(2,1)S(1)}, u32[]{:S(2)}, u32[]{:S(2)}) collective-permute-start(bf16[160,1024]{1,0:T(8,128)(2,1)S(1)} %collective-permute-done.28.refs_9_), channel_id=1, source_target_pairs={{0,16},{16,0},{32,48},{48,32},{64,80},{80,64},{96,112},{112,96},{1... | collective-permute-start | bytes 983048 | tf_op jit(solution)/shard_map/ppermute | solution.py:52
  134.3 11.2 %collective-permute-start.33 = (bf16[160,1024]{1,0:T(8,128)(2,1)S(1)}, bf16[160,1024]{1,0:T(8,128)(2,1)S(1)}, u32[]{:S(2)}, u32[]{:S(2)}) collective-permute-start(bf16[160,1024]{1,0:T(8,128)(2,1)S(1)} %get-tuple-element.85.refs_10_), channel_id=1, source_target_pairs={{0,32},{8,104},{16,48},{24,120},{32,64},{40,8},{48,80},{56,24},{64... | collective-permute-start | bytes 983048 | tf_op jit(solution)/shard_map/ppermute | solution.py:52
  136.9 9.8 %collective-permute-start.22 = (bf16[320,512]{1,0:T(8,128)(2,1)S(1)}, bf16[320,512]{1,0:T(8,128)(2,1)S(1)}, u32[]{:S(2)}, u32[]{:S(2)}) collective-permute-start(bf16[320,512]{1,0:T(8,128)(2,1)S(1)} %collective-permute-done.21.refs_2_), channel_id=1, source_target_pairs={{0,32},{8,104},{16,48},{24,120},{32,64},{40,8},{48,80},{56,24},{64... | collective-permute-start | bytes 983048 | tf_op jit(solution)/shard_map/ppermute | solution.py:52
  139.9 12.0 %collective-permute-start.34 = (bf16[160,1024]{1,0:T(8,128)(2,1)S(1)}, bf16[160,1024]{1,0:T(8,128)(2,1)S(1)}, u32[]{:S(2)}, u32[]{:S(2)}) collective-permute-start(bf16[160,1024]{1,0:T(8,128)(2,1)S(1)} %get-tuple-element.85.refs_10_), channel_id=1, source_target_pairs={{0,16},{16,0},{32,48},{48,32},{64,80},{80,64},{96,112},{112,96},{1... | collective-permute-start | bytes 983048 | tf_op jit(solution)/shard_map/ppermute | solution.py:52
  145.5 7.1 %collective-permute-start.30 = (bf16[320,512]{1,0:T(8,128)(2,1)S(1)}, bf16[320,512]{1,0:T(8,128)(2,1)S(1)}, u32[]{:S(2)}, u32[]{:S(2)}) collective-permute-start(bf16[320,512]{1,0:T(8,128)(2,1)S(1)} %get-tuple-element.84.refs_6_), channel_id=1, source_target_pairs={{0,32},{8,104},{16,48},{24,120},{32,64},{40,8},{48,80},{56,24},{64... | collective-permute-start | bytes 983048 | tf_op jit(solution)/shard_map/ppermute | solution.py:52
  145.5 10.0 %collective-permute-start.35 = (bf16[160,1024]{1,0:T(8,128)(2,1)S(1)}, bf16[160,1024]{1,0:T(8,128)(2,1)S(1)}, u32[]{:S(2)}, u32[]{:S(2)}) collective-permute-start(bf16[160,1024]{1,0:T(8,128)(2,1)S(1)} %collective-permute-done.33.refs_11_), channel_id=1, source_target_pairs={{0,16},{16,0},{32,48},{48,32},{64,80},{80,64},{96,112},{112,96},{1... | collective-permute-start | bytes 983048 | tf_op jit(solution)/shard_map/ppermute | solution.py:52

commit v4 on v3

--- a/solution.py
+++ b/solution.py
@@ -362,11 +362,11 @@
             extra = {(2, 1): [far[1], far[3]], (3, 1): far[2:3]}.get((k, p), [])
             piece, token = ring_terms(p, k, got[p], token, *extra)
             got[p] = (move(piece, RING, ("task", "row")),)
-    zb, token = cut(za, HALF, token)
-    zb = move(zb, CORE_SWAP, "row")
     a_sum, a_got, a_all = [None, None], [None, None], [None, None]
     a_sum[0], token = ring_terms(0, 0, got[0], token)
     a_got[0] = move(a_sum[0], Z_SWAP)
+    zb, token = cut(za, HALF, token)
+    zb = move(zb, CORE_SWAP, "row")
     b_got, early = (), []
     for k in (1, 2, 3):
         piece, token = far_terms(k, b_got, False, token)

time: 159 us -> 171 us (1.075)
  waiting for transfers between devices: 65.9 us -> 84.2 us
  starting transfers between devices: 57.4 us -> 50.8 us
    ppermute x36, waiting for transfers between devices: 65.9 us -> 84.2 us  [move(): return lax.ppermute(x, axis, perm)]
    ppermute x36, starting transfers between devices: 57.4 us -> 50.8 us  [move(): return lax.ppermute(x, axis, perm)]
  transfers between devices with their start and end apart: 36 -> 36, of which waited for: 19 -> 19; matrix products, arithmetic and copies ran while one was open for 0% -> 0% of each run, Pallas kernels for 17% -> 16%
where the time goes in v4:
time: 171 us
  waiting for transfers between devices  84.2 us (49%)
  starting transfers between devices  50.8 us (30%)
  Pallas kernels  35.1 us (21%)
    ppermute x36, waiting for transfers between devices, move(): return lax.ppermute(x, axis, perm)  84.2 us
    ppermute x36, starting transfers between devices, move(): return lax.ppermute(x, axis, perm)  50.8 us
    pallas_call x12, Pallas kernels, terms(): pl.pallas_call(functools.partial(term_kernel, rows, nb, [s[5] for s in so...  18.3 us
    pallas_call x1, Pallas kernels, project(): pl.pallas_call(functools.partial(project_kernel, step), in_specs=[SMEM] +...  10.5 us
  transfers between devices with their start and end apart: 36, of which 19 were waited for; matrix products, arithmetic and copies ran while one was open for 0% of the time, Pallas kernels for 16%

profile of v4, /device:TPU:56, one launch (start us, length us, event | category | flops | bytes accessed | tf_op | source)
XLA Modules:
  0.0 170.6 jit_solution(9166892264834876141)
XLA Ops:
  0.0 3.0 %collective-permute-start.4 = (bf16[512,256]{1,0:T(8,128)(2,1)}, bf16[512,256]{1,0:T(8,128)(2,1)S(1)}, u32[]{:S(2)}, u32[]{:S(2)}) collective-permute-start(bf16[512,256]{1,0:T(8,128)(2,1)} %bitcast.51), channel_id=1, source_target_pairs={{0,2},{1,3},{2,0},{3,1},{4,6},{5,7},{6,4},{7,5},{8,10},{9,11},{10,... | collective-permute-start | bytes 786440 | tf_op jit(solution)/shard_map/ppermute | solution.py:52
  5.1 1.9 %collective-permute-start.1 = (bf16[512,256]{1,0:T(8,128)(2,1)}, bf16[512,256]{1,0:T(8,128)(2,1)S(1)}, u32[]{:S(2)}, u32[]{:S(2)}) collective-permute-start(bf16[512,256]{1,0:T(8,128)(2,1)} %bitcast.54), channel_id=1, source_target_pairs={{0,20},{1,21},{2,22},{3,23},{4,16},{5,17},{6,18},{7,19},{16,4},{17... | collective-permute-start | bytes 786440 | tf_op jit(solution)/shard_map/ppermute | solution.py:52
  7.0 2.2 %collective-permute-start = (bf16[512,256]{1,0:T(8,128)(2,1)}, bf16[512,256]{1,0:T(8,128)(2,1)S(1)}, u32[]{:S(2)}, u32[]{:S(2)}) collective-permute-start(bf16[512,256]{1,0:T(8,128)(2,1)} %bitcast.55), channel_id=1, source_target_pairs={{0,4},{1,5},{2,6},{3,7},{4,0},{5,1},{6,2},{7,3},{8,12},{9,13},{10,... | collective-permute-start | bytes 786440 | tf_op jit(solution)/shard_map/ppermute | solution.py:52
  9.3 10.5 %shard_map.55 = (f32[2,256,1280]{2,1,0:T(8,128)S(1)}, bf16[2,256,1280]{2,1,0:T(8,128)(2,1)S(1)}, f32[8,128]{1,0:T(8,128)S(1)}) custom-call(s32[39]{0:T(128)S(1)} %stack.135.offs, bf16[512,2048]{1,0:T(8,128)(2,1)} %bitcast.62, bf16[2048,1280]{1,0:T(8,128)(2,1)} %bitcast.60, bf16[2048,1280]{1,0:T(8,128)(2,1)} %bitcast.61), custom_call_target="tpu_custom_call" | custom-call | tf_op jit(solution)/shard_map/pallas_call | solution.py:95
  20.0 3.0 %collective-permute-done.5.recv_ref = bf16[2,256,1280]{2,1,0:T(8,128)(2,1)S(1)} collective-permute-done((bf16[2,256,1280]{2,1,0:T(8,128)(2,1)S(1)}, bf16[2,256,1280]{2,1,0:T(8,128)(2,1)S(1)}, u32[]{:S(2)}, u32[]{:S(2)}) %collective-permute-start.5) | collective-permute-done | bytes 1310752 | tf_op jit(solution)/shard_map/ppermute | solution.py:52
  24.6 2.0 %collective-permute-done.6.refs_1_ = bf16[1280,256]{1,0:T(8,128)(2,1)S(1)} collective-permute-done((bf16[1280,256]{1,0:T(8,128)(2,1)S(1)}, bf16[1280,256]{1,0:T(8,128)(2,1)S(1)}, u32[]{:S(2)}, u32[]{:S(2)}) %collective-permute-start.6) | collective-permute-done | bytes 655392 | tf_op jit(solution)/shard_map/ppermute | solution.py:52
  26.6 1.5 shard_map.58
  28.4 1.5 shard_map.59
  29.9 1.6 collective-permute-start.9
  31.5 7.2 %collective-permute-done.7.refs_5_ = bf16[2,320,512]{2,1,0:T(8,128)(2,1)S(1)} collective-permute-done((bf16[2,320,512]{2,1,0:T(8,128)(2,1)S(1)}, bf16[2,320,512]{2,1,0:T(8,128)(2,1)S(1)}, u32[]{:S(2)}, u32[]{:S(2)}) %collective-permute-start.7) | collective-permute-done | bytes 655392 | tf_op jit(solution)/shard_map/ppermute | solution.py:52
  38.7 1.6 shard_map.60
  40.3 1.5 collective-permute-start.8
  41.8 2.3 %collective-permute-start.11 = (bf16[2,512,256]{2,1,0:T(8,128)(2,1)S(1)}, bf16[2,512,256]{2,1,0:T(8,128)(2,1)S(1)}, u32[]{:S(2)}, u32[]{:S(2)}) collective-permute-start(bf16[2,512,256]{2,1,0:T(8,128)(2,1)S(1)} %get-tuple-element.59.refs_2_.refs_9_), channel_id=1, source_target_pairs={{0,3},{1,0},{2,1},{3,2},{4,7},{5,4},{6,5},{7,6},{8,11},{9,8},{10,9... | collective-permute-start | bytes 1572872 | tf_op jit(solution)/shard_map/ppermute | solution.py:52
  44.2 10.6 %collective-permute-done.11.refs_8_.refs_5_.refs_12_ = bf16[2,512,256]{2,1,0:T(8,128)(2,1)S(1)} collective-permute-done((bf16[2,512,256]{2,1,0:T(8,128)(2,1)S(1)}, bf16[2,512,256]{2,1,0:T(8,128)(2,1)S(1)}, u32[]{:S(2)}, u32[]{:S(2)}) %collective-permute-start.11) | collective-permute-done | bytes 524320 | tf_op jit(solution)/shard_map/ppermute | solution.py:52
  54.8 3.3 %collective-permute-done.10.refs_7_.refs_3_.refs_10_ = bf16[2,512,256]{2,1,0:T(8,128)(2,1)S(1)} collective-permute-done((bf16[2,512,256]{2,1,0:T(8,128)(2,1)S(1)}, bf16[2,512,256]{2,1,0:T(8,128)(2,1)S(1)}, u32[]{:S(2)}, u32[]{:S(2)}) %collective-permute-start.10) | collective-permute-done | bytes 524320 | tf_op jit(solution)/shard_map/ppermute | solution.py:52
  58.1 1.6 shard_map.61
  59.7 2.3 %collective-permute-start.13 = (bf16[2,320,512]{2,1,0:T(8,128)(2,1)S(1)}, bf16[2,320,512]{2,1,0:T(8,128)(2,1)S(1)}, u32[]{:S(2)}, u32[]{:S(2)}) collective-permute-start(bf16[2,320,512]{2,1,0:T(8,128)(2,1)S(1)} %get-tuple-element.62), channel_id=1, source_target_pairs={{0,32},{8,104},{16,48},{24,120},{32,64},{40,8},{48,80},{56,24},{64... | collective-permute-start | bytes 1966088 | tf_op jit(solution)/shard_map/ppermute | solution.py:52
  61.9 1.6 shard_map.62
  63.7 11.1 %collective-permute-done.14.refs_7_.refs_4_.refs_11_ = bf16[2,512,256]{2,1,0:T(8,128)(2,1)S(1)} collective-permute-done((bf16[2,512,256]{2,1,0:T(8,128)(2,1)S(1)}, bf16[2,512,256]{2,1,0:T(8,128)(2,1)S(1)}, u32[]{:S(2)}, u32[]{:S(2)}) %collective-permute-start.14) | collective-permute-done | bytes 524320 | tf_op jit(solution)/shard_map/ppermute | solution.py:52
  74.8 1.6 shard_map.63
  77.3 1.6 shard_map.64
  79.0 3.6 %collective-permute-start.19 = (bf16[2,320,512]{2,1,0:T(8,128)(2,1)S(1)}, bf16[2,320,512]{2,1,0:T(8,128)(2,1)S(1)}, u32[]{:S(2)}, u32[]{:S(2)}) collective-permute-start(bf16[2,320,512]{2,1,0:T(8,128)(2,1)S(1)} %get-tuple-element.71), channel_id=1, source_target_pairs={{0,32},{8,104},{16,48},{24,120},{32,64},{40,8},{48,80},{56,24},{64... | collective-permute-start | bytes 1966088 | tf_op jit(solution)/shard_map/ppermute | solution.py:52
  82.6 1.4 shard_map.66
  84.1 1.8 %collective-permute-start.18 = (bf16[2,160,1024]{2,1,0:T(8,128)(2,1)S(1)}, bf16[2,160,1024]{2,1,0:T(8,128)(2,1)S(1)}, u32[]{:S(2)}, u32[]{:S(2)}) collective-permute-start(bf16[2,160,1024]{2,1,0:T(8,128)(2,1)S(1)} %get-tuple-element.70), channel_id=1, source_target_pairs={{0,32},{8,104},{16,48},{24,120},{32,64},{40,8},{48,80},{56,24},{64... | collective-permute-start | bytes 1966088 | tf_op jit(solution)/shard_map/ppermute | solution.py:52
  85.9 6.1 %collective-permute-done.19.refs_5_ = bf16[2,320,512]{2,1,0:T(8,128)(2,1)S(1)} collective-permute-done((bf16[2,320,512]{2,1,0:T(8,128)(2,1)S(1)}, bf16[2,320,512]{2,1,0:T(8,128)(2,1)S(1)}, u32[]{:S(2)}, u32[]{:S(2)}) %collective-permute-start.19) | collective-permute-done | bytes 655392 | tf_op jit(solution)/shard_map/ppermute | solution.py:52
  91.9 1.6 shard_map.67
  93.5 5.5 %collective-permute-done.18.refs_14_ = bf16[2,160,1024]{2,1,0:T(8,128)(2,1)S(1)} collective-permute-done((bf16[2,160,1024]{2,1,0:T(8,128)(2,1)S(1)}, bf16[2,160,1024]{2,1,0:T(8,128)(2,1)S(1)}, u32[]{:S(2)}, u32[]{:S(2)}) %collective-permute-start.18) | collective-permute-done | bytes 655392 | tf_op jit(solution)/shard_map/ppermute | solution.py:52
  98.9 1.5 shard_map.68
  100.4 2.6 %collective-permute-start.24 = (bf16[2,160,1024]{2,1,0:T(8,128)(2,1)S(1)}, bf16[2,160,1024]{2,1,0:T(8,128)(2,1)S(1)}, u32[]{:S(2)}, u32[]{:S(2)}) collective-permute-start(bf16[2,160,1024]{2,1,0:T(8,128)(2,1)S(1)} %get-tuple-element.77), channel_id=1, source_target_pairs={{0,32},{8,104},{16,48},{24,120},{32,64},{40,8},{48,80},{56,24},{64... | collective-permute-start | bytes 1966088 | tf_op jit(solution)/shard_map/ppermute | solution.py:52
  103.0 1.4 collective-permute-done.15.b
  104.6 6.5 %collective-permute-done.24.refs_14_ = bf16[2,160,1024]{2,1,0:T(8,128)(2,1)S(1)} collective-permute-done((bf16[2,160,1024]{2,1,0:T(8,128)(2,1)S(1)}, bf16[2,160,1024]{2,1,0:T(8,128)(2,1)S(1)}, u32[]{:S(2)}, u32[]{:S(2)}) %collective-permute-start.24) | collective-permute-done | bytes 655392 | tf_op jit(solution)/shard_map/ppermute | solution.py:52
  111.1 1.5 shard_map.70
  112.6 3.8 %collective-permute-start.27 = (bf16[2,160,1024]{2,1,0:T(8,128)(2,1)S(1)}, bf16[2,160,1024]{2,1,0:T(8,128)(2,1)S(1)}, u32[]{:S(2)}, u32[]{:S(2)}) collective-permute-start(bf16[2,160,1024]{2,1,0:T(8,128)(2,1)S(1)} %get-tuple-element.81), channel_id=1, source_target_pairs={{0,32},{8,104},{16,48},{24,120},{32,64},{40,8},{48,80},{56,24},{64... | collective-permute-start | bytes 1966088 | tf_op jit(solution)/shard_map/ppermute | solution.py:52
  116.4 3.6 %collective-permute-done.23.b = bf16[2,320,512]{2,1,0:T(8,128)(2,1)S(1)} collective-permute-done((bf16[2,320,512]{2,1,0:T(8,128)(2,1)S(1)}, bf16[2,320,512]{2,1,0:T(8,128)(2,1)S(1)}, u32[]{:S(2)}, u32[]{:S(2)}) %collective-permute-start.23) | collective-permute-done | bytes 655392 | tf_op jit(solution)/shard_map/ppermute | solution.py:52
  120.2 4.3 %collective-permute-done.27.refs_14_ = bf16[2,160,1024]{2,1,0:T(8,128)(2,1)S(1)} collective-permute-done((bf16[2,160,1024]{2,1,0:T(8,128)(2,1)S(1)}, bf16[2,160,1024]{2,1,0:T(8,128)(2,1)S(1)}, u32[]{:S(2)}, u32[]{:S(2)}) %collective-permute-start.27) | collective-permute-done | bytes 655392 | tf_op jit(solution)/shard_map/ppermute | solution.py:52
  124.5 1.5 shard_map.72
  126.0 3.8 %collective-permute-start.28 = (bf16[160,1024]{1,0:T(8,128)(2,1)S(1)}, bf16[160,1024]{1,0:T(8,128)(2,1)S(1)}, u32[]{:S(2)}, u32[]{:S(2)}) collective-permute-start(bf16[160,1024]{1,0:T(8,128)(2,1)S(1)} %get-tuple-element.83.refs_8_), channel_id=1, source_target_pairs={{0,32},{8,104},{16,48},{24,120},{32,64},{40,8},{48,80},{56,24},{64... | collective-permute-start | bytes 983048 | tf_op jit(solution)/shard_map/ppermute | solution.py:52
  129.9 4.4 %collective-permute-done.28.refs_9_ = bf16[160,1024]{1,0:T(8,128)(2,1)S(1)} collective-permute-done((bf16[160,1024]{1,0:T(8,128)(2,1)S(1)}, bf16[160,1024]{1,0:T(8,128)(2,1)S(1)}, u32[]{:S(2)}, u32[]{:S(2)}) %collective-permute-start.28) | collective-permute-done | bytes 327712 | tf_op jit(solution)/shard_map/ppermute | solution.py:52
  134.4 3.7 %collective-permute-start.31 = (bf16[160,1024]{1,0:T(8,128)(2,1)S(1)}, bf16[160,1024]{1,0:T(8,128)(2,1)S(1)}, u32[]{:S(2)}, u32[]{:S(2)}) collective-permute-start(bf16[160,1024]{1,0:T(8,128)(2,1)S(1)} %collective-permute-done.28.refs_9_), channel_id=1, source_target_pairs={{0,32},{8,104},{16,48},{24,120},{32,64},{40,8},{48,80},{56,24},{64... | collective-permute-start | bytes 983048 | tf_op jit(solution)/shard_map/ppermute | solution.py:52
  138.1 3.5 %collective-permute-start.21 = (bf16[320,512]{1,0:T(8,128)(2,1)S(1)}, bf16[320,512]{1,0:T(8,128)(2,1)S(1)}, u32[]{:S(2)}, u32[]{:S(2)}) collective-permute-start(bf16[320,512]{1,0:T(8,128)(2,1)S(1)} %collective-permute-done.20.refs_1_), channel_id=1, source_target_pairs={{0,32},{8,104},{16,48},{24,120},{32,64},{40,8},{48,80},{56,24},{64... | collective-permute-start | bytes 983048 | tf_op jit(solution)/shard_map/ppermute | solution.py:52
  141.6 3.5 %collective-permute-start.26 = (bf16[320,512]{1,0:T(8,128)(2,1)S(1)}, bf16[320,512]{1,0:T(8,128)(2,1)S(1)}, u32[]{:S(2)}, u32[]{:S(2)}) collective-permute-start(bf16[320,512]{1,0:T(8,128)(2,1)S(1)} %collective-permute-done.25.refs_5_), channel_id=1, source_target_pairs={{0,32},{8,104},{16,48},{24,120},{32,64},{40,8},{48,80},{56,24},{64... | collective-permute-start | bytes 983048 | tf_op jit(solution)/shard_map/ppermute | solution.py:52
  145.7 3.5 %collective-permute-start.33 = (bf16[160,1024]{1,0:T(8,128)(2,1)S(1)}, bf16[160,1024]{1,0:T(8,128)(2,1)S(1)}, u32[]{:S(2)}, u32[]{:S(2)}) collective-permute-start(bf16[160,1024]{1,0:T(8,128)(2,1)S(1)} %get-tuple-element.85.refs_10_), channel_id=1, source_target_pairs={{0,32},{8,104},{16,48},{24,120},{32,64},{40,8},{48,80},{56,24},{64... | collective-permute-start | bytes 983048 | tf_op jit(solution)/shard_map/ppermute | solution.py:52
  149.2 2.9 %collective-permute-start.22 = (bf16[320,512]{1,0:T(8,128)(2,1)S(1)}, bf16[320,512]{1,0:T(8,128)(2,1)S(1)}, u32[]{:S(2)}, u32[]{:S(2)}) collective-permute-start(bf16[320,512]{1,0:T(8,128)(2,1)S(1)} %collective-permute-done.21.refs_2_), channel_id=1, source_target_pairs={{0,32},{8,104},{16,48},{24,120},{32,64},{40,8},{48,80},{56,24},{64... | collective-permute-start | bytes 983048 | tf_op jit(solution)/shard_map/ppermute | solution.py:52
  152.1 4.4 %collective-permute-done.29.refs_1_.refs_13_ = bf16[160,1024]{1,0:T(8,128)(2,1)S(1)} collective-permute-done((bf16[160,1024]{1,0:T(8,128)(2,1)S(1)}, bf16[160,1024]{1,0:T(8,128)(2,1)S(1)}, u32[]{:S(2)}, u32[]{:S(2)}) %collective-permute-start.29) | collective-permute-done | bytes 327712 | tf_op jit(solution)/shard_map/ppermute | solution.py:52
  157.4 1.5 collective-permute-done.22.refs_3_
  158.9 4.8 %collective-permute-done.34.refs_14_ = bf16[160,1024]{1,0:T(8,128)(2,1)S(1)} collective-permute-done((bf16[160,1024]{1,0:T(8,128)(2,1)S(1)}, bf16[160,1024]{1,0:T(8,128)(2,1)S(1)}, u32[]{:S(2)}, u32[]{:S(2)}) %collective-permute-start.34) | collective-permute-done | bytes 327712 | tf_op jit(solution)/shard_map/ppermute | solution.py:52
  164.2 3.0 %collective-permute-done.35.refs_15_ = bf16[160,1024]{1,0:T(8,128)(2,1)S(1)} collective-permute-done((bf16[160,1024]{1,0:T(8,128)(2,1)S(1)}, bf16[160,1024]{1,0:T(8,128)(2,1)S(1)}, u32[]{:S(2)}, u32[]{:S(2)}) %collective-permute-start.35) | collective-permute-done | bytes 327712 | tf_op jit(solution)/shard_map/ppermute | solution.py:52
  167.2 3.3 %shard_map.75 = bf16[1280,2048]{1,0:T(8,128)(2,1)} custom-call(s32[39]{0:T(128)S(1)} %stack.135.offs, bf16[320,512]{1,0:T(8,128)(2,1)S(1)} %get-tuple-element.75.refs_0_, bf16[320,512]{1,0:T(8,128)(2,1)S(1)} %collective-permute-done.20.refs_1_, bf16[320,512]{1,0:T(8,128)(2,1)S(1)} %collective-permute-done.21.refs_2_, ...), custom_call_target="tpu_custom_call" | custom-call | tf_op jit(solution)/shard_map/pallas_call | solution.py:282
  (53 shorter events, 8.0 us)
Async XLA Ops:
  0.0 19.8 %collective-permute-start.4 = (bf16[512,256]{1,0:T(8,128)(2,1)}, bf16[512,256]{1,0:T(8,128)(2,1)S(1)}, u32[]{:S(2)}, u32[]{:S(2)}) collective-permute-start(bf16[512,256]{1,0:T(8,128)(2,1)} %bitcast.51), channel_id=1, source_target_pairs={{0,2},{1,3},{2,0},{3,1},{4,6},{5,7},{6,4},{7,5},{8,10},{9,11},{10,... | collective-permute-start | bytes 786440 | tf_op jit(solution)/shard_map/ppermute | solution.py:52
  3.0 16.8 %collective-permute-start.3 = (bf16[512,256]{1,0:T(8,128)(2,1)}, bf16[512,256]{1,0:T(8,128)(2,1)S(1)}, u32[]{:S(2)}, u32[]{:S(2)}) collective-permute-start(bf16[512,256]{1,0:T(8,128)(2,1)} %bitcast.52), channel_id=1, source_target_pairs={{0,3},{1,0},{2,1},{3,2},{4,7},{5,4},{6,5},{7,6},{8,11},{9,8},{10,9... | collective-permute-start | bytes 786440 | tf_op jit(solution)/shard_map/ppermute | solution.py:52
  4.2 15.7 %collective-permute-start.2 = (bf16[512,256]{1,0:T(8,128)(2,1)}, bf16[512,256]{1,0:T(8,128)(2,1)S(1)}, u32[]{:S(2)}, u32[]{:S(2)}) collective-permute-start(bf16[512,256]{1,0:T(8,128)(2,1)} %bitcast.53), channel_id=1, source_target_pairs={{0,1},{1,2},{2,3},{3,0},{4,5},{5,6},{6,7},{7,4},{8,9},{9,10},{10,1... | collective-permute-start | bytes 786440 | tf_op jit(solution)/shard_map/ppermute | solution.py:52
  5.1 14.8 %collective-permute-start.1 = (bf16[512,256]{1,0:T(8,128)(2,1)}, bf16[512,256]{1,0:T(8,128)(2,1)S(1)}, u32[]{:S(2)}, u32[]{:S(2)}) collective-permute-start(bf16[512,256]{1,0:T(8,128)(2,1)} %bitcast.54), channel_id=1, source_target_pairs={{0,20},{1,21},{2,22},{3,23},{4,16},{5,17},{6,18},{7,19},{16,4},{17... | collective-permute-start | bytes 786440 | tf_op jit(solution)/shard_map/ppermute | solution.py:52
  7.0 12.9 %collective-permute-start = (bf16[512,256]{1,0:T(8,128)(2,1)}, bf16[512,256]{1,0:T(8,128)(2,1)S(1)}, u32[]{:S(2)}, u32[]{:S(2)}) collective-permute-start(bf16[512,256]{1,0:T(8,128)(2,1)} %bitcast.55), channel_id=1, source_target_pairs={{0,4},{1,5},{2,6},{3,7},{4,0},{5,1},{6,2},{7,3},{8,12},{9,13},{10,... | collective-permute-start | bytes 786440 | tf_op jit(solution)/shard_map/ppermute | solution.py:52
  9.3 13.7 %slice-start = ((s8[5242880]{0:T(1024)(128)(4,1)}), s8[4194304]{0:T(1024)(128)(4,1)S(1)}, s32[]{:S(2)}) async-start(s8[5242880]{0:T(1024)(128)(4,1)} %bitcast.36), calls=%async_computation | async-start | bytes 8388608
  9.3 13.7 %slice-start.1 = ((s8[5242880]{0:T(1024)(128)(4,1)}), s8[1048576]{0:T(1024)(128)(4,1)S(1)}, s32[]{:S(2)}) async-start(s8[5242880]{0:T(1024)(128)(4,1)} %bitcast.36), calls=%async_computation.1 | async-start | bytes 2097152
  19.9 3.1 %collective-permute-start.5 = (bf16[2,256,1280]{2,1,0:T(8,128)(2,1)S(1)}, bf16[2,256,1280]{2,1,0:T(8,128)(2,1)S(1)}, u32[]{:S(2)}, u32[]{:S(2)}) collective-permute-start(bf16[2,256,1280]{2,1,0:T(8,128)(2,1)S(1)} %get-tuple-element.49), channel_id=1, source_target_pairs={{0,8},{8,0},{1,9},{9,1},{2,10},{10,2},{3,11},{11,3},{4,12},{12,4},... | collective-permute-start | bytes 3932168 | tf_op jit(solution)/shard_map/ppermute | solution.py:52
  23.0 3.5 %copy-start = (bf16[1,512,256]{2,1,0:T(8,128)(2,1)S(1)}, bf16[1,512,256]{2,1,0:T(8,128)(2,1)}, u32[]{:S(2)}) copy-start(bf16[1,512,256]{2,1,0:T(8,128)(2,1)} %param.8) | copy-start | bytes 786436
  24.4 2.2 %collective-permute-start.6 = (bf16[1280,256]{1,0:T(8,128)(2,1)S(1)}, bf16[1280,256]{1,0:T(8,128)(2,1)S(1)}, u32[]{:S(2)}, u32[]{:S(2)}) collective-permute-start(bf16[1280,256]{1,0:T(8,128)(2,1)S(1)} %get-tuple-element.51.refs_0_), channel_id=1, source_target_pairs={{0,8},{8,0},{1,9},{9,1},{2,10},{10,2},{3,11},{11,3},{4,12},{12,4},... | collective-permute-start | bytes 1966088 | tf_op jit(solution)/shard_map/ppermute | solution.py:52
  28.1 10.7 %collective-permute-start.7 = (bf16[2,320,512]{2,1,0:T(8,128)(2,1)S(1)}, bf16[2,320,512]{2,1,0:T(8,128)(2,1)S(1)}, u32[]{:S(2)}, u32[]{:S(2)}) collective-permute-start(bf16[2,320,512]{2,1,0:T(8,128)(2,1)S(1)} %get-tuple-element.53), channel_id=1, source_target_pairs={{0,32},{8,104},{16,48},{24,120},{32,64},{40,8},{48,80},{56,24},{64... | collective-permute-start | bytes 1966088 | tf_op jit(solution)/shard_map/ppermute | solution.py:52
  28.4 50.5 %collective-permute-start.16 = (bf16[640,1280]{1,0:T(8,128)(2,1)S(1)}, bf16[640,1280]{1,0:T(8,128)(2,1)S(1)}, u32[]{:S(2)}, u32[]{:S(2)}) collective-permute-start(bf16[640,1280]{1,0:T(8,128)(2,1)S(1)} %get-tuple-element.66), channel_id=1, source_target_pairs={{0,16},{16,0},{32,48},{48,32},{64,80},{80,64},{96,112},{112,96},{1... | collective-permute-start | bytes 4915208 | tf_op jit(solution)/shard_map/ppermute | solution.py:52
  29.9 28.2 %collective-permute-start.9 = (bf16[2,320,512]{2,1,0:T(8,128)(2,1)S(1)}, bf16[2,320,512]{2,1,0:T(8,128)(2,1)S(1)}, u32[]{:S(2)}, u32[]{:S(2)}) collective-permute-start(bf16[2,320,512]{2,1,0:T(8,128)(2,1)S(1)} %get-tuple-element.57), channel_id=1, source_target_pairs={{0,32},{8,104},{16,48},{24,120},{32,64},{40,8},{48,80},{56,24},{64... | collective-permute-start | bytes 1966088 | tf_op jit(solution)/shard_map/ppermute | solution.py:52
  40.3 21.6 %collective-permute-start.8 = (bf16[2,320,512]{2,1,0:T(8,128)(2,1)S(1)}, bf16[2,320,512]{2,1,0:T(8,128)(2,1)S(1)}, u32[]{:S(2)}, u32[]{:S(2)}) collective-permute-start(bf16[2,320,512]{2,1,0:T(8,128)(2,1)S(1)} %get-tuple-element.56), channel_id=1, source_target_pairs={{0,32},{8,104},{16,48},{24,120},{32,64},{40,8},{48,80},{56,24},{64... | collective-permute-start | bytes 1966088 | tf_op jit(solution)/shard_map/ppermute | solution.py:52
  41.8 13.0 %collective-permute-start.11 = (bf16[2,512,256]{2,1,0:T(8,128)(2,1)S(1)}, bf16[2,512,256]{2,1,0:T(8,128)(2,1)S(1)}, u32[]{:S(2)}, u32[]{:S(2)}) collective-permute-start(bf16[2,512,256]{2,1,0:T(8,128)(2,1)S(1)} %get-tuple-element.59.refs_2_.refs_9_), channel_id=1, source_target_pairs={{0,3},{1,0},{2,1},{3,2},{4,7},{5,4},{6,5},{7,6},{8,11},{9,8},{10,9... | collective-permute-start | bytes 1572872 | tf_op jit(solution)/shard_map/ppermute | solution.py:52
  44.2 13.9 %collective-permute-start.10 = (bf16[2,512,256]{2,1,0:T(8,128)(2,1)S(1)}, bf16[2,512,256]{2,1,0:T(8,128)(2,1)S(1)}, u32[]{:S(2)}, u32[]{:S(2)}) collective-permute-start(bf16[2,512,256]{2,1,0:T(8,128)(2,1)S(1)} %get-tuple-element.59.refs_2_.refs_9_), channel_id=1, source_target_pairs={{0,1},{1,2},{2,3},{3,0},{4,5},{5,6},{6,7},{7,4},{8,9},{9,10},{10,1... | collective-permute-start | bytes 1572872 | tf_op jit(solution)/shard_map/ppermute | solution.py:52
  59.7 15.1 %collective-permute-start.13 = (bf16[2,320,512]{2,1,0:T(8,128)(2,1)S(1)}, bf16[2,320,512]{2,1,0:T(8,128)(2,1)S(1)}, u32[]{:S(2)}, u32[]{:S(2)}) collective-permute-start(bf16[2,320,512]{2,1,0:T(8,128)(2,1)S(1)} %get-tuple-element.62), channel_id=1, source_target_pairs={{0,32},{8,104},{16,48},{24,120},{32,64},{40,8},{48,80},{56,24},{64... | collective-permute-start | bytes 1966088 | tf_op jit(solution)/shard_map/ppermute | solution.py:52
  63.5 13.8 %collective-permute-start.12 = (bf16[2,320,512]{2,1,0:T(8,128)(2,1)S(1)}, bf16[2,320,512]{2,1,0:T(8,128)(2,1)S(1)}, u32[]{:S(2)}, u32[]{:S(2)}) collective-permute-start(bf16[2,320,512]{2,1,0:T(8,128)(2,1)S(1)} %get-tuple-element.61), channel_id=1, source_target_pairs={{0,32},{8,104},{16,48},{24,120},{32,64},{40,8},{48,80},{56,24},{64... | collective-permute-start | bytes 1966088 | tf_op jit(solution)/shard_map/ppermute | solution.py:52
  63.6 11.2 %collective-permute-start.14 = (bf16[2,512,256]{2,1,0:T(8,128)(2,1)S(1)}, bf16[2,512,256]{2,1,0:T(8,128)(2,1)S(1)}, u32[]{:S(2)}, u32[]{:S(2)}) collective-permute-start(bf16[2,512,256]{2,1,0:T(8,128)(2,1)S(1)} %get-tuple-element.59.refs_2_.refs_9_), channel_id=1, source_target_pairs={{0,2},{1,3},{2,0},{3,1},{4,6},{5,7},{6,4},{7,5},{8,10},{9,11},{10,... | collective-permute-start | bytes 1572872 | tf_op jit(solution)/shard_map/ppermute | solution.py:52
  78.9 3.7 %collective-permute-start.17 = (bf16[640,256]{1,0:T(8,128)(2,1)S(1)}, bf16[640,256]{1,0:T(8,128)(2,1)S(1)}, u32[]{:S(2)}, u32[]{:S(2)}) collective-permute-start(bf16[640,256]{1,0:T(8,128)(2,1)S(1)} %get-tuple-element.68), channel_id=1, source_target_pairs={{0,8},{8,0},{1,9},{9,1},{2,10},{10,2},{3,11},{11,3},{4,12},{12,4},... | collective-permute-start | bytes 983048 | tf_op jit(solution)/shard_map/ppermute | solution.py:52
  79.0 12.9 %collective-permute-start.19 = (bf16[2,320,512]{2,1,0:T(8,128)(2,1)S(1)}, bf16[2,320,512]{2,1,0:T(8,128)(2,1)S(1)}, u32[]{:S(2)}, u32[]{:S(2)}) collective-permute-start(bf16[2,320,512]{2,1,0:T(8,128)(2,1)S(1)} %get-tuple-element.71), channel_id=1, source_target_pairs={{0,32},{8,104},{16,48},{24,120},{32,64},{40,8},{48,80},{56,24},{64... | collective-permute-start | bytes 1966088 | tf_op jit(solution)/shard_map/ppermute | solution.py:52
  84.1 14.9 %collective-permute-start.18 = (bf16[2,160,1024]{2,1,0:T(8,128)(2,1)S(1)}, bf16[2,160,1024]{2,1,0:T(8,128)(2,1)S(1)}, u32[]{:S(2)}, u32[]{:S(2)}) collective-permute-start(bf16[2,160,1024]{2,1,0:T(8,128)(2,1)S(1)} %get-tuple-element.70), channel_id=1, source_target_pairs={{0,32},{8,104},{16,48},{24,120},{32,64},{40,8},{48,80},{56,24},{64... | collective-permute-start | bytes 1966088 | tf_op jit(solution)/shard_map/ppermute | solution.py:52
  85.8 18.6 %collective-permute-start.15 = (bf16[2,320,512]{2,1,0:T(8,128)(2,1)S(1)}, bf16[2,320,512]{2,1,0:T(8,128)(2,1)S(1)}, u32[]{:S(2)}, u32[]{:S(2)}) collective-permute-start(bf16[2,320,512]{2,1,0:T(8,128)(2,1)S(1)} %get-tuple-element.65.a), channel_id=1, source_target_pairs={{0,16},{16,0},{32,48},{48,32},{64,80},{80,64},{96,112},{112,96},{1... | collective-permute-start | bytes 1966088 | tf_op jit(solution)/shard_map/ppermute | solution.py:52
  100.4 10.7 %collective-permute-start.24 = (bf16[2,160,1024]{2,1,0:T(8,128)(2,1)S(1)}, bf16[2,160,1024]{2,1,0:T(8,128)(2,1)S(1)}, u32[]{:S(2)}, u32[]{:S(2)}) collective-permute-start(bf16[2,160,1024]{2,1,0:T(8,128)(2,1)S(1)} %get-tuple-element.77), channel_id=1, source_target_pairs={{0,32},{8,104},{16,48},{24,120},{32,64},{40,8},{48,80},{56,24},{64... | collective-permute-start | bytes 1966088 | tf_op jit(solution)/shard_map/ppermute | solution.py:52
  103.0 17.0 %collective-permute-start.23 = (bf16[2,320,512]{2,1,0:T(8,128)(2,1)S(1)}, bf16[2,320,512]{2,1,0:T(8,128)(2,1)S(1)}, u32[]{:S(2)}, u32[]{:S(2)}) collective-permute-start(bf16[2,320,512]{2,1,0:T(8,128)(2,1)S(1)} %get-tuple-element.76.a), channel_id=1, source_target_pairs={{0,16},{16,0},{32,48},{48,32},{64,80},{80,64},{96,112},{112,96},{1... | collective-permute-start | bytes 1966088 | tf_op jit(solution)/shard_map/ppermute | solution.py:52
  112.6 11.9 %collective-permute-start.27 = (bf16[2,160,1024]{2,1,0:T(8,128)(2,1)S(1)}, bf16[2,160,1024]{2,1,0:T(8,128)(2,1)S(1)}, u32[]{:S(2)}, u32[]{:S(2)}) collective-permute-start(bf16[2,160,1024]{2,1,0:T(8,128)(2,1)S(1)} %get-tuple-element.81), channel_id=1, source_target_pairs={{0,32},{8,104},{16,48},{24,120},{32,64},{40,8},{48,80},{56,24},{64... | collective-permute-start | bytes 1966088 | tf_op jit(solution)/shard_map/ppermute | solution.py:52
  126.0 8.4 %collective-permute-start.28 = (bf16[160,1024]{1,0:T(8,128)(2,1)S(1)}, bf16[160,1024]{1,0:T(8,128)(2,1)S(1)}, u32[]{:S(2)}, u32[]{:S(2)}) collective-permute-start(bf16[160,1024]{1,0:T(8,128)(2,1)S(1)} %get-tuple-element.83.refs_8_), channel_id=1, source_target_pairs={{0,32},{8,104},{16,48},{24,120},{32,64},{40,8},{48,80},{56,24},{64... | collective-permute-start | bytes 983048 | tf_op jit(solution)/shard_map/ppermute | solution.py:52
  129.8 8.3 %collective-permute-start.20 = (bf16[320,512]{1,0:T(8,128)(2,1)S(1)}, bf16[320,512]{1,0:T(8,128)(2,1)S(1)}, u32[]{:S(2)}, u32[]{:S(2)}) collective-permute-start(bf16[320,512]{1,0:T(8,128)(2,1)S(1)} %get-tuple-element.75.refs_0_), channel_id=1, source_target_pairs={{0,32},{8,104},{16,48},{24,120},{32,64},{40,8},{48,80},{56,24},{64... | collective-permute-start | bytes 983048 | tf_op jit(solution)/shard_map/ppermute | solution.py:52
  129.9 11.7 %collective-permute-start.25 = (bf16[320,512]{1,0:T(8,128)(2,1)S(1)}, bf16[320,512]{1,0:T(8,128)(2,1)S(1)}, u32[]{:S(2)}, u32[]{:S(2)}) collective-permute-start(bf16[320,512]{1,0:T(8,128)(2,1)S(1)} %get-tuple-element.80.refs_4_), channel_id=1, source_target_pairs={{0,32},{8,104},{16,48},{24,120},{32,64},{40,8},{48,80},{56,24},{64... | collective-permute-start | bytes 983048 | tf_op jit(solution)/shard_map/ppermute | solution.py:52
  129.9 15.1 %collective-permute-start.32 = (bf16[160,1024]{1,0:T(8,128)(2,1)S(1)}, bf16[160,1024]{1,0:T(8,128)(2,1)S(1)}, u32[]{:S(2)}, u32[]{:S(2)}) collective-permute-start(bf16[160,1024]{1,0:T(8,128)(2,1)S(1)} %get-tuple-element.83.refs_8_), channel_id=1, source_target_pairs={{0,16},{16,0},{32,48},{48,32},{64,80},{80,64},{96,112},{112,96},{1... | collective-permute-start | bytes 983048 | tf_op jit(solution)/shard_map/ppermute | solution.py:52
  134.4 10.7 %collective-permute-start.31 = (bf16[160,1024]{1,0:T(8,128)(2,1)S(1)}, bf16[160,1024]{1,0:T(8,128)(2,1)S(1)}, u32[]{:S(2)}, u32[]{:S(2)}) collective-permute-start(bf16[160,1024]{1,0:T(8,128)(2,1)S(1)} %collective-permute-done.28.refs_9_), channel_id=1, source_target_pairs={{0,32},{8,104},{16,48},{24,120},{32,64},{40,8},{48,80},{56,24},{64... | collective-permute-start | bytes 983048 | tf_op jit(solution)/shard_map/ppermute | solution.py:52
  138.1 11.1 %collective-permute-start.21 = (bf16[320,512]{1,0:T(8,128)(2,1)S(1)}, bf16[320,512]{1,0:T(8,128)(2,1)S(1)}, u32[]{:S(2)}, u32[]{:S(2)}) collective-permute-start(bf16[320,512]{1,0:T(8,128)(2,1)S(1)} %collective-permute-done.20.refs_1_), channel_id=1, source_target_pairs={{0,32},{8,104},{16,48},{24,120},{32,64},{40,8},{48,80},{56,24},{64... | collective-permute-start | bytes 983048 | tf_op jit(solution)/shard_map/ppermute | solution.py:52
  141.6 10.5 %collective-permute-start.26 = (bf16[320,512]{1,0:T(8,128)(2,1)S(1)}, bf16[320,512]{1,0:T(8,128)(2,1)S(1)}, u32[]{:S(2)}, u32[]{:S(2)}) collective-permute-start(bf16[320,512]{1,0:T(8,128)(2,1)S(1)} %collective-permute-done.25.refs_5_), channel_id=1, source_target_pairs={{0,32},{8,104},{16,48},{24,120},{32,64},{40,8},{48,80},{56,24},{64... | collective-permute-start | bytes 983048 | tf_op jit(solution)/shard_map/ppermute | solution.py:52
  145.1 11.5 %collective-permute-start.29 = (bf16[160,1024]{1,0:T(8,128)(2,1)S(1)}, bf16[160,1024]{1,0:T(8,128)(2,1)S(1)}, u32[]{:S(2)}, u32[]{:S(2)}) collective-permute-start(bf16[160,1024]{1,0:T(8,128)(2,1)S(1)} %collective-permute-done.28.refs_9_), channel_id=1, source_target_pairs={{0,16},{16,0},{32,48},{48,32},{64,80},{80,64},{96,112},{112,96},{1... | collective-permute-start | bytes 983048 | tf_op jit(solution)/shard_map/ppermute | solution.py:52
  145.7 11.5 %collective-permute-start.33 = (bf16[160,1024]{1,0:T(8,128)(2,1)S(1)}, bf16[160,1024]{1,0:T(8,128)(2,1)S(1)}, u32[]{:S(2)}, u32[]{:S(2)}) collective-permute-start(bf16[160,1024]{1,0:T(8,128)(2,1)S(1)} %get-tuple-element.85.refs_10_), channel_id=1, source_target_pairs={{0,32},{8,104},{16,48},{24,120},{32,64},{40,8},{48,80},{56,24},{64... | collective-permute-start | bytes 983048 | tf_op jit(solution)/shard_map/ppermute | solution.py:52
  149.2 9.8 %collective-permute-start.22 = (bf16[320,512]{1,0:T(8,128)(2,1)S(1)}, bf16[320,512]{1,0:T(8,128)(2,1)S(1)}, u32[]{:S(2)}, u32[]{:S(2)}) collective-permute-start(bf16[320,512]{1,0:T(8,128)(2,1)S(1)} %collective-permute-done.21.refs_2_), channel_id=1, source_target_pairs={{0,32},{8,104},{16,48},{24,120},{32,64},{40,8},{48,80},{56,24},{64... | collective-permute-start | bytes 983048 | tf_op jit(solution)/shard_map/ppermute | solution.py:52
  152.1 11.6 %collective-permute-start.34 = (bf16[160,1024]{1,0:T(8,128)(2,1)S(1)}, bf16[160,1024]{1,0:T(8,128)(2,1)S(1)}, u32[]{:S(2)}, u32[]{:S(2)}) collective-permute-start(bf16[160,1024]{1,0:T(8,128)(2,1)S(1)} %get-tuple-element.85.refs_10_), channel_id=1, source_target_pairs={{0,16},{16,0},{32,48},{48,32},{64,80},{80,64},{96,112},{112,96},{1... | collective-permute-start | bytes 983048 | tf_op jit(solution)/shard_map/ppermute | solution.py:52
  157.1 7.1 %collective-permute-start.30 = (bf16[320,512]{1,0:T(8,128)(2,1)S(1)}, bf16[320,512]{1,0:T(8,128)(2,1)S(1)}, u32[]{:S(2)}, u32[]{:S(2)}) collective-permute-start(bf16[320,512]{1,0:T(8,128)(2,1)S(1)} %get-tuple-element.84.refs_6_), channel_id=1, source_target_pairs={{0,32},{8,104},{16,48},{24,120},{32,64},{40,8},{48,80},{56,24},{64... | collective-permute-start | bytes 983048 | tf_op jit(solution)/shard_map/ppermute | solution.py:52
  157.1 10.1 %collective-permute-start.35 = (bf16[160,1024]{1,0:T(8,128)(2,1)S(1)}, bf16[160,1024]{1,0:T(8,128)(2,1)S(1)}, u32[]{:S(2)}, u32[]{:S(2)}) collective-permute-start(bf16[160,1024]{1,0:T(8,128)(2,1)S(1)} %collective-permute-done.33.refs_11_), channel_id=1, source_target_pairs={{0,16},{16,0},{32,48},{48,32},{64,80},{80,64},{96,112},{112,96},{1... | collective-permute-start | bytes 983048 | tf_op jit(solution)/shard_map/ppermute | solution.py:52

commit v5 on v3

--- a/solution.py
+++ b/solution.py
@@ -262,15 +262,15 @@
 
 
 def place_kernel(plan, n_parts, offs, *refs):
-    parts, out, sem = refs[:n_parts], refs[-2], refs[-1]
+    parts, (out, token, sem) = refs[:n_parts], refs[-3:]
+    token[...] = jnp.zeros_like(token)
     copies = []
-    for part, lead, rows, row_at, col_at, nb in plan:
-        src = parts[part] if lead is None else parts[part].at[lead]
+    for part, rows, row_at, col_at, nb in plan:
         row = pl.multiple_of(offs[row_at], 16)
         for j in range(nb):
             col = pl.multiple_of(offs[col_at + j], BLK)
             copy = pltpu.make_async_copy(
-                src.at[:, pl.ds(j * BLK, BLK)], out.at[pl.ds(row, rows), pl.ds(col, BLK)], sem.at[len(copies)]
+                parts[part].at[:, pl.ds(j * BLK, BLK)], out.at[pl.ds(row, rows), pl.ds(col, BLK)], sem.at[len(copies)]
             )
             copy.start()
             copies.append(copy)
@@ -278,16 +278,21 @@
         copy.wait()
 
 
-def place(shape, offs, parts, plan, before):
+def place(shape, offs, pieces, into, before):
+    parts = [piece[0] for piece in pieces]
+    plan = [(n, piece[0].shape[0], *piece[1:]) for n, piece in enumerate(pieces)]
+    operands = [offs, *parts, *before] + ([] if into is None else [into])
+    last = len(operands) - 1
     return pl.pallas_call(
         functools.partial(place_kernel, plan, len(parts)),
-        in_specs=[SMEM] + [VMEM] * (len(parts) + len(before)),
-        out_specs=HBM,
-        out_shape=jax.ShapeDtypeStruct(shape, BF),
+        in_specs=[SMEM] + [VMEM] * (len(parts) + len(before)) + ([] if into is None else [HBM]),
+        out_specs=[HBM, VMEM],
+        out_shape=[jax.ShapeDtypeStruct(shape, BF), TOKEN],
         scratch_shapes=[pltpu.SemaphoreType.DMA((sum(p[-1] for p in plan),))],
+        input_output_aliases={} if into is None else {last: 0},
         compiler_params=pltpu.CompilerParams(vmem_limit_bytes=2**20),
         cost_estimate=FREE,
-    )(offs, *parts, *before)
+    )(*operands)
 
 
 def in_hbm(x):
@@ -390,15 +395,26 @@
     a_all[1].append(onward(a_all[1][1]))
     b_near[2], _ = hold(b_near[2], [b_far[0]])
     b_near.append(onward(b_near[2]))
-    a_all[1][2], _ = hold(a_all[1][2], [b_far[1]])
+
+    def a_place(p, k):
+        return a_all[p][k], BACK + k, NEAR + 2 * p, 2
+
+    def b_place(k):
+        return b_near[k], BACK_HERE + k, FAR, 4
+
+    def b_place_far(k):
+        return b_far[k], BACK_AWAY + k, FAR, 4
+
+    shape = (width, wide)
+    first = [a_place(0, 0), a_place(0, 1), a_place(1, 0), a_place(1, 1), b_place(0), b_place(1), b_place(2), b_place_far(0)]
+    begun, done = place(shape, offs, first, None, [])
+    a_all[1][2], _ = hold(a_all[1][2], [b_far[1], done])
     a_all[1].append(onward(a_all[1][2]))
     b_far += [move(piece, Z_SWAP) for piece in b_near[2:]]
 
-    plan = []
-    for k in range(4):
-        plan += [(4 * p + k, None, quarter, BACK + k, NEAR + 2 * p, 2) for p in range(2)]
-        plan += [(8 + k, None, part, BACK_HERE + k, FAR, 4), (12 + k, None, part, BACK_AWAY + k, FAR, 4)]
-    return place((width, wide), offs, [*a_all[0], *a_all[1], *b_near, *b_far], plan, [token])
+    rest = [a_place(0, 2), a_place(0, 3), a_place(1, 2), a_place(1, 3), b_place(3)]
+    rest += [b_place_far(k) for k in (1, 2, 3)]
+    return place(shape, offs, rest, begun, [])[0]
 
 
 def solution(mesh):

time: 159 us -> 159 us (level)
  waiting for transfers between devices: 65.9 us -> 63.6 us
  Pallas kernels: 35.1 us -> 37.3 us
    ppermute x36, waiting for transfers between devices: 65.9 us -> 63.6 us  [move(): return lax.ppermute(x, axis, perm)]
    pallas_call x1 -> x2, Pallas kernels: 3.27 us -> 5.04 us  [place(): pl.pallas_call(functools.partial(place_kernel, plan, len(parts)), in_spec...]
  transfers between devices with their start and end apart: 36 -> 36, of which waited for: 19 -> 19; matrix products, arithmetic and copies ran while one was open for 0% -> 0% of each run, Pallas kernels for 17% -> 19%
where the time goes in v5:
time: 159 us
  waiting for transfers between devices  63.6 us (40%)
  starting transfers between devices  57.4 us (36%)
  Pallas kernels  37.3 us (23%)
    ppermute x36, waiting for transfers between devices, move(): return lax.ppermute(x, axis, perm)  63.6 us
    ppermute x36, starting transfers between devices, move(): return lax.ppermute(x, axis, perm)  57.4 us
    pallas_call x12, Pallas kernels, terms(): pl.pallas_call(functools.partial(term_kernel, rows, nb, [s[5] for s in so...  18.9 us
    pallas_call x1, Pallas kernels, project(): pl.pallas_call(functools.partial(project_kernel, step), in_specs=[SMEM] +...  10.5 us
    pallas_call x2, Pallas kernels, place(): pl.pallas_call(functools.partial(place_kernel, plan, len(parts)), in_spec...  5.04 us
  transfers between devices with their start and end apart: 36, of which 19 were waited for; matrix products, arithmetic and copies ran while one was open for 0% of the time, Pallas kernels for 19%

profile of v5, /device:TPU:56, one launch (start us, length us, event | category | flops | bytes accessed | tf_op | source)
XLA Modules:
  0.0 158.9 jit_solution(5583322811622671260)
XLA Ops:
  0.0 3.0 %collective-permute-start.4 = (bf16[512,256]{1,0:T(8,128)(2,1)}, bf16[512,256]{1,0:T(8,128)(2,1)S(1)}, u32[]{:S(2)}, u32[]{:S(2)}) collective-permute-start(bf16[512,256]{1,0:T(8,128)(2,1)} %bitcast.51), channel_id=1, source_target_pairs={{0,2},{1,3},{2,0},{3,1},{4,6},{5,7},{6,4},{7,5},{8,10},{9,11},{10,... | collective-permute-start | bytes 786440 | tf_op jit(solution)/shard_map/ppermute | solution.py:52
  5.1 1.9 %collective-permute-start.1 = (bf16[512,256]{1,0:T(8,128)(2,1)}, bf16[512,256]{1,0:T(8,128)(2,1)S(1)}, u32[]{:S(2)}, u32[]{:S(2)}) collective-permute-start(bf16[512,256]{1,0:T(8,128)(2,1)} %bitcast.54), channel_id=1, source_target_pairs={{0,20},{1,21},{2,22},{3,23},{4,16},{5,17},{6,18},{7,19},{16,4},{17... | collective-permute-start | bytes 786440 | tf_op jit(solution)/shard_map/ppermute | solution.py:52
  7.0 2.2 %collective-permute-start = (bf16[512,256]{1,0:T(8,128)(2,1)}, bf16[512,256]{1,0:T(8,128)(2,1)S(1)}, u32[]{:S(2)}, u32[]{:S(2)}) collective-permute-start(bf16[512,256]{1,0:T(8,128)(2,1)} %bitcast.55), channel_id=1, source_target_pairs={{0,4},{1,5},{2,6},{3,7},{4,0},{5,1},{6,2},{7,3},{8,12},{9,13},{10,... | collective-permute-start | bytes 786440 | tf_op jit(solution)/shard_map/ppermute | solution.py:52
  9.3 10.5 %shard_map.55 = (f32[2,256,1280]{2,1,0:T(8,128)S(1)}, bf16[2,256,1280]{2,1,0:T(8,128)(2,1)S(1)}, f32[8,128]{1,0:T(8,128)S(1)}) custom-call(s32[39]{0:T(128)S(1)} %stack.135.offs, bf16[512,2048]{1,0:T(8,128)(2,1)} %bitcast.62, bf16[2048,1280]{1,0:T(8,128)(2,1)} %bitcast.60, bf16[2048,1280]{1,0:T(8,128)(2,1)} %bitcast.61), custom_call_target="tpu_custom_call" | custom-call | tf_op jit(solution)/shard_map/pallas_call | solution.py:95
  20.0 3.0 %collective-permute-done.5.recv_ref = bf16[2,256,1280]{2,1,0:T(8,128)(2,1)S(1)} collective-permute-done((bf16[2,256,1280]{2,1,0:T(8,128)(2,1)S(1)}, bf16[2,256,1280]{2,1,0:T(8,128)(2,1)S(1)}, u32[]{:S(2)}, u32[]{:S(2)}) %collective-permute-start.5) | collective-permute-done | bytes 1310752 | tf_op jit(solution)/shard_map/ppermute | solution.py:52
  24.6 2.0 %collective-permute-done.6.refs_1_ = bf16[1280,256]{1,0:T(8,128)(2,1)S(1)} collective-permute-done((bf16[1280,256]{1,0:T(8,128)(2,1)S(1)}, bf16[1280,256]{1,0:T(8,128)(2,1)S(1)}, u32[]{:S(2)}, u32[]{:S(2)}) %collective-permute-start.6) | collective-permute-done | bytes 655392 | tf_op jit(solution)/shard_map/ppermute | solution.py:52
  26.6 1.5 shard_map.58
  28.4 1.5 shard_map.59
  29.9 1.6 %collective-permute-start.9 = (bf16[2,320,512]{2,1,0:T(8,128)(2,1)S(1)}, bf16[2,320,512]{2,1,0:T(8,128)(2,1)S(1)}, u32[]{:S(2)}, u32[]{:S(2)}) collective-permute-start(bf16[2,320,512]{2,1,0:T(8,128)(2,1)S(1)} %get-tuple-element.59), channel_id=1, source_target_pairs={{0,32},{8,104},{16,48},{24,120},{32,64},{40,8},{48,80},{56,24},{64... | collective-permute-start | bytes 1966088 | tf_op jit(solution)/shard_map/ppermute | solution.py:52
  31.5 2.3 %collective-permute-start.11 = (bf16[2,512,256]{2,1,0:T(8,128)(2,1)S(1)}, bf16[2,512,256]{2,1,0:T(8,128)(2,1)S(1)}, u32[]{:S(2)}, u32[]{:S(2)}) collective-permute-start(bf16[2,512,256]{2,1,0:T(8,128)(2,1)S(1)} %get-tuple-element.61.refs_2_.refs_9_), channel_id=1, source_target_pairs={{0,3},{1,0},{2,1},{3,2},{4,7},{5,4},{6,5},{7,6},{8,11},{9,8},{10,9... | collective-permute-start | bytes 1572872 | tf_op jit(solution)/shard_map/ppermute | solution.py:52
  33.9 4.8 %collective-permute-done.7.refs_5_ = bf16[2,320,512]{2,1,0:T(8,128)(2,1)S(1)} collective-permute-done((bf16[2,320,512]{2,1,0:T(8,128)(2,1)S(1)}, bf16[2,320,512]{2,1,0:T(8,128)(2,1)S(1)}, u32[]{:S(2)}, u32[]{:S(2)}) %collective-permute-start.7) | collective-permute-done | bytes 655392 | tf_op jit(solution)/shard_map/ppermute | solution.py:52
  38.7 1.6 shard_map.60
  40.3 1.5 collective-permute-start.8
  41.8 2.5 %collective-permute-done.11.refs_8_.refs_5_.refs_12_ = bf16[2,512,256]{2,1,0:T(8,128)(2,1)S(1)} collective-permute-done((bf16[2,512,256]{2,1,0:T(8,128)(2,1)S(1)}, bf16[2,512,256]{2,1,0:T(8,128)(2,1)S(1)}, u32[]{:S(2)}, u32[]{:S(2)}) %collective-permute-start.11) | collective-permute-done | bytes 524320 | tf_op jit(solution)/shard_map/ppermute | solution.py:52
  44.3 3.3 %collective-permute-done.10.refs_7_.refs_3_.refs_10_ = bf16[2,512,256]{2,1,0:T(8,128)(2,1)S(1)} collective-permute-done((bf16[2,512,256]{2,1,0:T(8,128)(2,1)S(1)}, bf16[2,512,256]{2,1,0:T(8,128)(2,1)S(1)}, u32[]{:S(2)}, u32[]{:S(2)}) %collective-permute-start.10) | collective-permute-done | bytes 524320 | tf_op jit(solution)/shard_map/ppermute | solution.py:52
  47.6 1.6 shard_map.61
  49.2 2.9 %collective-permute-start.14 = (bf16[2,320,512]{2,1,0:T(8,128)(2,1)S(1)}, bf16[2,320,512]{2,1,0:T(8,128)(2,1)S(1)}, u32[]{:S(2)}, u32[]{:S(2)}) collective-permute-start(bf16[2,320,512]{2,1,0:T(8,128)(2,1)S(1)} %get-tuple-element.65), channel_id=1, source_target_pairs={{0,32},{8,104},{16,48},{24,120},{32,64},{40,8},{48,80},{56,24},{64... | collective-permute-start | bytes 1966088 | tf_op jit(solution)/shard_map/ppermute | solution.py:52
  52.8 1.6 shard_map.62
  54.3 1.5 collective-permute-start.12
  55.8 7.5 %collective-permute-done.15.refs_7_.refs_4_.refs_11_ = bf16[2,512,256]{2,1,0:T(8,128)(2,1)S(1)} collective-permute-done((bf16[2,512,256]{2,1,0:T(8,128)(2,1)S(1)}, bf16[2,512,256]{2,1,0:T(8,128)(2,1)S(1)}, u32[]{:S(2)}, u32[]{:S(2)}) %collective-permute-start.15) | collective-permute-done | bytes 524320 | tf_op jit(solution)/shard_map/ppermute | solution.py:52
  63.3 1.6 shard_map.63
  64.9 3.1 %collective-permute-done.13.a_ref.refs_7_.refs_13_ = bf16[640,1280]{1,0:T(8,128)(2,1)S(1)} collective-permute-done((bf16[640,1280]{1,0:T(8,128)(2,1)S(1)}, bf16[640,1280]{1,0:T(8,128)(2,1)S(1)}, u32[]{:S(2)}, u32[]{:S(2)}) %collective-permute-start.13) | collective-permute-done | bytes 1638432 | tf_op jit(solution)/shard_map/ppermute | solution.py:52
  68.1 2.3 %collective-permute-start.19 = (bf16[2,320,512]{2,1,0:T(8,128)(2,1)S(1)}, bf16[2,320,512]{2,1,0:T(8,128)(2,1)S(1)}, u32[]{:S(2)}, u32[]{:S(2)}) collective-permute-start(bf16[2,320,512]{2,1,0:T(8,128)(2,1)S(1)} %get-tuple-element.73), channel_id=1, source_target_pairs={{0,32},{8,104},{16,48},{24,120},{32,64},{40,8},{48,80},{56,24},{64... | collective-permute-start | bytes 1966088 | tf_op jit(solution)/shard_map/ppermute | solution.py:52
  70.4 1.6 shard_map.65
  74.0 3.3 %collective-permute-start.16 = (bf16[2,320,512]{2,1,0:T(8,128)(2,1)S(1)}, bf16[2,320,512]{2,1,0:T(8,128)(2,1)S(1)}, u32[]{:S(2)}, u32[]{:S(2)}) collective-permute-start(bf16[2,320,512]{2,1,0:T(8,128)(2,1)S(1)} %get-tuple-element.69.a), channel_id=1, source_target_pairs={{0,16},{16,0},{32,48},{48,32},{64,80},{80,64},{96,112},{112,96},{1... | collective-permute-start | bytes 1966088 | tf_op jit(solution)/shard_map/ppermute | solution.py:52
  77.2 1.5 collective-permute-done.19.refs_5_
  78.7 1.6 shard_map.67
  80.3 5.5 %collective-permute-done.18.refs_14_ = bf16[2,160,1024]{2,1,0:T(8,128)(2,1)S(1)} collective-permute-done((bf16[2,160,1024]{2,1,0:T(8,128)(2,1)S(1)}, bf16[2,160,1024]{2,1,0:T(8,128)(2,1)S(1)}, u32[]{:S(2)}, u32[]{:S(2)}) %collective-permute-start.18) | collective-permute-done | bytes 655392 | tf_op jit(solution)/shard_map/ppermute | solution.py:52
  85.8 1.5 shard_map.68
  87.3 3.5 %collective-permute-start.24 = (bf16[2,160,1024]{2,1,0:T(8,128)(2,1)S(1)}, bf16[2,160,1024]{2,1,0:T(8,128)(2,1)S(1)}, u32[]{:S(2)}, u32[]{:S(2)}) collective-permute-start(bf16[2,160,1024]{2,1,0:T(8,128)(2,1)S(1)} %get-tuple-element.79), channel_id=1, source_target_pairs={{0,32},{8,104},{16,48},{24,120},{32,64},{40,8},{48,80},{56,24},{64... | collective-permute-start | bytes 1966088 | tf_op jit(solution)/shard_map/ppermute | solution.py:52
  91.8 7.0 %collective-permute-done.24.refs_14_ = bf16[2,160,1024]{2,1,0:T(8,128)(2,1)S(1)} collective-permute-done((bf16[2,160,1024]{2,1,0:T(8,128)(2,1)S(1)}, bf16[2,160,1024]{2,1,0:T(8,128)(2,1)S(1)}, u32[]{:S(2)}, u32[]{:S(2)}) %collective-permute-start.24) | collective-permute-done | bytes 655392 | tf_op jit(solution)/shard_map/ppermute | solution.py:52
  98.9 1.5 shard_map.70
  100.4 3.8 %collective-permute-start.27 = (bf16[2,160,1024]{2,1,0:T(8,128)(2,1)S(1)}, bf16[2,160,1024]{2,1,0:T(8,128)(2,1)S(1)}, u32[]{:S(2)}, u32[]{:S(2)}) collective-permute-start(bf16[2,160,1024]{2,1,0:T(8,128)(2,1)S(1)} %get-tuple-element.83), channel_id=1, source_target_pairs={{0,32},{8,104},{16,48},{24,120},{32,64},{40,8},{48,80},{56,24},{64... | collective-permute-start | bytes 1966088 | tf_op jit(solution)/shard_map/ppermute | solution.py:52
  104.1 2.1 %collective-permute-done.23.b = bf16[2,320,512]{2,1,0:T(8,128)(2,1)S(1)} collective-permute-done((bf16[2,320,512]{2,1,0:T(8,128)(2,1)S(1)}, bf16[2,320,512]{2,1,0:T(8,128)(2,1)S(1)}, u32[]{:S(2)}, u32[]{:S(2)}) %collective-permute-start.23) | collective-permute-done | bytes 655392 | tf_op jit(solution)/shard_map/ppermute | solution.py:52
  106.4 5.8 %collective-permute-done.27.refs_14_ = bf16[2,160,1024]{2,1,0:T(8,128)(2,1)S(1)} collective-permute-done((bf16[2,160,1024]{2,1,0:T(8,128)(2,1)S(1)}, bf16[2,160,1024]{2,1,0:T(8,128)(2,1)S(1)}, u32[]{:S(2)}, u32[]{:S(2)}) %collective-permute-start.27) | collective-permute-done | bytes 655392 | tf_op jit(solution)/shard_map/ppermute | solution.py:52
  112.2 2.0 %shard_map.72 = (bf16[160,1024]{1,0:T(8,128)(2,1)S(1)}, f32[8,128]{1,0:T(8,128)}) custom-call(s32[39]{0:T(128)S(1)} %stack.135.offs, bf16[1280,256]{1,0:T(8,128)(2,1)S(1)} %get-tuple-element.53.refs_0_, bf16[1280,256]{1,0:T(8,128)(2,1)S(1)} %collective-permute-done.6.refs_1_, bf16[2,512,256]{2,1,0:T(8,128)(2,1)S(1)} %get-tuple-element.61.refs_2_.refs_9_, ...), custom_call_target="tpu_custom_call" | custom-call | tf_op jit(solution)/shard_map/pallas_call | solution.py:236
  114.3 3.7 %collective-permute-start.28 = (bf16[160,1024]{1,0:T(8,128)(2,1)S(1)}, bf16[160,1024]{1,0:T(8,128)(2,1)S(1)}, u32[]{:S(2)}, u32[]{:S(2)}) collective-permute-start(bf16[160,1024]{1,0:T(8,128)(2,1)S(1)} %get-tuple-element.85.refs_4_), channel_id=1, source_target_pairs={{0,32},{8,104},{16,48},{24,120},{32,64},{40,8},{48,80},{56,24},{64... | collective-permute-start | bytes 983048 | tf_op jit(solution)/shard_map/ppermute | solution.py:52
  118.9 3.7 %collective-permute-done.28.refs_5_ = bf16[160,1024]{1,0:T(8,128)(2,1)S(1)} collective-permute-done((bf16[160,1024]{1,0:T(8,128)(2,1)S(1)}, bf16[160,1024]{1,0:T(8,128)(2,1)S(1)}, u32[]{:S(2)}, u32[]{:S(2)}) %collective-permute-start.28) | collective-permute-done | bytes 327712 | tf_op jit(solution)/shard_map/ppermute | solution.py:52
  122.6 3.7 %collective-permute-start.30 = (bf16[160,1024]{1,0:T(8,128)(2,1)S(1)}, bf16[160,1024]{1,0:T(8,128)(2,1)S(1)}, u32[]{:S(2)}, u32[]{:S(2)}) collective-permute-start(bf16[160,1024]{1,0:T(8,128)(2,1)S(1)} %collective-permute-done.28.refs_5_), channel_id=1, source_target_pairs={{0,32},{8,104},{16,48},{24,120},{32,64},{40,8},{48,80},{56,24},{64... | collective-permute-start | bytes 983048 | tf_op jit(solution)/shard_map/ppermute | solution.py:52
  126.2 3.5 %collective-permute-start.21 = (bf16[320,512]{1,0:T(8,128)(2,1)S(1)}, bf16[320,512]{1,0:T(8,128)(2,1)S(1)}, u32[]{:S(2)}, u32[]{:S(2)}) collective-permute-start(bf16[320,512]{1,0:T(8,128)(2,1)S(1)} %collective-permute-done.20.refs_1_), channel_id=1, source_target_pairs={{0,32},{8,104},{16,48},{24,120},{32,64},{40,8},{48,80},{56,24},{64... | collective-permute-start | bytes 983048 | tf_op jit(solution)/shard_map/ppermute | solution.py:52
  129.8 3.5 %collective-permute-start.26 = (bf16[320,512]{1,0:T(8,128)(2,1)S(1)}, bf16[320,512]{1,0:T(8,128)(2,1)S(1)}, u32[]{:S(2)}, u32[]{:S(2)}) collective-permute-start(bf16[320,512]{1,0:T(8,128)(2,1)S(1)} %collective-permute-done.25.refs_3_), channel_id=1, source_target_pairs={{0,32},{8,104},{16,48},{24,120},{32,64},{40,8},{48,80},{56,24},{64... | collective-permute-start | bytes 983048 | tf_op jit(solution)/shard_map/ppermute | solution.py:52
  134.7 2.6 %collective-permute-start.33 = (bf16[160,1024]{1,0:T(8,128)(2,1)S(1)}, bf16[160,1024]{1,0:T(8,128)(2,1)S(1)}, u32[]{:S(2)}, u32[]{:S(2)}) collective-permute-start(bf16[160,1024]{1,0:T(8,128)(2,1)S(1)} %get-tuple-element.86.refs_6_), channel_id=1, source_target_pairs={{0,32},{8,104},{16,48},{24,120},{32,64},{40,8},{48,80},{56,24},{64... | collective-permute-start | bytes 983048 | tf_op jit(solution)/shard_map/ppermute | solution.py:52
  137.4 2.9 %collective-permute-start.22 = (bf16[320,512]{1,0:T(8,128)(2,1)S(1)}, bf16[320,512]{1,0:T(8,128)(2,1)S(1)}, u32[]{:S(2)}, u32[]{:S(2)}) collective-permute-start(bf16[320,512]{1,0:T(8,128)(2,1)S(1)} %collective-permute-done.21.refs_0_), channel_id=1, source_target_pairs={{0,32},{8,104},{16,48},{24,120},{32,64},{40,8},{48,80},{56,24},{64... | collective-permute-start | bytes 983048 | tf_op jit(solution)/shard_map/ppermute | solution.py:52
  141.2 2.2 %shard_map.74 = (bf16[1280,2048]{1,0:T(8,128)(2,1)}, f32[8,128]{1,0:T(8,128)S(1)}) custom-call(s32[39]{0:T(128)S(1)} %stack.135.offs, bf16[320,512]{1,0:T(8,128)(2,1)S(1)} %get-tuple-element.77.refs_0_, bf16[320,512]{1,0:T(8,128)(2,1)S(1)} %collective-permute-done.20.refs_1_, bf16[320,512]{1,0:T(8,128)(2,1)S(1)} %get-tuple-element.82.refs_2_, ...), custom_call_target="tpu_custom_call" | custom-call | tf_op jit(solution)/shard_map/pallas_call | solution.py:286
  143.4 1.9 %collective-permute-done.29.refs_1_.refs_5_ = bf16[160,1024]{1,0:T(8,128)(2,1)S(1)} collective-permute-done((bf16[160,1024]{1,0:T(8,128)(2,1)S(1)}, bf16[160,1024]{1,0:T(8,128)(2,1)S(1)}, u32[]{:S(2)}, u32[]{:S(2)}) %collective-permute-start.29) | collective-permute-done | bytes 327712 | tf_op jit(solution)/shard_map/ppermute | solution.py:52
  147.1 5.2 %collective-permute-done.34.refs_6_ = bf16[160,1024]{1,0:T(8,128)(2,1)S(1)} collective-permute-done((bf16[160,1024]{1,0:T(8,128)(2,1)S(1)}, bf16[160,1024]{1,0:T(8,128)(2,1)S(1)}, u32[]{:S(2)}, u32[]{:S(2)}) %collective-permute-start.34) | collective-permute-done | bytes 327712 | tf_op jit(solution)/shard_map/ppermute | solution.py:52
  153.0 2.9 %collective-permute-done.35.refs_7_ = bf16[160,1024]{1,0:T(8,128)(2,1)S(1)} collective-permute-done((bf16[160,1024]{1,0:T(8,128)(2,1)S(1)}, bf16[160,1024]{1,0:T(8,128)(2,1)S(1)}, u32[]{:S(2)}, u32[]{:S(2)}) %collective-permute-start.35) | collective-permute-done | bytes 327712 | tf_op jit(solution)/shard_map/ppermute | solution.py:52
  155.9 2.8 %shard_map.76 = (bf16[1280,2048]{1,0:T(8,128)(2,1)}, f32[8,128]{1,0:T(8,128)}) custom-call(s32[39]{0:T(128)S(1)} %stack.135.offs, bf16[320,512]{1,0:T(8,128)(2,1)S(1)} %collective-permute-done.21.refs_0_, bf16[320,512]{1,0:T(8,128)(2,1)S(1)} %collective-permute-done.22.refs_1_, ...), custom_call_target="tpu_custom_call", output_to_operand_aliasing={{0}: (9, {})} | custom-call | tf_op jit(solution)/shard_map/pallas_call | solution.py:286
  (54 shorter events, 14.0 us)
Async XLA Ops:
  0.0 19.8 %collective-permute-start.4 = (bf16[512,256]{1,0:T(8,128)(2,1)}, bf16[512,256]{1,0:T(8,128)(2,1)S(1)}, u32[]{:S(2)}, u32[]{:S(2)}) collective-permute-start(bf16[512,256]{1,0:T(8,128)(2,1)} %bitcast.51), channel_id=1, source_target_pairs={{0,2},{1,3},{2,0},{3,1},{4,6},{5,7},{6,4},{7,5},{8,10},{9,11},{10,... | collective-permute-start | bytes 786440 | tf_op jit(solution)/shard_map/ppermute | solution.py:52
  3.0 16.8 %collective-permute-start.3 = (bf16[512,256]{1,0:T(8,128)(2,1)}, bf16[512,256]{1,0:T(8,128)(2,1)S(1)}, u32[]{:S(2)}, u32[]{:S(2)}) collective-permute-start(bf16[512,256]{1,0:T(8,128)(2,1)} %bitcast.52), channel_id=1, source_target_pairs={{0,3},{1,0},{2,1},{3,2},{4,7},{5,4},{6,5},{7,6},{8,11},{9,8},{10,9... | collective-permute-start | bytes 786440 | tf_op jit(solution)/shard_map/ppermute | solution.py:52
  4.2 15.7 %collective-permute-start.2 = (bf16[512,256]{1,0:T(8,128)(2,1)}, bf16[512,256]{1,0:T(8,128)(2,1)S(1)}, u32[]{:S(2)}, u32[]{:S(2)}) collective-permute-start(bf16[512,256]{1,0:T(8,128)(2,1)} %bitcast.53), channel_id=1, source_target_pairs={{0,1},{1,2},{2,3},{3,0},{4,5},{5,6},{6,7},{7,4},{8,9},{9,10},{10,1... | collective-permute-start | bytes 786440 | tf_op jit(solution)/shard_map/ppermute | solution.py:52
  5.1 14.8 %collective-permute-start.1 = (bf16[512,256]{1,0:T(8,128)(2,1)}, bf16[512,256]{1,0:T(8,128)(2,1)S(1)}, u32[]{:S(2)}, u32[]{:S(2)}) collective-permute-start(bf16[512,256]{1,0:T(8,128)(2,1)} %bitcast.54), channel_id=1, source_target_pairs={{0,20},{1,21},{2,22},{3,23},{4,16},{5,17},{6,18},{7,19},{16,4},{17... | collective-permute-start | bytes 786440 | tf_op jit(solution)/shard_map/ppermute | solution.py:52
  7.0 12.9 %collective-permute-start = (bf16[512,256]{1,0:T(8,128)(2,1)}, bf16[512,256]{1,0:T(8,128)(2,1)S(1)}, u32[]{:S(2)}, u32[]{:S(2)}) collective-permute-start(bf16[512,256]{1,0:T(8,128)(2,1)} %bitcast.55), channel_id=1, source_target_pairs={{0,4},{1,5},{2,6},{3,7},{4,0},{5,1},{6,2},{7,3},{8,12},{9,13},{10,... | collective-permute-start | bytes 786440 | tf_op jit(solution)/shard_map/ppermute | solution.py:52
  9.3 13.7 %slice-start = ((s8[5242880]{0:T(1024)(128)(4,1)}), s8[4194304]{0:T(1024)(128)(4,1)S(1)}, s32[]{:S(2)}) async-start(s8[5242880]{0:T(1024)(128)(4,1)} %bitcast.36), calls=%async_computation | async-start | bytes 8388608
  9.3 13.7 %slice-start.1 = ((s8[5242880]{0:T(1024)(128)(4,1)}), s8[1048576]{0:T(1024)(128)(4,1)S(1)}, s32[]{:S(2)}) async-start(s8[5242880]{0:T(1024)(128)(4,1)} %bitcast.36), calls=%async_computation.1 | async-start | bytes 2097152
  19.9 3.1 %collective-permute-start.5 = (bf16[2,256,1280]{2,1,0:T(8,128)(2,1)S(1)}, bf16[2,256,1280]{2,1,0:T(8,128)(2,1)S(1)}, u32[]{:S(2)}, u32[]{:S(2)}) collective-permute-start(bf16[2,256,1280]{2,1,0:T(8,128)(2,1)S(1)} %get-tuple-element.51), channel_id=1, source_target_pairs={{0,8},{8,0},{1,9},{9,1},{2,10},{10,2},{3,11},{11,3},{4,12},{12,4},... | collective-permute-start | bytes 3932168 | tf_op jit(solution)/shard_map/ppermute | solution.py:52
  23.0 3.5 %copy-start = (bf16[1,512,256]{2,1,0:T(8,128)(2,1)S(1)}, bf16[1,512,256]{2,1,0:T(8,128)(2,1)}, u32[]{:S(2)}) copy-start(bf16[1,512,256]{2,1,0:T(8,128)(2,1)} %param.8) | copy-start | bytes 786436
  24.4 2.2 %collective-permute-start.6 = (bf16[1280,256]{1,0:T(8,128)(2,1)S(1)}, bf16[1280,256]{1,0:T(8,128)(2,1)S(1)}, u32[]{:S(2)}, u32[]{:S(2)}) collective-permute-start(bf16[1280,256]{1,0:T(8,128)(2,1)S(1)} %get-tuple-element.53.refs_0_), channel_id=1, source_target_pairs={{0,8},{8,0},{1,9},{9,1},{2,10},{10,2},{3,11},{11,3},{4,12},{12,4},... | collective-permute-start | bytes 1966088 | tf_op jit(solution)/shard_map/ppermute | solution.py:52
  28.1 10.7 %collective-permute-start.7 = (bf16[2,320,512]{2,1,0:T(8,128)(2,1)S(1)}, bf16[2,320,512]{2,1,0:T(8,128)(2,1)S(1)}, u32[]{:S(2)}, u32[]{:S(2)}) collective-permute-start(bf16[2,320,512]{2,1,0:T(8,128)(2,1)S(1)} %get-tuple-element.55), channel_id=1, source_target_pairs={{0,32},{8,104},{16,48},{24,120},{32,64},{40,8},{48,80},{56,24},{64... | collective-permute-start | bytes 1966088 | tf_op jit(solution)/shard_map/ppermute | solution.py:52
  28.4 39.6 %collective-permute-start.13 = (bf16[640,1280]{1,0:T(8,128)(2,1)S(1)}, bf16[640,1280]{1,0:T(8,128)(2,1)S(1)}, u32[]{:S(2)}, u32[]{:S(2)}) collective-permute-start(bf16[640,1280]{1,0:T(8,128)(2,1)S(1)} %get-tuple-element.64), channel_id=1, source_target_pairs={{0,16},{16,0},{32,48},{48,32},{64,80},{80,64},{96,112},{112,96},{1... | collective-permute-start | bytes 4915208 | tf_op jit(solution)/shard_map/ppermute | solution.py:52
  29.9 17.7 %collective-permute-start.9 = (bf16[2,320,512]{2,1,0:T(8,128)(2,1)S(1)}, bf16[2,320,512]{2,1,0:T(8,128)(2,1)S(1)}, u32[]{:S(2)}, u32[]{:S(2)}) collective-permute-start(bf16[2,320,512]{2,1,0:T(8,128)(2,1)S(1)} %get-tuple-element.59), channel_id=1, source_target_pairs={{0,32},{8,104},{16,48},{24,120},{32,64},{40,8},{48,80},{56,24},{64... | collective-permute-start | bytes 1966088 | tf_op jit(solution)/shard_map/ppermute | solution.py:52
  31.5 12.8 %collective-permute-start.11 = (bf16[2,512,256]{2,1,0:T(8,128)(2,1)S(1)}, bf16[2,512,256]{2,1,0:T(8,128)(2,1)S(1)}, u32[]{:S(2)}, u32[]{:S(2)}) collective-permute-start(bf16[2,512,256]{2,1,0:T(8,128)(2,1)S(1)} %get-tuple-element.61.refs_2_.refs_9_), channel_id=1, source_target_pairs={{0,3},{1,0},{2,1},{3,2},{4,7},{5,4},{6,5},{7,6},{8,11},{9,8},{10,9... | collective-permute-start | bytes 1572872 | tf_op jit(solution)/shard_map/ppermute | solution.py:52
  33.9 13.7 %collective-permute-start.10 = (bf16[2,512,256]{2,1,0:T(8,128)(2,1)S(1)}, bf16[2,512,256]{2,1,0:T(8,128)(2,1)S(1)}, u32[]{:S(2)}, u32[]{:S(2)}) collective-permute-start(bf16[2,512,256]{2,1,0:T(8,128)(2,1)S(1)} %get-tuple-element.61.refs_2_.refs_9_), channel_id=1, source_target_pairs={{0,1},{1,2},{2,3},{3,0},{4,5},{5,6},{6,7},{7,4},{8,9},{9,10},{10,1... | collective-permute-start | bytes 1572872 | tf_op jit(solution)/shard_map/ppermute | solution.py:52
  40.3 12.5 %collective-permute-start.8 = (bf16[2,320,512]{2,1,0:T(8,128)(2,1)S(1)}, bf16[2,320,512]{2,1,0:T(8,128)(2,1)S(1)}, u32[]{:S(2)}, u32[]{:S(2)}) collective-permute-start(bf16[2,320,512]{2,1,0:T(8,128)(2,1)S(1)} %get-tuple-element.58), channel_id=1, source_target_pairs={{0,32},{8,104},{16,48},{24,120},{32,64},{40,8},{48,80},{56,24},{64... | collective-permute-start | bytes 1966088 | tf_op jit(solution)/shard_map/ppermute | solution.py:52
  49.2 14.1 %collective-permute-start.14 = (bf16[2,320,512]{2,1,0:T(8,128)(2,1)S(1)}, bf16[2,320,512]{2,1,0:T(8,128)(2,1)S(1)}, u32[]{:S(2)}, u32[]{:S(2)}) collective-permute-start(bf16[2,320,512]{2,1,0:T(8,128)(2,1)S(1)} %get-tuple-element.65), channel_id=1, source_target_pairs={{0,32},{8,104},{16,48},{24,120},{32,64},{40,8},{48,80},{56,24},{64... | collective-permute-start | bytes 1966088 | tf_op jit(solution)/shard_map/ppermute | solution.py:52
  52.0 11.3 %collective-permute-start.15 = (bf16[2,512,256]{2,1,0:T(8,128)(2,1)S(1)}, bf16[2,512,256]{2,1,0:T(8,128)(2,1)S(1)}, u32[]{:S(2)}, u32[]{:S(2)}) collective-permute-start(bf16[2,512,256]{2,1,0:T(8,128)(2,1)S(1)} %get-tuple-element.61.refs_2_.refs_9_), channel_id=1, source_target_pairs={{0,2},{1,3},{2,0},{3,1},{4,6},{5,7},{6,4},{7,5},{8,10},{9,11},{10,... | collective-permute-start | bytes 1572872 | tf_op jit(solution)/shard_map/ppermute | solution.py:52
  54.3 16.0 %collective-permute-start.12 = (bf16[2,320,512]{2,1,0:T(8,128)(2,1)S(1)}, bf16[2,320,512]{2,1,0:T(8,128)(2,1)S(1)}, u32[]{:S(2)}, u32[]{:S(2)}) collective-permute-start(bf16[2,320,512]{2,1,0:T(8,128)(2,1)S(1)} %get-tuple-element.63), channel_id=1, source_target_pairs={{0,32},{8,104},{16,48},{24,120},{32,64},{40,8},{48,80},{56,24},{64... | collective-permute-start | bytes 1966088 | tf_op jit(solution)/shard_map/ppermute | solution.py:52
  68.0 3.9 %collective-permute-start.17 = (bf16[640,256]{1,0:T(8,128)(2,1)S(1)}, bf16[640,256]{1,0:T(8,128)(2,1)S(1)}, u32[]{:S(2)}, u32[]{:S(2)}) collective-permute-start(bf16[640,256]{1,0:T(8,128)(2,1)S(1)} %get-tuple-element.70), channel_id=1, source_target_pairs={{0,8},{8,0},{1,9},{9,1},{2,10},{10,2},{3,11},{11,3},{4,12},{12,4},... | collective-permute-start | bytes 983048 | tf_op jit(solution)/shard_map/ppermute | solution.py:52
  68.1 10.7 %collective-permute-start.19 = (bf16[2,320,512]{2,1,0:T(8,128)(2,1)S(1)}, bf16[2,320,512]{2,1,0:T(8,128)(2,1)S(1)}, u32[]{:S(2)}, u32[]{:S(2)}) collective-permute-start(bf16[2,320,512]{2,1,0:T(8,128)(2,1)S(1)} %get-tuple-element.73), channel_id=1, source_target_pairs={{0,32},{8,104},{16,48},{24,120},{32,64},{40,8},{48,80},{56,24},{64... | collective-permute-start | bytes 1966088 | tf_op jit(solution)/shard_map/ppermute | solution.py:52
  73.4 12.4 %collective-permute-start.18 = (bf16[2,160,1024]{2,1,0:T(8,128)(2,1)S(1)}, bf16[2,160,1024]{2,1,0:T(8,128)(2,1)S(1)}, u32[]{:S(2)}, u32[]{:S(2)}) collective-permute-start(bf16[2,160,1024]{2,1,0:T(8,128)(2,1)S(1)} %get-tuple-element.72), channel_id=1, source_target_pairs={{0,32},{8,104},{16,48},{24,120},{32,64},{40,8},{48,80},{56,24},{64... | collective-permute-start | bytes 1966088 | tf_op jit(solution)/shard_map/ppermute | solution.py:52
  74.0 17.7 %collective-permute-start.16 = (bf16[2,320,512]{2,1,0:T(8,128)(2,1)S(1)}, bf16[2,320,512]{2,1,0:T(8,128)(2,1)S(1)}, u32[]{:S(2)}, u32[]{:S(2)}) collective-permute-start(bf16[2,320,512]{2,1,0:T(8,128)(2,1)S(1)} %get-tuple-element.69.a), channel_id=1, source_target_pairs={{0,16},{16,0},{32,48},{48,32},{64,80},{80,64},{96,112},{112,96},{1... | collective-permute-start | bytes 1966088 | tf_op jit(solution)/shard_map/ppermute | solution.py:52
  87.3 11.6 %collective-permute-start.24 = (bf16[2,160,1024]{2,1,0:T(8,128)(2,1)S(1)}, bf16[2,160,1024]{2,1,0:T(8,128)(2,1)S(1)}, u32[]{:S(2)}, u32[]{:S(2)}) collective-permute-start(bf16[2,160,1024]{2,1,0:T(8,128)(2,1)S(1)} %get-tuple-element.79), channel_id=1, source_target_pairs={{0,32},{8,104},{16,48},{24,120},{32,64},{40,8},{48,80},{56,24},{64... | collective-permute-start | bytes 1966088 | tf_op jit(solution)/shard_map/ppermute | solution.py:52
  90.7 15.4 %collective-permute-start.23 = (bf16[2,320,512]{2,1,0:T(8,128)(2,1)S(1)}, bf16[2,320,512]{2,1,0:T(8,128)(2,1)S(1)}, u32[]{:S(2)}, u32[]{:S(2)}) collective-permute-start(bf16[2,320,512]{2,1,0:T(8,128)(2,1)S(1)} %get-tuple-element.78.a), channel_id=1, source_target_pairs={{0,16},{16,0},{32,48},{48,32},{64,80},{80,64},{96,112},{112,96},{1... | collective-permute-start | bytes 1966088 | tf_op jit(solution)/shard_map/ppermute | solution.py:52
  100.4 11.9 %collective-permute-start.27 = (bf16[2,160,1024]{2,1,0:T(8,128)(2,1)S(1)}, bf16[2,160,1024]{2,1,0:T(8,128)(2,1)S(1)}, u32[]{:S(2)}, u32[]{:S(2)}) collective-permute-start(bf16[2,160,1024]{2,1,0:T(8,128)(2,1)S(1)} %get-tuple-element.83), channel_id=1, source_target_pairs={{0,32},{8,104},{16,48},{24,120},{32,64},{40,8},{48,80},{56,24},{64... | collective-permute-start | bytes 1966088 | tf_op jit(solution)/shard_map/ppermute | solution.py:52
  114.3 8.3 %collective-permute-start.28 = (bf16[160,1024]{1,0:T(8,128)(2,1)S(1)}, bf16[160,1024]{1,0:T(8,128)(2,1)S(1)}, u32[]{:S(2)}, u32[]{:S(2)}) collective-permute-start(bf16[160,1024]{1,0:T(8,128)(2,1)S(1)} %get-tuple-element.85.refs_4_), channel_id=1, source_target_pairs={{0,32},{8,104},{16,48},{24,120},{32,64},{40,8},{48,80},{56,24},{64... | collective-permute-start | bytes 983048 | tf_op jit(solution)/shard_map/ppermute | solution.py:52
  118.0 8.3 %collective-permute-start.20 = (bf16[320,512]{1,0:T(8,128)(2,1)S(1)}, bf16[320,512]{1,0:T(8,128)(2,1)S(1)}, u32[]{:S(2)}, u32[]{:S(2)}) collective-permute-start(bf16[320,512]{1,0:T(8,128)(2,1)S(1)} %get-tuple-element.77.refs_0_), channel_id=1, source_target_pairs={{0,32},{8,104},{16,48},{24,120},{32,64},{40,8},{48,80},{56,24},{64... | collective-permute-start | bytes 983048 | tf_op jit(solution)/shard_map/ppermute | solution.py:52
  118.0 11.8 %collective-permute-start.25 = (bf16[320,512]{1,0:T(8,128)(2,1)S(1)}, bf16[320,512]{1,0:T(8,128)(2,1)S(1)}, u32[]{:S(2)}, u32[]{:S(2)}) collective-permute-start(bf16[320,512]{1,0:T(8,128)(2,1)S(1)} %get-tuple-element.82.refs_2_), channel_id=1, source_target_pairs={{0,32},{8,104},{16,48},{24,120},{32,64},{40,8},{48,80},{56,24},{64... | collective-permute-start | bytes 983048 | tf_op jit(solution)/shard_map/ppermute | solution.py:52
  118.0 16.1 %collective-permute-start.31 = (bf16[160,1024]{1,0:T(8,128)(2,1)S(1)}, bf16[160,1024]{1,0:T(8,128)(2,1)S(1)}, u32[]{:S(2)}, u32[]{:S(2)}) collective-permute-start(bf16[160,1024]{1,0:T(8,128)(2,1)S(1)} %get-tuple-element.85.refs_4_), channel_id=1, source_target_pairs={{0,16},{16,0},{32,48},{48,32},{64,80},{80,64},{96,112},{112,96},{1... | collective-permute-start | bytes 983048 | tf_op jit(solution)/shard_map/ppermute | solution.py:52
  122.6 11.6 %collective-permute-start.30 = (bf16[160,1024]{1,0:T(8,128)(2,1)S(1)}, bf16[160,1024]{1,0:T(8,128)(2,1)S(1)}, u32[]{:S(2)}, u32[]{:S(2)}) collective-permute-start(bf16[160,1024]{1,0:T(8,128)(2,1)S(1)} %collective-permute-done.28.refs_5_), channel_id=1, source_target_pairs={{0,32},{8,104},{16,48},{24,120},{32,64},{40,8},{48,80},{56,24},{64... | collective-permute-start | bytes 983048 | tf_op jit(solution)/shard_map/ppermute | solution.py:52
  126.2 11.1 %collective-permute-start.21 = (bf16[320,512]{1,0:T(8,128)(2,1)S(1)}, bf16[320,512]{1,0:T(8,128)(2,1)S(1)}, u32[]{:S(2)}, u32[]{:S(2)}) collective-permute-start(bf16[320,512]{1,0:T(8,128)(2,1)S(1)} %collective-permute-done.20.refs_1_), channel_id=1, source_target_pairs={{0,32},{8,104},{16,48},{24,120},{32,64},{40,8},{48,80},{56,24},{64... | collective-permute-start | bytes 983048 | tf_op jit(solution)/shard_map/ppermute | solution.py:52
  129.8 13.6 %collective-permute-start.26 = (bf16[320,512]{1,0:T(8,128)(2,1)S(1)}, bf16[320,512]{1,0:T(8,128)(2,1)S(1)}, u32[]{:S(2)}, u32[]{:S(2)}) collective-permute-start(bf16[320,512]{1,0:T(8,128)(2,1)S(1)} %collective-permute-done.25.refs_3_), channel_id=1, source_target_pairs={{0,32},{8,104},{16,48},{24,120},{32,64},{40,8},{48,80},{56,24},{64... | collective-permute-start | bytes 983048 | tf_op jit(solution)/shard_map/ppermute | solution.py:52
  133.3 12.0 %collective-permute-start.29 = (bf16[160,1024]{1,0:T(8,128)(2,1)S(1)}, bf16[160,1024]{1,0:T(8,128)(2,1)S(1)}, u32[]{:S(2)}, u32[]{:S(2)}) collective-permute-start(bf16[160,1024]{1,0:T(8,128)(2,1)S(1)} %collective-permute-done.28.refs_5_), channel_id=1, source_target_pairs={{0,16},{16,0},{32,48},{48,32},{64,80},{80,64},{96,112},{112,96},{1... | collective-permute-start | bytes 983048 | tf_op jit(solution)/shard_map/ppermute | solution.py:52
  134.7 11.2 %collective-permute-start.33 = (bf16[160,1024]{1,0:T(8,128)(2,1)S(1)}, bf16[160,1024]{1,0:T(8,128)(2,1)S(1)}, u32[]{:S(2)}, u32[]{:S(2)}) collective-permute-start(bf16[160,1024]{1,0:T(8,128)(2,1)S(1)} %get-tuple-element.86.refs_6_), channel_id=1, source_target_pairs={{0,32},{8,104},{16,48},{24,120},{32,64},{40,8},{48,80},{56,24},{64... | collective-permute-start | bytes 983048 | tf_op jit(solution)/shard_map/ppermute | solution.py:52
  137.4 9.8 %collective-permute-start.22 = (bf16[320,512]{1,0:T(8,128)(2,1)S(1)}, bf16[320,512]{1,0:T(8,128)(2,1)S(1)}, u32[]{:S(2)}, u32[]{:S(2)}) collective-permute-start(bf16[320,512]{1,0:T(8,128)(2,1)S(1)} %collective-permute-done.21.refs_0_), channel_id=1, source_target_pairs={{0,32},{8,104},{16,48},{24,120},{32,64},{40,8},{48,80},{56,24},{64... | collective-permute-start | bytes 983048 | tf_op jit(solution)/shard_map/ppermute | solution.py:52
  140.3 12.0 %collective-permute-start.34 = (bf16[160,1024]{1,0:T(8,128)(2,1)S(1)}, bf16[160,1024]{1,0:T(8,128)(2,1)S(1)}, u32[]{:S(2)}, u32[]{:S(2)}) collective-permute-start(bf16[160,1024]{1,0:T(8,128)(2,1)S(1)} %get-tuple-element.86.refs_6_), channel_id=1, source_target_pairs={{0,16},{16,0},{32,48},{48,32},{64,80},{80,64},{96,112},{112,96},{1... | collective-permute-start | bytes 983048 | tf_op jit(solution)/shard_map/ppermute | solution.py:52
  145.9 7.1 %collective-permute-start.32 = (bf16[320,512]{1,0:T(8,128)(2,1)S(1)}, bf16[320,512]{1,0:T(8,128)(2,1)S(1)}, u32[]{:S(2)}, u32[]{:S(2)}) collective-permute-start(bf16[320,512]{1,0:T(8,128)(2,1)S(1)} %get-tuple-element.88.refs_2_), channel_id=1, source_target_pairs={{0,32},{8,104},{16,48},{24,120},{32,64},{40,8},{48,80},{56,24},{64... | collective-permute-start | bytes 983048 | tf_op jit(solution)/shard_map/ppermute | solution.py:52
  145.9 10.0 %collective-permute-start.35 = (bf16[160,1024]{1,0:T(8,128)(2,1)S(1)}, bf16[160,1024]{1,0:T(8,128)(2,1)S(1)}, u32[]{:S(2)}, u32[]{:S(2)}) collective-permute-start(bf16[160,1024]{1,0:T(8,128)(2,1)S(1)} %collective-permute-done.33.refs_4_), channel_id=1, source_target_pairs={{0,16},{16,0},{32,48},{48,32},{64,80},{80,64},{96,112},{112,96},{1... | collective-permute-start | bytes 983048 | tf_op jit(solution)/shard_map/ppermute | solution.py:52

commit v6 on v3

--- a/solution.py
+++ b/solution.py
@@ -383,16 +383,16 @@
             out, token = merge(a_sum[1], a_got[1], token)
             a_all[1] = [out, onward(out)]
     b_out, token = far_terms(0, b_got, True, token)
-    a_all[0].append(onward(a_all[0][2]))
     b_near = [b_out, onward(b_out)]
     b_far = [move(piece, Z_SWAP) for piece in b_near]
     b_near.append(onward(b_near[1]))
     a_all[1].append(onward(a_all[1][1]))
     b_near[2], _ = hold(b_near[2], [b_far[0]])
     b_near.append(onward(b_near[2]))
-    a_all[1][2], _ = hold(a_all[1][2], [b_far[1]])
-    a_all[1].append(onward(a_all[1][2]))
     b_far += [move(piece, Z_SWAP) for piece in b_near[2:]]
+    for p in range(2):
+        a_all[p][2], _ = hold(a_all[p][2], [b_far[1 + p]])
+        a_all[p].append(onward(a_all[p][2]))
 
     plan = []
     for k in range(4):

time: 159 us -> 161 us (1.013)
  waiting for transfers between devices: 65.9 us -> 68.6 us
  starting transfers between devices: 57.4 us -> 55 us
    ppermute x36, waiting for transfers between devices: 65.9 us -> 68.6 us  [move(): return lax.ppermute(x, axis, perm)]
    ppermute x36, starting transfers between devices: 57.4 us -> 55 us  [move(): return lax.ppermute(x, axis, perm)]
  transfers between devices with their start and end apart: 36 -> 36, of which waited for: 19 -> 20; matrix products, arithmetic and copies ran while one was open for 0% -> 0% of each run, Pallas kernels for 17% -> 18%
where the time goes in v6:
time: 161 us; the launch traced here: 160 us
  waiting for transfers between devices  68.6 us (43%)
  starting transfers between devices  55 us (34%)
  Pallas kernels  35.7 us (22%)
    ppermute x36, waiting for transfers between devices, move(): return lax.ppermute(x, axis, perm)  68.6 us
    ppermute x36, starting transfers between devices, move(): return lax.ppermute(x, axis, perm)  55 us
    pallas_call x12, Pallas kernels, terms(): pl.pallas_call(functools.partial(term_kernel, rows, nb, [s[5] for s in so...  18.4 us
    pallas_call x1, Pallas kernels, project(): pl.pallas_call(functools.partial(project_kernel, step), in_specs=[SMEM] +...  10.5 us
    pallas_call x1, Pallas kernels, place(): pl.pallas_call(functools.partial(place_kernel, plan, len(parts)), in_spec...  3.27 us
  transfers between devices with their start and end apart: 36, of which 20 were waited for; matrix products, arithmetic and copies ran while one was open for 0% of the time, Pallas kernels for 18%

profile of v6, /device:TPU:56, one launch (start us, length us, event | category | flops | bytes accessed | tf_op | source)
XLA Modules:
  0.0 159.8 jit_solution(2366746261161733892)
XLA Ops:
  0.0 3.0 %collective-permute-start.4 = (bf16[512,256]{1,0:T(8,128)(2,1)}, bf16[512,256]{1,0:T(8,128)(2,1)S(1)}, u32[]{:S(2)}, u32[]{:S(2)}) collective-permute-start(bf16[512,256]{1,0:T(8,128)(2,1)} %bitcast.51), channel_id=1, source_target_pairs={{0,2},{1,3},{2,0},{3,1},{4,6},{5,7},{6,4},{7,5},{8,10},{9,11},{10,... | collective-permute-start | bytes 786440 | tf_op jit(solution)/shard_map/ppermute | solution.py:52
  5.1 1.9 %collective-permute-start.1 = (bf16[512,256]{1,0:T(8,128)(2,1)}, bf16[512,256]{1,0:T(8,128)(2,1)S(1)}, u32[]{:S(2)}, u32[]{:S(2)}) collective-permute-start(bf16[512,256]{1,0:T(8,128)(2,1)} %bitcast.54), channel_id=1, source_target_pairs={{0,20},{1,21},{2,22},{3,23},{4,16},{5,17},{6,18},{7,19},{16,4},{17... | collective-permute-start | bytes 786440 | tf_op jit(solution)/shard_map/ppermute | solution.py:52
  7.0 2.2 %collective-permute-start = (bf16[512,256]{1,0:T(8,128)(2,1)}, bf16[512,256]{1,0:T(8,128)(2,1)S(1)}, u32[]{:S(2)}, u32[]{:S(2)}) collective-permute-start(bf16[512,256]{1,0:T(8,128)(2,1)} %bitcast.55), channel_id=1, source_target_pairs={{0,4},{1,5},{2,6},{3,7},{4,0},{5,1},{6,2},{7,3},{8,12},{9,13},{10,... | collective-permute-start | bytes 786440 | tf_op jit(solution)/shard_map/ppermute | solution.py:52
  9.3 10.5 %shard_map.55 = (f32[2,256,1280]{2,1,0:T(8,128)S(1)}, bf16[2,256,1280]{2,1,0:T(8,128)(2,1)S(1)}, f32[8,128]{1,0:T(8,128)S(1)}) custom-call(s32[39]{0:T(128)S(1)} %stack.135.offs, bf16[512,2048]{1,0:T(8,128)(2,1)} %bitcast.62, bf16[2048,1280]{1,0:T(8,128)(2,1)} %bitcast.60, bf16[2048,1280]{1,0:T(8,128)(2,1)} %bitcast.61), custom_call_target="tpu_custom_call" | custom-call | tf_op jit(solution)/shard_map/pallas_call | solution.py:95
  20.0 3.0 %collective-permute-done.5.recv_ref = bf16[2,256,1280]{2,1,0:T(8,128)(2,1)S(1)} collective-permute-done((bf16[2,256,1280]{2,1,0:T(8,128)(2,1)S(1)}, bf16[2,256,1280]{2,1,0:T(8,128)(2,1)S(1)}, u32[]{:S(2)}, u32[]{:S(2)}) %collective-permute-start.5) | collective-permute-done | bytes 1310752 | tf_op jit(solution)/shard_map/ppermute | solution.py:52
  24.6 2.0 %collective-permute-done.6.refs_1_ = bf16[1280,256]{1,0:T(8,128)(2,1)S(1)} collective-permute-done((bf16[1280,256]{1,0:T(8,128)(2,1)S(1)}, bf16[1280,256]{1,0:T(8,128)(2,1)S(1)}, u32[]{:S(2)}, u32[]{:S(2)}) %collective-permute-start.6) | collective-permute-done | bytes 655392 | tf_op jit(solution)/shard_map/ppermute | solution.py:52
  26.6 1.5 shard_map.58
  28.4 1.5 shard_map.59
  29.9 1.6 %collective-permute-start.9 = (bf16[2,320,512]{2,1,0:T(8,128)(2,1)S(1)}, bf16[2,320,512]{2,1,0:T(8,128)(2,1)S(1)}, u32[]{:S(2)}, u32[]{:S(2)}) collective-permute-start(bf16[2,320,512]{2,1,0:T(8,128)(2,1)S(1)} %get-tuple-element.58), channel_id=1, source_target_pairs={{0,32},{8,104},{16,48},{24,120},{32,64},{40,8},{48,80},{56,24},{64... | collective-permute-start | bytes 1966088 | tf_op jit(solution)/shard_map/ppermute | solution.py:52
  31.5 2.3 %collective-permute-start.11 = (bf16[2,512,256]{2,1,0:T(8,128)(2,1)S(1)}, bf16[2,512,256]{2,1,0:T(8,128)(2,1)S(1)}, u32[]{:S(2)}, u32[]{:S(2)}) collective-permute-start(bf16[2,512,256]{2,1,0:T(8,128)(2,1)S(1)} %get-tuple-element.60.refs_2_.refs_9_), channel_id=1, source_target_pairs={{0,3},{1,0},{2,1},{3,2},{4,7},{5,4},{6,5},{7,6},{8,11},{9,8},{10,9... | collective-permute-start | bytes 1572872 | tf_op jit(solution)/shard_map/ppermute | solution.py:52
  33.9 4.8 %collective-permute-done.7.refs_5_ = bf16[2,320,512]{2,1,0:T(8,128)(2,1)S(1)} collective-permute-done((bf16[2,320,512]{2,1,0:T(8,128)(2,1)S(1)}, bf16[2,320,512]{2,1,0:T(8,128)(2,1)S(1)}, u32[]{:S(2)}, u32[]{:S(2)}) %collective-permute-start.7) | collective-permute-done | bytes 655392 | tf_op jit(solution)/shard_map/ppermute | solution.py:52
  38.7 1.6 shard_map.60
  40.3 1.5 collective-permute-start.8
  41.8 2.5 %collective-permute-done.11.refs_8_.refs_5_.refs_12_ = bf16[2,512,256]{2,1,0:T(8,128)(2,1)S(1)} collective-permute-done((bf16[2,512,256]{2,1,0:T(8,128)(2,1)S(1)}, bf16[2,512,256]{2,1,0:T(8,128)(2,1)S(1)}, u32[]{:S(2)}, u32[]{:S(2)}) %collective-permute-start.11) | collective-permute-done | bytes 524320 | tf_op jit(solution)/shard_map/ppermute | solution.py:52
  44.3 3.3 %collective-permute-done.10.refs_7_.refs_3_.refs_10_ = bf16[2,512,256]{2,1,0:T(8,128)(2,1)S(1)} collective-permute-done((bf16[2,512,256]{2,1,0:T(8,128)(2,1)S(1)}, bf16[2,512,256]{2,1,0:T(8,128)(2,1)S(1)}, u32[]{:S(2)}, u32[]{:S(2)}) %collective-permute-start.10) | collective-permute-done | bytes 524320 | tf_op jit(solution)/shard_map/ppermute | solution.py:52
  47.6 1.6 shard_map.61
  49.2 2.9 %collective-permute-start.14 = (bf16[2,320,512]{2,1,0:T(8,128)(2,1)S(1)}, bf16[2,320,512]{2,1,0:T(8,128)(2,1)S(1)}, u32[]{:S(2)}, u32[]{:S(2)}) collective-permute-start(bf16[2,320,512]{2,1,0:T(8,128)(2,1)S(1)} %get-tuple-element.64), channel_id=1, source_target_pairs={{0,32},{8,104},{16,48},{24,120},{32,64},{40,8},{48,80},{56,24},{64... | collective-permute-start | bytes 1966088 | tf_op jit(solution)/shard_map/ppermute | solution.py:52
  52.8 1.6 shard_map.62
  54.3 1.5 collective-permute-start.12
  55.8 7.5 %collective-permute-done.15.refs_7_.refs_4_.refs_11_ = bf16[2,512,256]{2,1,0:T(8,128)(2,1)S(1)} collective-permute-done((bf16[2,512,256]{2,1,0:T(8,128)(2,1)S(1)}, bf16[2,512,256]{2,1,0:T(8,128)(2,1)S(1)}, u32[]{:S(2)}, u32[]{:S(2)}) %collective-permute-start.15) | collective-permute-done | bytes 524320 | tf_op jit(solution)/shard_map/ppermute | solution.py:52
  63.3 1.6 shard_map.63
  64.9 3.1 %collective-permute-done.13.a_ref.refs_7_.refs_13_ = bf16[640,1280]{1,0:T(8,128)(2,1)S(1)} collective-permute-done((bf16[640,1280]{1,0:T(8,128)(2,1)S(1)}, bf16[640,1280]{1,0:T(8,128)(2,1)S(1)}, u32[]{:S(2)}, u32[]{:S(2)}) %collective-permute-start.13) | collective-permute-done | bytes 1638432 | tf_op jit(solution)/shard_map/ppermute | solution.py:52
  68.1 2.3 %collective-permute-start.19 = (bf16[2,320,512]{2,1,0:T(8,128)(2,1)S(1)}, bf16[2,320,512]{2,1,0:T(8,128)(2,1)S(1)}, u32[]{:S(2)}, u32[]{:S(2)}) collective-permute-start(bf16[2,320,512]{2,1,0:T(8,128)(2,1)S(1)} %get-tuple-element.72), channel_id=1, source_target_pairs={{0,32},{8,104},{16,48},{24,120},{32,64},{40,8},{48,80},{56,24},{64... | collective-permute-start | bytes 1966088 | tf_op jit(solution)/shard_map/ppermute | solution.py:52
  70.4 1.6 shard_map.65
  74.0 3.3 %collective-permute-start.16 = (bf16[2,320,512]{2,1,0:T(8,128)(2,1)S(1)}, bf16[2,320,512]{2,1,0:T(8,128)(2,1)S(1)}, u32[]{:S(2)}, u32[]{:S(2)}) collective-permute-start(bf16[2,320,512]{2,1,0:T(8,128)(2,1)S(1)} %get-tuple-element.68.a), channel_id=1, source_target_pairs={{0,16},{16,0},{32,48},{48,32},{64,80},{80,64},{96,112},{112,96},{1... | collective-permute-start | bytes 1966088 | tf_op jit(solution)/shard_map/ppermute | solution.py:52
  77.2 1.5 collective-permute-done.19.refs_5_
  78.7 1.6 shard_map.67
  80.3 5.5 %collective-permute-done.18.refs_14_ = bf16[2,160,1024]{2,1,0:T(8,128)(2,1)S(1)} collective-permute-done((bf16[2,160,1024]{2,1,0:T(8,128)(2,1)S(1)}, bf16[2,160,1024]{2,1,0:T(8,128)(2,1)S(1)}, u32[]{:S(2)}, u32[]{:S(2)}) %collective-permute-start.18) | collective-permute-done | bytes 655392 | tf_op jit(solution)/shard_map/ppermute | solution.py:52
  85.8 1.5 shard_map.68
  87.3 3.5 %collective-permute-start.22 = (bf16[2,160,1024]{2,1,0:T(8,128)(2,1)S(1)}, bf16[2,160,1024]{2,1,0:T(8,128)(2,1)S(1)}, u32[]{:S(2)}, u32[]{:S(2)}) collective-permute-start(bf16[2,160,1024]{2,1,0:T(8,128)(2,1)S(1)} %get-tuple-element.77), channel_id=1, source_target_pairs={{0,32},{8,104},{16,48},{24,120},{32,64},{40,8},{48,80},{56,24},{64... | collective-permute-start | bytes 1966088 | tf_op jit(solution)/shard_map/ppermute | solution.py:52
  91.8 7.0 %collective-permute-done.22.refs_14_ = bf16[2,160,1024]{2,1,0:T(8,128)(2,1)S(1)} collective-permute-done((bf16[2,160,1024]{2,1,0:T(8,128)(2,1)S(1)}, bf16[2,160,1024]{2,1,0:T(8,128)(2,1)S(1)}, u32[]{:S(2)}, u32[]{:S(2)}) %collective-permute-start.22) | collective-permute-done | bytes 655392 | tf_op jit(solution)/shard_map/ppermute | solution.py:52
  98.9 1.5 shard_map.70
  100.4 3.8 %collective-permute-start.23 = (bf16[2,160,1024]{2,1,0:T(8,128)(2,1)S(1)}, bf16[2,160,1024]{2,1,0:T(8,128)(2,1)S(1)}, u32[]{:S(2)}, u32[]{:S(2)}) collective-permute-start(bf16[2,160,1024]{2,1,0:T(8,128)(2,1)S(1)} %get-tuple-element.79), channel_id=1, source_target_pairs={{0,32},{8,104},{16,48},{24,120},{32,64},{40,8},{48,80},{56,24},{64... | collective-permute-start | bytes 1966088 | tf_op jit(solution)/shard_map/ppermute | solution.py:52
  104.1 2.1 %collective-permute-done.24.b = bf16[2,320,512]{2,1,0:T(8,128)(2,1)S(1)} collective-permute-done((bf16[2,320,512]{2,1,0:T(8,128)(2,1)S(1)}, bf16[2,320,512]{2,1,0:T(8,128)(2,1)S(1)}, u32[]{:S(2)}, u32[]{:S(2)}) %collective-permute-start.24) | collective-permute-done | bytes 655392 | tf_op jit(solution)/shard_map/ppermute | solution.py:52
  106.4 5.8 %collective-permute-done.23.refs_14_ = bf16[2,160,1024]{2,1,0:T(8,128)(2,1)S(1)} collective-permute-done((bf16[2,160,1024]{2,1,0:T(8,128)(2,1)S(1)}, bf16[2,160,1024]{2,1,0:T(8,128)(2,1)S(1)}, u32[]{:S(2)}, u32[]{:S(2)}) %collective-permute-start.23) | collective-permute-done | bytes 655392 | tf_op jit(solution)/shard_map/ppermute | solution.py:52
  112.2 1.5 shard_map.72
  113.8 3.8 %collective-permute-start.25 = (bf16[160,1024]{1,0:T(8,128)(2,1)S(1)}, bf16[160,1024]{1,0:T(8,128)(2,1)S(1)}, u32[]{:S(2)}, u32[]{:S(2)}) collective-permute-start(bf16[160,1024]{1,0:T(8,128)(2,1)S(1)} %get-tuple-element.83.refs_8_), channel_id=1, source_target_pairs={{0,32},{8,104},{16,48},{24,120},{32,64},{40,8},{48,80},{56,24},{64... | collective-permute-start | bytes 983048 | tf_op jit(solution)/shard_map/ppermute | solution.py:52
  118.5 3.6 %collective-permute-done.25.refs_9_ = bf16[160,1024]{1,0:T(8,128)(2,1)S(1)} collective-permute-done((bf16[160,1024]{1,0:T(8,128)(2,1)S(1)}, bf16[160,1024]{1,0:T(8,128)(2,1)S(1)}, u32[]{:S(2)}, u32[]{:S(2)}) %collective-permute-start.25) | collective-permute-done | bytes 327712 | tf_op jit(solution)/shard_map/ppermute | solution.py:52
  122.1 3.7 %collective-permute-start.30 = (bf16[160,1024]{1,0:T(8,128)(2,1)S(1)}, bf16[160,1024]{1,0:T(8,128)(2,1)S(1)}, u32[]{:S(2)}, u32[]{:S(2)}) collective-permute-start(bf16[160,1024]{1,0:T(8,128)(2,1)S(1)} %collective-permute-done.25.refs_9_), channel_id=1, source_target_pairs={{0,32},{8,104},{16,48},{24,120},{32,64},{40,8},{48,80},{56,24},{64... | collective-permute-start | bytes 983048 | tf_op jit(solution)/shard_map/ppermute | solution.py:52
  125.8 3.5 %collective-permute-start.21 = (bf16[320,512]{1,0:T(8,128)(2,1)S(1)}, bf16[320,512]{1,0:T(8,128)(2,1)S(1)}, u32[]{:S(2)}, u32[]{:S(2)}) collective-permute-start(bf16[320,512]{1,0:T(8,128)(2,1)S(1)} %collective-permute-done.20.refs_1_), channel_id=1, source_target_pairs={{0,32},{8,104},{16,48},{24,120},{32,64},{40,8},{48,80},{56,24},{64... | collective-permute-start | bytes 983048 | tf_op jit(solution)/shard_map/ppermute | solution.py:52
  131.0 3.7 %collective-permute-start.34 = (bf16[160,1024]{1,0:T(8,128)(2,1)S(1)}, bf16[160,1024]{1,0:T(8,128)(2,1)S(1)}, u32[]{:S(2)}, u32[]{:S(2)}) collective-permute-start(bf16[160,1024]{1,0:T(8,128)(2,1)S(1)} %get-tuple-element.86.refs_10_), channel_id=1, source_target_pairs={{0,32},{8,104},{16,48},{24,120},{32,64},{40,8},{48,80},{56,24},{64... | collective-permute-start | bytes 983048 | tf_op jit(solution)/shard_map/ppermute | solution.py:52
  134.7 2.9 %collective-permute-start.29 = (bf16[320,512]{1,0:T(8,128)(2,1)S(1)}, bf16[320,512]{1,0:T(8,128)(2,1)S(1)}, u32[]{:S(2)}, u32[]{:S(2)}) collective-permute-start(bf16[320,512]{1,0:T(8,128)(2,1)S(1)} %collective-permute-done.28.refs_5_), channel_id=1, source_target_pairs={{0,32},{8,104},{16,48},{24,120},{32,64},{40,8},{48,80},{56,24},{64... | collective-permute-start | bytes 983048 | tf_op jit(solution)/shard_map/ppermute | solution.py:52
  138.5 2.9 %collective-permute-done.26.refs_1_.refs_13_ = bf16[160,1024]{1,0:T(8,128)(2,1)S(1)} collective-permute-done((bf16[160,1024]{1,0:T(8,128)(2,1)S(1)}, bf16[160,1024]{1,0:T(8,128)(2,1)S(1)}, u32[]{:S(2)}, u32[]{:S(2)}) %collective-permute-start.26) | collective-permute-done | bytes 327712 | tf_op jit(solution)/shard_map/ppermute | solution.py:52
  142.7 1.8 %collective-permute-done.29.refs_0_ = bf16[320,512]{1,0:T(8,128)(2,1)S(1)} collective-permute-done((bf16[320,512]{1,0:T(8,128)(2,1)S(1)}, bf16[320,512]{1,0:T(8,128)(2,1)S(1)}, u32[]{:S(2)}, u32[]{:S(2)}) %collective-permute-start.29) | collective-permute-done | bytes 327712 | tf_op jit(solution)/shard_map/ppermute | solution.py:52
  144.4 4.2 %collective-permute-done.32.refs_1_.refs_14_ = bf16[160,1024]{1,0:T(8,128)(2,1)S(1)} collective-permute-done((bf16[160,1024]{1,0:T(8,128)(2,1)S(1)}, bf16[160,1024]{1,0:T(8,128)(2,1)S(1)}, u32[]{:S(2)}, u32[]{:S(2)}) %collective-permute-start.32) | collective-permute-done | bytes 327712 | tf_op jit(solution)/shard_map/ppermute | solution.py:52
  149.2 2.9 %collective-permute-done.35.refs_15_ = bf16[160,1024]{1,0:T(8,128)(2,1)S(1)} collective-permute-done((bf16[160,1024]{1,0:T(8,128)(2,1)S(1)}, bf16[160,1024]{1,0:T(8,128)(2,1)S(1)}, u32[]{:S(2)}, u32[]{:S(2)}) %collective-permute-start.35) | collective-permute-done | bytes 327712 | tf_op jit(solution)/shard_map/ppermute | solution.py:52
  152.1 4.2 %collective-permute-done.33.refs_7_ = bf16[320,512]{1,0:T(8,128)(2,1)S(1)} collective-permute-done((bf16[320,512]{1,0:T(8,128)(2,1)S(1)}, bf16[320,512]{1,0:T(8,128)(2,1)S(1)}, u32[]{:S(2)}, u32[]{:S(2)}) %collective-permute-start.33) | collective-permute-done | bytes 327712 | tf_op jit(solution)/shard_map/ppermute | solution.py:52
  156.3 3.3 %shard_map.76 = bf16[1280,2048]{1,0:T(8,128)(2,1)} custom-call(s32[39]{0:T(128)S(1)} %stack.135.offs, bf16[320,512]{1,0:T(8,128)(2,1)S(1)} %get-tuple-element.76.refs_0_, bf16[320,512]{1,0:T(8,128)(2,1)S(1)} %collective-permute-done.20.refs_1_, bf16[320,512]{1,0:T(8,128)(2,1)S(1)} %get-tuple-element.84.refs_2_, ...), custom_call_target="tpu_custom_call" | custom-call | tf_op jit(solution)/shard_map/pallas_call | solution.py:282
  (54 shorter events, 13.7 us)
Async XLA Ops:
  0.0 19.8 %collective-permute-start.4 = (bf16[512,256]{1,0:T(8,128)(2,1)}, bf16[512,256]{1,0:T(8,128)(2,1)S(1)}, u32[]{:S(2)}, u32[]{:S(2)}) collective-permute-start(bf16[512,256]{1,0:T(8,128)(2,1)} %bitcast.51), channel_id=1, source_target_pairs={{0,2},{1,3},{2,0},{3,1},{4,6},{5,7},{6,4},{7,5},{8,10},{9,11},{10,... | collective-permute-start | bytes 786440 | tf_op jit(solution)/shard_map/ppermute | solution.py:52
  3.0 16.8 %collective-permute-start.3 = (bf16[512,256]{1,0:T(8,128)(2,1)}, bf16[512,256]{1,0:T(8,128)(2,1)S(1)}, u32[]{:S(2)}, u32[]{:S(2)}) collective-permute-start(bf16[512,256]{1,0:T(8,128)(2,1)} %bitcast.52), channel_id=1, source_target_pairs={{0,3},{1,0},{2,1},{3,2},{4,7},{5,4},{6,5},{7,6},{8,11},{9,8},{10,9... | collective-permute-start | bytes 786440 | tf_op jit(solution)/shard_map/ppermute | solution.py:52
  4.2 15.7 %collective-permute-start.2 = (bf16[512,256]{1,0:T(8,128)(2,1)}, bf16[512,256]{1,0:T(8,128)(2,1)S(1)}, u32[]{:S(2)}, u32[]{:S(2)}) collective-permute-start(bf16[512,256]{1,0:T(8,128)(2,1)} %bitcast.53), channel_id=1, source_target_pairs={{0,1},{1,2},{2,3},{3,0},{4,5},{5,6},{6,7},{7,4},{8,9},{9,10},{10,1... | collective-permute-start | bytes 786440 | tf_op jit(solution)/shard_map/ppermute | solution.py:52
  5.1 14.8 %collective-permute-start.1 = (bf16[512,256]{1,0:T(8,128)(2,1)}, bf16[512,256]{1,0:T(8,128)(2,1)S(1)}, u32[]{:S(2)}, u32[]{:S(2)}) collective-permute-start(bf16[512,256]{1,0:T(8,128)(2,1)} %bitcast.54), channel_id=1, source_target_pairs={{0,20},{1,21},{2,22},{3,23},{4,16},{5,17},{6,18},{7,19},{16,4},{17... | collective-permute-start | bytes 786440 | tf_op jit(solution)/shard_map/ppermute | solution.py:52
  7.0 12.9 %collective-permute-start = (bf16[512,256]{1,0:T(8,128)(2,1)}, bf16[512,256]{1,0:T(8,128)(2,1)S(1)}, u32[]{:S(2)}, u32[]{:S(2)}) collective-permute-start(bf16[512,256]{1,0:T(8,128)(2,1)} %bitcast.55), channel_id=1, source_target_pairs={{0,4},{1,5},{2,6},{3,7},{4,0},{5,1},{6,2},{7,3},{8,12},{9,13},{10,... | collective-permute-start | bytes 786440 | tf_op jit(solution)/shard_map/ppermute | solution.py:52
  9.3 13.7 %slice-start = ((s8[5242880]{0:T(1024)(128)(4,1)}), s8[4194304]{0:T(1024)(128)(4,1)S(1)}, s32[]{:S(2)}) async-start(s8[5242880]{0:T(1024)(128)(4,1)} %bitcast.36), calls=%async_computation | async-start | bytes 8388608
  9.3 13.7 %slice-start.1 = ((s8[5242880]{0:T(1024)(128)(4,1)}), s8[1048576]{0:T(1024)(128)(4,1)S(1)}, s32[]{:S(2)}) async-start(s8[5242880]{0:T(1024)(128)(4,1)} %bitcast.36), calls=%async_computation.1 | async-start | bytes 2097152
  19.9 3.1 %collective-permute-start.5 = (bf16[2,256,1280]{2,1,0:T(8,128)(2,1)S(1)}, bf16[2,256,1280]{2,1,0:T(8,128)(2,1)S(1)}, u32[]{:S(2)}, u32[]{:S(2)}) collective-permute-start(bf16[2,256,1280]{2,1,0:T(8,128)(2,1)S(1)} %get-tuple-element.50), channel_id=1, source_target_pairs={{0,8},{8,0},{1,9},{9,1},{2,10},{10,2},{3,11},{11,3},{4,12},{12,4},... | collective-permute-start | bytes 3932168 | tf_op jit(solution)/shard_map/ppermute | solution.py:52
  23.0 3.5 %copy-start = (bf16[1,512,256]{2,1,0:T(8,128)(2,1)S(1)}, bf16[1,512,256]{2,1,0:T(8,128)(2,1)}, u32[]{:S(2)}) copy-start(bf16[1,512,256]{2,1,0:T(8,128)(2,1)} %param.8) | copy-start | bytes 786436
  24.4 2.2 %collective-permute-start.6 = (bf16[1280,256]{1,0:T(8,128)(2,1)S(1)}, bf16[1280,256]{1,0:T(8,128)(2,1)S(1)}, u32[]{:S(2)}, u32[]{:S(2)}) collective-permute-start(bf16[1280,256]{1,0:T(8,128)(2,1)S(1)} %get-tuple-element.52.refs_0_), channel_id=1, source_target_pairs={{0,8},{8,0},{1,9},{9,1},{2,10},{10,2},{3,11},{11,3},{4,12},{12,4},... | collective-permute-start | bytes 1966088 | tf_op jit(solution)/shard_map/ppermute | solution.py:52
  28.1 10.7 %collective-permute-start.7 = (bf16[2,320,512]{2,1,0:T(8,128)(2,1)S(1)}, bf16[2,320,512]{2,1,0:T(8,128)(2,1)S(1)}, u32[]{:S(2)}, u32[]{:S(2)}) collective-permute-start(bf16[2,320,512]{2,1,0:T(8,128)(2,1)S(1)} %get-tuple-element.54), channel_id=1, source_target_pairs={{0,32},{8,104},{16,48},{24,120},{32,64},{40,8},{48,80},{56,24},{64... | collective-permute-start | bytes 1966088 | tf_op jit(solution)/shard_map/ppermute | solution.py:52
  28.4 39.6 %collective-permute-start.13 = (bf16[640,1280]{1,0:T(8,128)(2,1)S(1)}, bf16[640,1280]{1,0:T(8,128)(2,1)S(1)}, u32[]{:S(2)}, u32[]{:S(2)}) collective-permute-start(bf16[640,1280]{1,0:T(8,128)(2,1)S(1)} %get-tuple-element.63), channel_id=1, source_target_pairs={{0,16},{16,0},{32,48},{48,32},{64,80},{80,64},{96,112},{112,96},{1... | collective-permute-start | bytes 4915208 | tf_op jit(solution)/shard_map/ppermute | solution.py:52
  29.9 17.7 %collective-permute-start.9 = (bf16[2,320,512]{2,1,0:T(8,128)(2,1)S(1)}, bf16[2,320,512]{2,1,0:T(8,128)(2,1)S(1)}, u32[]{:S(2)}, u32[]{:S(2)}) collective-permute-start(bf16[2,320,512]{2,1,0:T(8,128)(2,1)S(1)} %get-tuple-element.58), channel_id=1, source_target_pairs={{0,32},{8,104},{16,48},{24,120},{32,64},{40,8},{48,80},{56,24},{64... | collective-permute-start | bytes 1966088 | tf_op jit(solution)/shard_map/ppermute | solution.py:52
  31.5 12.8 %collective-permute-start.11 = (bf16[2,512,256]{2,1,0:T(8,128)(2,1)S(1)}, bf16[2,512,256]{2,1,0:T(8,128)(2,1)S(1)}, u32[]{:S(2)}, u32[]{:S(2)}) collective-permute-start(bf16[2,512,256]{2,1,0:T(8,128)(2,1)S(1)} %get-tuple-element.60.refs_2_.refs_9_), channel_id=1, source_target_pairs={{0,3},{1,0},{2,1},{3,2},{4,7},{5,4},{6,5},{7,6},{8,11},{9,8},{10,9... | collective-permute-start | bytes 1572872 | tf_op jit(solution)/shard_map/ppermute | solution.py:52
  33.9 13.7 %collective-permute-start.10 = (bf16[2,512,256]{2,1,0:T(8,128)(2,1)S(1)}, bf16[2,512,256]{2,1,0:T(8,128)(2,1)S(1)}, u32[]{:S(2)}, u32[]{:S(2)}) collective-permute-start(bf16[2,512,256]{2,1,0:T(8,128)(2,1)S(1)} %get-tuple-element.60.refs_2_.refs_9_), channel_id=1, source_target_pairs={{0,1},{1,2},{2,3},{3,0},{4,5},{5,6},{6,7},{7,4},{8,9},{9,10},{10,1... | collective-permute-start | bytes 1572872 | tf_op jit(solution)/shard_map/ppermute | solution.py:52
  40.3 12.5 %collective-permute-start.8 = (bf16[2,320,512]{2,1,0:T(8,128)(2,1)S(1)}, bf16[2,320,512]{2,1,0:T(8,128)(2,1)S(1)}, u32[]{:S(2)}, u32[]{:S(2)}) collective-permute-start(bf16[2,320,512]{2,1,0:T(8,128)(2,1)S(1)} %get-tuple-element.57), channel_id=1, source_target_pairs={{0,32},{8,104},{16,48},{24,120},{32,64},{40,8},{48,80},{56,24},{64... | collective-permute-start | bytes 1966088 | tf_op jit(solution)/shard_map/ppermute | solution.py:52
  49.2 14.1 %collective-permute-start.14 = (bf16[2,320,512]{2,1,0:T(8,128)(2,1)S(1)}, bf16[2,320,512]{2,1,0:T(8,128)(2,1)S(1)}, u32[]{:S(2)}, u32[]{:S(2)}) collective-permute-start(bf16[2,320,512]{2,1,0:T(8,128)(2,1)S(1)} %get-tuple-element.64), channel_id=1, source_target_pairs={{0,32},{8,104},{16,48},{24,120},{32,64},{40,8},{48,80},{56,24},{64... | collective-permute-start | bytes 1966088 | tf_op jit(solution)/shard_map/ppermute | solution.py:52
  52.0 11.3 %collective-permute-start.15 = (bf16[2,512,256]{2,1,0:T(8,128)(2,1)S(1)}, bf16[2,512,256]{2,1,0:T(8,128)(2,1)S(1)}, u32[]{:S(2)}, u32[]{:S(2)}) collective-permute-start(bf16[2,512,256]{2,1,0:T(8,128)(2,1)S(1)} %get-tuple-element.60.refs_2_.refs_9_), channel_id=1, source_target_pairs={{0,2},{1,3},{2,0},{3,1},{4,6},{5,7},{6,4},{7,5},{8,10},{9,11},{10,... | collective-permute-start | bytes 1572872 | tf_op jit(solution)/shard_map/ppermute | solution.py:52
  54.3 16.0 %collective-permute-start.12 = (bf16[2,320,512]{2,1,0:T(8,128)(2,1)S(1)}, bf16[2,320,512]{2,1,0:T(8,128)(2,1)S(1)}, u32[]{:S(2)}, u32[]{:S(2)}) collective-permute-start(bf16[2,320,512]{2,1,0:T(8,128)(2,1)S(1)} %get-tuple-element.62), channel_id=1, source_target_pairs={{0,32},{8,104},{16,48},{24,120},{32,64},{40,8},{48,80},{56,24},{64... | collective-permute-start | bytes 1966088 | tf_op jit(solution)/shard_map/ppermute | solution.py:52
  68.0 3.9 %collective-permute-start.17 = (bf16[640,256]{1,0:T(8,128)(2,1)S(1)}, bf16[640,256]{1,0:T(8,128)(2,1)S(1)}, u32[]{:S(2)}, u32[]{:S(2)}) collective-permute-start(bf16[640,256]{1,0:T(8,128)(2,1)S(1)} %get-tuple-element.69), channel_id=1, source_target_pairs={{0,8},{8,0},{1,9},{9,1},{2,10},{10,2},{3,11},{11,3},{4,12},{12,4},... | collective-permute-start | bytes 983048 | tf_op jit(solution)/shard_map/ppermute | solution.py:52
  68.1 10.7 %collective-permute-start.19 = (bf16[2,320,512]{2,1,0:T(8,128)(2,1)S(1)}, bf16[2,320,512]{2,1,0:T(8,128)(2,1)S(1)}, u32[]{:S(2)}, u32[]{:S(2)}) collective-permute-start(bf16[2,320,512]{2,1,0:T(8,128)(2,1)S(1)} %get-tuple-element.72), channel_id=1, source_target_pairs={{0,32},{8,104},{16,48},{24,120},{32,64},{40,8},{48,80},{56,24},{64... | collective-permute-start | bytes 1966088 | tf_op jit(solution)/shard_map/ppermute | solution.py:52
  73.4 12.4 %collective-permute-start.18 = (bf16[2,160,1024]{2,1,0:T(8,128)(2,1)S(1)}, bf16[2,160,1024]{2,1,0:T(8,128)(2,1)S(1)}, u32[]{:S(2)}, u32[]{:S(2)}) collective-permute-start(bf16[2,160,1024]{2,1,0:T(8,128)(2,1)S(1)} %get-tuple-element.71), channel_id=1, source_target_pairs={{0,32},{8,104},{16,48},{24,120},{32,64},{40,8},{48,80},{56,24},{64... | collective-permute-start | bytes 1966088 | tf_op jit(solution)/shard_map/ppermute | solution.py:52
  74.0 17.7 %collective-permute-start.16 = (bf16[2,320,512]{2,1,0:T(8,128)(2,1)S(1)}, bf16[2,320,512]{2,1,0:T(8,128)(2,1)S(1)}, u32[]{:S(2)}, u32[]{:S(2)}) collective-permute-start(bf16[2,320,512]{2,1,0:T(8,128)(2,1)S(1)} %get-tuple-element.68.a), channel_id=1, source_target_pairs={{0,16},{16,0},{32,48},{48,32},{64,80},{80,64},{96,112},{112,96},{1... | collective-permute-start | bytes 1966088 | tf_op jit(solution)/shard_map/ppermute | solution.py:52
  87.3 11.6 %collective-permute-start.22 = (bf16[2,160,1024]{2,1,0:T(8,128)(2,1)S(1)}, bf16[2,160,1024]{2,1,0:T(8,128)(2,1)S(1)}, u32[]{:S(2)}, u32[]{:S(2)}) collective-permute-start(bf16[2,160,1024]{2,1,0:T(8,128)(2,1)S(1)} %get-tuple-element.77), channel_id=1, source_target_pairs={{0,32},{8,104},{16,48},{24,120},{32,64},{40,8},{48,80},{56,24},{64... | collective-permute-start | bytes 1966088 | tf_op jit(solution)/shard_map/ppermute | solution.py:52
  90.7 15.4 %collective-permute-start.24 = (bf16[2,320,512]{2,1,0:T(8,128)(2,1)S(1)}, bf16[2,320,512]{2,1,0:T(8,128)(2,1)S(1)}, u32[]{:S(2)}, u32[]{:S(2)}) collective-permute-start(bf16[2,320,512]{2,1,0:T(8,128)(2,1)S(1)} %get-tuple-element.80.a), channel_id=1, source_target_pairs={{0,16},{16,0},{32,48},{48,32},{64,80},{80,64},{96,112},{112,96},{1... | collective-permute-start | bytes 1966088 | tf_op jit(solution)/shard_map/ppermute | solution.py:52
  100.4 11.9 %collective-permute-start.23 = (bf16[2,160,1024]{2,1,0:T(8,128)(2,1)S(1)}, bf16[2,160,1024]{2,1,0:T(8,128)(2,1)S(1)}, u32[]{:S(2)}, u32[]{:S(2)}) collective-permute-start(bf16[2,160,1024]{2,1,0:T(8,128)(2,1)S(1)} %get-tuple-element.79), channel_id=1, source_target_pairs={{0,32},{8,104},{16,48},{24,120},{32,64},{40,8},{48,80},{56,24},{64... | collective-permute-start | bytes 1966088 | tf_op jit(solution)/shard_map/ppermute | solution.py:52
  113.8 8.4 %collective-permute-start.25 = (bf16[160,1024]{1,0:T(8,128)(2,1)S(1)}, bf16[160,1024]{1,0:T(8,128)(2,1)S(1)}, u32[]{:S(2)}, u32[]{:S(2)}) collective-permute-start(bf16[160,1024]{1,0:T(8,128)(2,1)S(1)} %get-tuple-element.83.refs_8_), channel_id=1, source_target_pairs={{0,32},{8,104},{16,48},{24,120},{32,64},{40,8},{48,80},{56,24},{64... | collective-permute-start | bytes 983048 | tf_op jit(solution)/shard_map/ppermute | solution.py:52
  117.5 8.3 %collective-permute-start.20 = (bf16[320,512]{1,0:T(8,128)(2,1)S(1)}, bf16[320,512]{1,0:T(8,128)(2,1)S(1)}, u32[]{:S(2)}, u32[]{:S(2)}) collective-permute-start(bf16[320,512]{1,0:T(8,128)(2,1)S(1)} %get-tuple-element.76.refs_0_), channel_id=1, source_target_pairs={{0,32},{8,104},{16,48},{24,120},{32,64},{40,8},{48,80},{56,24},{64... | collective-permute-start | bytes 983048 | tf_op jit(solution)/shard_map/ppermute | solution.py:52
  117.6 12.6 %collective-permute-start.31 = (bf16[160,1024]{1,0:T(8,128)(2,1)S(1)}, bf16[160,1024]{1,0:T(8,128)(2,1)S(1)}, u32[]{:S(2)}, u32[]{:S(2)}) collective-permute-start(bf16[160,1024]{1,0:T(8,128)(2,1)S(1)} %get-tuple-element.83.refs_8_), channel_id=1, source_target_pairs={{0,16},{16,0},{32,48},{48,32},{64,80},{80,64},{96,112},{112,96},{1... | collective-permute-start | bytes 983048 | tf_op jit(solution)/shard_map/ppermute | solution.py:52
  122.1 8.3 %collective-permute-start.30 = (bf16[160,1024]{1,0:T(8,128)(2,1)S(1)}, bf16[160,1024]{1,0:T(8,128)(2,1)S(1)}, u32[]{:S(2)}, u32[]{:S(2)}) collective-permute-start(bf16[160,1024]{1,0:T(8,128)(2,1)S(1)} %collective-permute-done.25.refs_9_), channel_id=1, source_target_pairs={{0,32},{8,104},{16,48},{24,120},{32,64},{40,8},{48,80},{56,24},{64... | collective-permute-start | bytes 983048 | tf_op jit(solution)/shard_map/ppermute | solution.py:52
  125.8 8.9 %collective-permute-start.28 = (bf16[320,512]{1,0:T(8,128)(2,1)S(1)}, bf16[320,512]{1,0:T(8,128)(2,1)S(1)}, u32[]{:S(2)}, u32[]{:S(2)}) collective-permute-start(bf16[320,512]{1,0:T(8,128)(2,1)S(1)} %get-tuple-element.85.refs_4_), channel_id=1, source_target_pairs={{0,32},{8,104},{16,48},{24,120},{32,64},{40,8},{48,80},{56,24},{64... | collective-permute-start | bytes 983048 | tf_op jit(solution)/shard_map/ppermute | solution.py:52
  125.8 12.6 %collective-permute-start.21 = (bf16[320,512]{1,0:T(8,128)(2,1)S(1)}, bf16[320,512]{1,0:T(8,128)(2,1)S(1)}, u32[]{:S(2)}, u32[]{:S(2)}) collective-permute-start(bf16[320,512]{1,0:T(8,128)(2,1)S(1)} %collective-permute-done.20.refs_1_), channel_id=1, source_target_pairs={{0,32},{8,104},{16,48},{24,120},{32,64},{40,8},{48,80},{56,24},{64... | collective-permute-start | bytes 983048 | tf_op jit(solution)/shard_map/ppermute | solution.py:52
  129.3 12.0 %collective-permute-start.26 = (bf16[160,1024]{1,0:T(8,128)(2,1)S(1)}, bf16[160,1024]{1,0:T(8,128)(2,1)S(1)}, u32[]{:S(2)}, u32[]{:S(2)}) collective-permute-start(bf16[160,1024]{1,0:T(8,128)(2,1)S(1)} %collective-permute-done.25.refs_9_), channel_id=1, source_target_pairs={{0,16},{16,0},{32,48},{48,32},{64,80},{80,64},{96,112},{112,96},{1... | collective-permute-start | bytes 983048 | tf_op jit(solution)/shard_map/ppermute | solution.py:52
  131.0 10.9 %collective-permute-start.34 = (bf16[160,1024]{1,0:T(8,128)(2,1)S(1)}, bf16[160,1024]{1,0:T(8,128)(2,1)S(1)}, u32[]{:S(2)}, u32[]{:S(2)}) collective-permute-start(bf16[160,1024]{1,0:T(8,128)(2,1)S(1)} %get-tuple-element.86.refs_10_), channel_id=1, source_target_pairs={{0,32},{8,104},{16,48},{24,120},{32,64},{40,8},{48,80},{56,24},{64... | collective-permute-start | bytes 983048 | tf_op jit(solution)/shard_map/ppermute | solution.py:52
  134.7 9.8 %collective-permute-start.29 = (bf16[320,512]{1,0:T(8,128)(2,1)S(1)}, bf16[320,512]{1,0:T(8,128)(2,1)S(1)}, u32[]{:S(2)}, u32[]{:S(2)}) collective-permute-start(bf16[320,512]{1,0:T(8,128)(2,1)S(1)} %collective-permute-done.28.refs_5_), channel_id=1, source_target_pairs={{0,32},{8,104},{16,48},{24,120},{32,64},{40,8},{48,80},{56,24},{64... | collective-permute-start | bytes 983048 | tf_op jit(solution)/shard_map/ppermute | solution.py:52
  137.6 11.0 %collective-permute-start.32 = (bf16[160,1024]{1,0:T(8,128)(2,1)S(1)}, bf16[160,1024]{1,0:T(8,128)(2,1)S(1)}, u32[]{:S(2)}, u32[]{:S(2)}) collective-permute-start(bf16[160,1024]{1,0:T(8,128)(2,1)S(1)} %get-tuple-element.86.refs_10_), channel_id=1, source_target_pairs={{0,16},{16,0},{32,48},{48,32},{64,80},{80,64},{96,112},{112,96},{1... | collective-permute-start | bytes 983048 | tf_op jit(solution)/shard_map/ppermute | solution.py:52
  141.9 7.3 %collective-permute-start.27 = (bf16[320,512]{1,0:T(8,128)(2,1)S(1)}, bf16[320,512]{1,0:T(8,128)(2,1)S(1)}, u32[]{:S(2)}, u32[]{:S(2)}) collective-permute-start(bf16[320,512]{1,0:T(8,128)(2,1)S(1)} %get-tuple-element.84.refs_2_), channel_id=1, source_target_pairs={{0,32},{8,104},{16,48},{24,120},{32,64},{40,8},{48,80},{56,24},{64... | collective-permute-start | bytes 983048 | tf_op jit(solution)/shard_map/ppermute | solution.py:52
  141.9 10.2 %collective-permute-start.35 = (bf16[160,1024]{1,0:T(8,128)(2,1)S(1)}, bf16[160,1024]{1,0:T(8,128)(2,1)S(1)}, u32[]{:S(2)}, u32[]{:S(2)}) collective-permute-start(bf16[160,1024]{1,0:T(8,128)(2,1)S(1)} %collective-permute-done.34.refs_11_), channel_id=1, source_target_pairs={{0,16},{16,0},{32,48},{48,32},{64,80},{80,64},{96,112},{112,96},{1... | collective-permute-start | bytes 983048 | tf_op jit(solution)/shard_map/ppermute | solution.py:52
  149.2 7.1 %collective-permute-start.33 = (bf16[320,512]{1,0:T(8,128)(2,1)S(1)}, bf16[320,512]{1,0:T(8,128)(2,1)S(1)}, u32[]{:S(2)}, u32[]{:S(2)}) collective-permute-start(bf16[320,512]{1,0:T(8,128)(2,1)S(1)} %get-tuple-element.87.refs_6_), channel_id=1, source_target_pairs={{0,32},{8,104},{16,48},{24,120},{32,64},{40,8},{48,80},{56,24},{64... | collective-permute-start | bytes 983048 | tf_op jit(solution)/shard_map/ppermute | solution.py:52
